TPU v7x, 32 devices: a whole 2x2x4 slice. The times are simulated.
32 devices in a mesh: row: 4 (over x, core), col: 8 (over z, y).
Axes of the slice: x: 2, y: 2, z: 4, core: 2. Of those that a mesh axis runs over, the one named last changes fastest.
Arguments:
- hidden_in: bfloat16 [14336, 2048], P('col', 'row'), may hold values from -6 to 6
- gain_before: float32 [2048], P('row'), may hold values from 0.25 to 1.75
- query_weight: bfloat16 [2048, 2048], P('row', 'col'), may hold values from -0.125 to 0.125
- key_weight: bfloat16 [2048, 2048], P('row', 'col'), may hold values from -0.125 to 0.125
- value_weight: bfloat16 [2048, 2048], P('row', 'col'), may hold values from -0.125 to 0.125
- output_weight: bfloat16 [2048, 2048], P('col', 'row'), may hold values from -2 to 2
- gain_middle: float32 [2048], P('row'), may hold values from 0.25 to 1.75
- gate_weight: bfloat16 [2048, 8192], P('row', 'col'), may hold values from -0.125 to 0.125
- up_weight: bfloat16 [2048, 8192], P('row', 'col'), may hold values from -0.125 to 0.125
- down_weight: bfloat16 [8192, 2048], P('col', 'row'), may hold values from -0.0625 to 0.0625
- cotangent: bfloat16 [14336, 2048], P('col', 'row'), may hold values from -6 to 6
- branch_points: int32 [4, 6], replicated, may hold values from 1024 to 2048, as said below
- lengths: int32 [4, 6], replicated, may hold values from 128 to 256, as said below
Outputs:
- layer_out: bfloat16 [14336, 2048], P('col', 'row')
- input_grad: float32 [14336, 2048], P('col', 'row')
- before_grad: float32 [2048], P('row')
- query_grad: float32 [2048, 2048], P('row', 'col')
- key_grad: float32 [2048, 2048], P('row', 'col')
- value_grad: float32 [2048, 2048], P('row', 'col')
- output_grad: float32 [2048, 2048], P('col', 'row')
- middle_grad: float32 [2048], P('row')
- gate_grad: float32 [2048, 8192], P('row', 'col')
- up_grad: float32 [2048, 8192], P('row', 'col')
- down_grad: float32 [8192, 2048], P('col', 'row')
- rms_values: float32 [3], replicated
Inputs may be any that keep to these rules, and one draw needn't show every extreme that they name: `branch_points`: in every group one continuation follows the whole prompt of 2048 tokens. `lengths`: in every group one continuation fills all 256 slots.
All inputs are finite; a program needn't handle non-finite values.
Results may differ from a plain program's by a relative error of at most 0.014.
Values may be sent and summed in bfloat16 or wider, within the bound.
No kernel may reach another device: no remote copies, remote signals or barrier semaphores. Data moves between devices by JAX's collectives and lax.ppermute only.
A program may use at most 768 MiB of HBM per device.

v0:
```python
import jax
import jax.numpy as jnp
from jax import lax
from jax.sharding import PartitionSpec as P

D = 2048
HD = 64
PROMPT = 2048
CLEN = 256
CONTS = 6
GTOK = 3584


EPSILON = 1e-05
THETA = 130000.0
NEGATIVE = -1e30


def norm_sum(values):
    return lax.psum(values, "row")


def rows_gather(values):
    return lax.all_gather(values, "col", axis=0, tiled=True)


def group_gather(values):
    return lax.all_gather(values, "row", axis=0, tiled=True)


def group_sum(term, rows):
    return lax.psum_scatter(
        term(jnp.int32(0), rows * lax.axis_size("row")), "row", scatter_dimension=0, tiled=True
    )


def column_sum(term, rows):
    return lax.psum_scatter(
        term(jnp.int32(0), rows * lax.axis_size("col")), "col", scatter_dimension=0, tiled=True
    )


def unit_sum(values):
    return lax.psum_scatter(values, "row", scatter_dimension=2, tiled=True)


def unit_gather(values):
    return lax.all_gather(values, "row", axis=2, tiled=True)


def rope_tables(positions):
    halfway = HD // 2
    frequency = THETA ** (-2.0 * jnp.arange(halfway, dtype=jnp.float32) / HD)
    angles = positions.astype(jnp.float32)[:, None] * frequency[None, :]
    return (jnp.cos(angles), jnp.sin(angles))


def rotate(values, cosine, sine):
    halfway = values.shape[-1] // 2
    former = values[..., :halfway]
    latter = values[..., halfway:]
    cos_rows = cosine[:, None, :]
    sin_rows = sine[:, None, :]
    return jnp.concatenate(
        [former * cos_rows - latter * sin_rows, latter * cos_rows + former * sin_rows], -1
    )


def rotate_back(values, cosine, sine):
    halfway = values.shape[-1] // 2
    former = values[..., :halfway]
    latter = values[..., halfway:]
    cos_rows = cosine[:, None, :]
    sin_rows = sine[:, None, :]
    return jnp.concatenate(
        [former * cos_rows + latter * sin_rows, latter * cos_rows - former * sin_rows], -1
    )


def group_positions(branch_row):
    prompt_part = jnp.arange(PROMPT, dtype=jnp.int32)
    branch_part = branch_row[:, None] + jnp.arange(CLEN, dtype=jnp.int32)[None, :]
    return jnp.concatenate([prompt_part, branch_part.reshape(-1)])


def prompt_mask(start, span):
    rows = start + jnp.arange(span, dtype=jnp.int32)[:, None]
    return jnp.arange(start + span, dtype=jnp.int32)[None, :] <= rows


def pair_mask(branch_row, length_row, pair):
    span = 2 * CLEN
    rows = jnp.arange(span, dtype=jnp.int32)[:, None]
    columns = jnp.arange(span, dtype=jnp.int32)[None, :]
    reach = jnp.where(rows < CLEN, branch_row[2 * pair], branch_row[2 * pair + 1])
    from_prompt = jnp.arange(PROMPT, dtype=jnp.int32)[None, :] < reach
    limit = jnp.where(columns < CLEN, length_row[2 * pair], length_row[2 * pair + 1])
    from_own = (
        (columns // CLEN == rows // CLEN)
        & (columns % CLEN <= rows % CLEN)
        & (columns % CLEN < limit)
    )
    return jnp.concatenate([from_prompt, from_own], 1)


def block_forward(query, keys, values, allowed, scale):
    scores = jnp.einsum("qhd,khd->hqk", query, keys, preferred_element_type=jnp.float32) * scale
    shifted = jnp.where(allowed[None], scores, NEGATIVE)
    peak = jnp.max(shifted, -1, keepdims=True)
    weights = jnp.exp(shifted - peak)
    total = jnp.sum(weights, -1, keepdims=True)
    probs = (weights / total).astype(jnp.bfloat16)
    result = jnp.einsum("hqk,khd->qhd", probs, values, preferred_element_type=jnp.float32)
    return (result, peak, total)


def block_backward(query, keys, values, allowed, peak, total, d_out, scale):
    scores = jnp.einsum("qhd,khd->hqk", query, keys, preferred_element_type=jnp.float32) * scale
    shifted = jnp.where(allowed[None], scores, NEGATIVE)
    probs = jnp.exp(shifted - peak) / total
    d_probs = jnp.einsum("qhd,khd->hqk", d_out, values, preferred_element_type=jnp.float32)
    inner = jnp.sum(probs * d_probs, -1, keepdims=True)
    d_scores = (probs * (d_probs - inner)).astype(jnp.bfloat16)
    d_query = jnp.einsum("hqk,khd->qhd", d_scores, keys, preferred_element_type=jnp.float32) * scale
    d_keys = jnp.einsum("hqk,qhd->khd", d_scores, query, preferred_element_type=jnp.float32) * scale
    d_values = jnp.einsum(
        "hqk,qhd->khd", probs.astype(jnp.bfloat16), d_out, preferred_element_type=jnp.float32
    )
    return (d_query, d_keys, d_values)


def attend_forward(query, keys, values, branch_row, length_row, scale):
    span = 2 * CLEN
    results, peaks, totals = ([], [], [])
    for block in range(PROMPT // span):
        start = block * span
        stop = start + span
        result, peak, total = block_forward(
            query[start:stop], keys[:stop], values[:stop], prompt_mask(start, span), scale
        )
        results.append(result)
        peaks.append(peak)
        totals.append(total)
    for pair in range(CONTS // 2):
        start = PROMPT + pair * span
        stop = start + span
        key_rows = jnp.concatenate([keys[:PROMPT], keys[start:stop]], 0)
        value_rows = jnp.concatenate([values[:PROMPT], values[start:stop]], 0)
        result, peak, total = block_forward(
            query[start:stop], key_rows, value_rows, pair_mask(branch_row, length_row, pair), scale
        )
        results.append(result)
        peaks.append(peak)
        totals.append(total)
    return (jnp.concatenate(results, 0), jnp.concatenate(peaks, 1), jnp.concatenate(totals, 1))


def attend_backward(query, keys, values, peaks, totals, d_out, branch_row, length_row, scale):
    span = 2 * CLEN
    query_parts = []
    d_keys = jnp.zeros(keys.shape, jnp.float32)
    d_values = jnp.zeros(values.shape, jnp.float32)
    for block in range(PROMPT // span):
        start = block * span
        stop = start + span
        part_query, part_keys, part_values = block_backward(
            query[start:stop],
            keys[:stop],
            values[:stop],
            prompt_mask(start, span),
            peaks[:, start:stop],
            totals[:, start:stop],
            d_out[start:stop],
            scale,
        )
        query_parts.append(part_query)
        d_keys = d_keys.at[:stop].add(part_keys)
        d_values = d_values.at[:stop].add(part_values)
    for pair in range(CONTS // 2):
        start = PROMPT + pair * span
        stop = start + span
        key_rows = jnp.concatenate([keys[:PROMPT], keys[start:stop]], 0)
        value_rows = jnp.concatenate([values[:PROMPT], values[start:stop]], 0)
        part_query, part_keys, part_values = block_backward(
            query[start:stop],
            key_rows,
            value_rows,
            pair_mask(branch_row, length_row, pair),
            peaks[:, start:stop],
            totals[:, start:stop],
            d_out[start:stop],
            scale,
        )
        query_parts.append(part_query)
        d_keys = d_keys.at[:PROMPT].add(part_keys[:PROMPT])
        d_keys = d_keys.at[start:stop].add(part_keys[PROMPT:])
        d_values = d_values.at[:PROMPT].add(part_values[:PROMPT])
        d_values = d_values.at[start:stop].add(part_values[PROMPT:])
    return (jnp.concatenate(query_parts, 0), d_keys, d_values)


def local(
    hidden_in,
    gain_before,
    query_weight,
    key_weight,
    value_weight,
    output_weight,
    gain_middle,
    gate_weight,
    up_weight,
    down_weight,
    cotangent,
    branch_points,
    lengths,
):
    local_tokens = hidden_in.shape[0]
    all_tokens = local_tokens * lax.axis_size("col")
    group_tokens = all_tokens // lax.axis_size("row")
    local_groups = group_tokens // GTOK
    head_width = query_weight.shape[1]
    local_heads = head_width // HD
    units_col = gate_weight.shape[1]
    scale = HD ** (-0.5)
    row_index = lax.axis_index("row")
    branch_local = lax.dynamic_slice_in_dim(
        branch_points, row_index * local_groups, local_groups, 0
    )
    length_local = lax.dynamic_slice_in_dim(lengths, row_index * local_groups, local_groups, 0)
    token_ids = lax.axis_index("col") * local_tokens + jnp.arange(local_tokens, dtype=jnp.int32)
    within = token_ids % GTOK
    offset = jnp.maximum(within - PROMPT, 0)
    slot_ids = token_ids // GTOK * CONTS + offset // CLEN
    table = lengths.reshape(-1)
    picked = jnp.sum(
        jnp.where(
            slot_ids[:, None] == jnp.arange(table.shape[0], dtype=jnp.int32)[None, :],
            table[None, :],
            0,
        ),
        1,
    )
    valid = jnp.where((within < PROMPT) | (offset % CLEN < picked), 1.0, 0.0).astype(jnp.float32)
    valid_count = (lengths.shape[0] * PROMPT + jnp.sum(lengths)).astype(jnp.float32)
    residual = hidden_in.astype(jnp.float32)
    scale_one = lax.rsqrt(norm_sum(jnp.sum(residual * residual, -1)) / D + EPSILON)
    norm_one = residual * scale_one[:, None]
    low_one = (norm_one * gain_before).astype(jnp.bfloat16)
    rows_one = rows_gather(low_one)
    joined_weights = jnp.concatenate([query_weight, key_weight, value_weight], 1)
    projected = group_sum(
        lambda start, count: jnp.dot(rows_one, joined_weights, preferred_element_type=jnp.float32),
        group_tokens,
    )
    group = 0
    cosine, sine = rope_tables(group_positions(branch_local[group]))
    query = rotate(projected[:, :head_width].reshape(GTOK, local_heads, HD), cosine, sine).astype(
        jnp.bfloat16
    )
    keys = rotate(
        projected[:, head_width : 2 * head_width].reshape(GTOK, local_heads, HD), cosine, sine
    ).astype(jnp.bfloat16)
    values = projected[:, 2 * head_width :].reshape(GTOK, local_heads, HD).astype(jnp.bfloat16)
    result, peaks, totals = attend_forward(
        query, keys, values, branch_local[group], length_local[group], scale
    )
    heads_parts = result.astype(jnp.bfloat16).reshape(GTOK, head_width)
    kept = [(query, keys, values, peaks, totals, cosine, sine)]
    heads_rows = group_gather(heads_parts)
    attention = column_sum(
        lambda start, count: jnp.dot(heads_rows, output_weight, preferred_element_type=jnp.float32),
        local_tokens,
    )
    middle = residual + attention
    scale_two = lax.rsqrt(norm_sum(jnp.sum(middle * middle, -1)) / D + EPSILON)
    norm_two = middle * scale_two[:, None]
    low_two = (norm_two * gain_middle).astype(jnp.bfloat16)
    rows_two = rows_gather(low_two)
    gate_up = jnp.concatenate([gate_weight, up_weight], 1)
    partial_value = jnp.dot(rows_two, gate_up, preferred_element_type=jnp.float32).reshape(
        all_tokens, 2, units_col
    )
    summed = unit_sum(partial_value)
    gate = summed[:, 0]
    up = summed[:, 1]
    hidden = (gate * jax.nn.sigmoid(gate) * up).astype(jnp.bfloat16)
    hidden_rows = unit_gather(hidden[:, None, :])[:, 0]
    mixed = column_sum(
        lambda start, count: jnp.dot(hidden_rows, down_weight, preferred_element_type=jnp.float32),
        local_tokens,
    )
    layer_out = (middle + mixed).astype(jnp.bfloat16)
    upstream = cotangent.astype(jnp.float32)
    upstream_rows = rows_gather(cotangent)
    down_grad = jnp.einsum(
        "tf,td->fd", hidden_rows, upstream_rows, preferred_element_type=jnp.float32
    )
    d_hidden = unit_sum(
        jnp.einsum("td,fd->tf", upstream_rows, down_weight, preferred_element_type=jnp.float32)[
            :, None, :
        ]
    )[:, 0]
    sigma = jax.nn.sigmoid(gate)
    d_gate = (d_hidden * up * sigma * (1.0 + gate * (1.0 - sigma))).astype(jnp.bfloat16)
    d_up = (d_hidden * (gate * sigma)).astype(jnp.bfloat16)
    d_rows = unit_gather(jnp.stack([d_gate, d_up], 1)).reshape(all_tokens, 2 * units_col)
    joined_unit_grad = jnp.einsum("td,tf->df", rows_two, d_rows, preferred_element_type=jnp.float32)
    gate_grad = joined_unit_grad[:, :units_col]
    up_grad = joined_unit_grad[:, units_col:]
    d_two = column_sum(
        lambda start, count: jnp.einsum(
            "tf,df->td", d_rows, gate_up, preferred_element_type=jnp.float32
        ),
        local_tokens,
    )
    middle_local = jnp.sum(d_two * norm_two, 0)
    scaled_two = d_two * gain_middle
    inner_two = norm_sum(jnp.sum(scaled_two * norm_two, -1))
    d_middle = upstream + scale_two[:, None] * (scaled_two - norm_two * (inner_two / D)[:, None])
    d_attention = d_middle.astype(jnp.bfloat16)
    attention_rows = rows_gather(d_attention)
    output_grad = jnp.einsum(
        "tq,td->qd", heads_rows, attention_rows, preferred_element_type=jnp.float32
    )
    d_heads = group_sum(
        lambda start, count: jnp.einsum(
            "td,qd->tq", attention_rows, output_weight, preferred_element_type=jnp.float32
        ),
        group_tokens,
    ).astype(jnp.bfloat16)
    group = 0
    query, keys, values, peaks, totals, cosine, sine = kept[group]
    d_out = d_heads.reshape(GTOK, local_heads, HD)
    d_query, d_keys, d_values = attend_backward(
        query, keys, values, peaks, totals, d_out, branch_local[group], length_local[group], scale
    )
    d_query_raw = rotate_back(d_query, cosine, sine).astype(jnp.bfloat16).reshape(GTOK, head_width)
    d_key_raw = rotate_back(d_keys, cosine, sine).astype(jnp.bfloat16).reshape(GTOK, head_width)
    d_value_low = d_values.astype(jnp.bfloat16).reshape(GTOK, head_width)
    joined_parts = jnp.concatenate([d_query_raw, d_key_raw, d_value_low], 1)
    joined_rows = group_gather(joined_parts)
    joined_grad = jnp.einsum("td,tq->dq", rows_one, joined_rows, preferred_element_type=jnp.float32)
    query_grad = joined_grad[:, :head_width]
    key_grad = joined_grad[:, head_width : 2 * head_width]
    value_grad = joined_grad[:, 2 * head_width :]
    d_one = column_sum(
        lambda start, count: jnp.einsum(
            "tq,dq->td", joined_rows, joined_weights, preferred_element_type=jnp.float32
        ),
        local_tokens,
    )
    before_local = jnp.sum(d_one * norm_one, 0)
    scaled_one = d_one * gain_before
    out_value = layer_out.astype(jnp.float32)
    squares = jnp.stack(
        [
            jnp.sum(valid * jnp.sum(out_value * out_value, -1)),
            jnp.sum(valid * jnp.sum(attention * attention, -1)),
            jnp.sum(valid * jnp.sum(d_middle * d_middle, -1)),
        ]
    )
    inner_one, squares_row = lax.psum((jnp.sum(scaled_one * norm_one, -1), squares), "row")
    input_grad = d_middle + scale_one[:, None] * (scaled_one - norm_one * (inner_one / D)[:, None])
    gains, squares_all = lax.psum((jnp.stack([before_local, middle_local]), squares_row), "col")
    rms_values = jnp.sqrt(squares_all / (valid_count * D))
    return (
        layer_out,
        input_grad,
        gains[0],
        query_grad,
        key_grad,
        value_grad,
        output_grad,
        gains[1],
        gate_grad,
        up_grad,
        down_grad,
        rms_values,
    )


def solution(mesh):
    return jax.shard_map(
        local,
        mesh=mesh,
        in_specs=(
            P("col", "row"),
            P("row"),
            P("row", "col"),
            P("row", "col"),
            P("row", "col"),
            P("col", "row"),
            P("row"),
            P("row", "col"),
            P("row", "col"),
            P("col", "row"),
            P("col", "row"),
            P(),
            P(),
        ),
        out_specs=(
            P("col", "row"),
            P("col", "row"),
            P("row"),
            P("row", "col"),
            P("row", "col"),
            P("row", "col"),
            P("col", "row"),
            P("row"),
            P("row", "col"),
            P("row", "col"),
            P("col", "row"),
            P(),
        ),
        check_vma=False,
    )
```

profile of v0, /device:TPU:0, one launch (start us, length us, event | category | flops | bytes accessed | tf_op | source)
XLA Modules:
  0.0 5619.7 jit_solution(4362563541608373797)
XLA Ops:
  22.0 202.3 %all-gather.9.cloned.1.call-done = bf16[14336,512]{1,0:T(8,128)(2,1)} async-done(((bf16[1792,512]{1,0:T(8,128)(2,1)}), bf16[14336,512]{1,0:T(8,128)(2,1)}) %all-gather.9.cloned.1.call-update) | async-done | bytes 14680080 | tf_op jit(solution)/shard_map/all_gather | solution.py:24
  272.3 276.4 %reduce-scatter.9.cloned.1.call-done = f32[3584,768]{1,0:T(8,128)} async-done(((f32[14336,768]{1,0:T(8,128)}), f32[3584,768]{1,0:T(8,128)}) %reduce-scatter.9.cloned.1.call-update) | async-done | bytes 11010064 | tf_op jit(solution)/shard_map/reduce_scatter | solution.py:32
  726.0 52.4 all-gather.11.cloned.1.call-done
  794.0 463.6 %reduce-scatter.11.cloned.1.call-done = f32[1792,512]{1,0:T(8,128)} async-done(((f32[14336,512]{1,0:T(8,128)}), f32[1792,512]{1,0:T(8,128)}) %reduce-scatter.11.cloned.1.call-update) | async-done | bytes 3670032 | tf_op jit(solution)/shard_map/reduce_scatter | solution.py:38
  1274.1 186.9 %all-gather.17.cloned.1.call-done = bf16[14336,512]{1,0:T(8,128)(2,1)} async-done(((bf16[1792,512]{1,0:T(8,128)(2,1)}), bf16[14336,512]{1,0:T(8,128)(2,1)}) %all-gather.17.cloned.1.call-update) | async-done | bytes 14680080 | tf_op jit(solution)/shard_map/all_gather | solution.py:24
  1461.0 29.2 convolution_bitcast_fusion
  1493.6 170.5 %all-gather.13.cloned.1.call-done = bf16[14336,512]{1,0:T(8,128)(2,1)} async-done(((bf16[1792,512]{1,0:T(8,128)(2,1)}), bf16[14336,512]{1,0:T(8,128)(2,1)}) %all-gather.13.cloned.1.call-update) | async-done | bytes 14680080 | tf_op jit(solution)/shard_map/all_gather | solution.py:24
  1664.1 74.2 %fusion.358 = f32[14336,2048]{0,1:T(8,128)} fusion(bf16[14336,512]{1,0:T(8,128)(2,1)} %all-gather.13.cloned.1.call-done, bf16[512,2048]{1,0:T(8,128)(2,1)} %constant_dynamic-update-slice_fusion.10), kind=kOutput, calls=%fused_computation.411 | convolution fusion | flops 30064771072 | bytes 134217728 | tf_op jit(solution)/shard_map/dot_general | solution.py:280
  1738.3 116.1 %copy.94 = f32[14336,2,1024]{2,0,1:T(8,128)} copy(f32[14336,2,1024]{0,2,1:T(8,128)} %bitcast.36) | data formatting | bytes 234881024 | tf_op jit(solution)/shard_map/reshape | solution.py:280
  1854.5 208.3 %reduce-scatter.17.cloned.1.call-done = f32[14336,1,256]{2,0,1:T(8,128)} async-done(((f32[14336,1,1024]{2,0,1:T(8,128)}), f32[14336,1,256]{2,0,1:T(8,128)}) %reduce-scatter.17.cloned.1.call-update) | async-done | bytes 14680080 | tf_op jit(solution)/shard_map/reduce_scatter | solution.py:44
  2062.8 780.1 %reduce-scatter.13.cloned.1.call-done = f32[14336,2,256]{2,0,1:T(8,128)} async-done(((f32[14336,2,1024]{2,0,1:T(8,128)}), f32[14336,2,256]{2,0,1:T(8,128)}) %reduce-scatter.13.cloned.1.call-update) | async-done | bytes 29360144 | tf_op jit(solution)/shard_map/reduce_scatter | solution.py:44
  2868.1 353.4 %all-gather.19.cloned.1.call-done = bf16[14336,2,1024]{2,0,1:T(8,128)(2,1)} async-done(((bf16[14336,2,256]{2,0,1:T(8,128)(2,1)}), bf16[14336,2,1024]{2,0,1:T(8,128)(2,1)}) %all-gather.19.cloned.1.call-update) | async-done | bytes 58720272 | tf_op jit(solution)/shard_map/all_gather | solution.py:48
  3221.5 70.8 %copy.95 = bf16[14336,2,1024]{0,2,1:T(8,128)(2,1)} copy(bf16[14336,2,1024]{2,0,1:T(8,128)(2,1)} %all-gather.19.cloned.1.call-done) | data formatting | bytes 117440512 | tf_op jit(solution)/shard_map/all_gather | solution.py:48
  3292.4 40.5 fusion.359
  3333.1 71.9 %all-gather.15.cloned.1.call-done = bf16[14336,1,1024]{2,0,1:T(8,128)(2,1)} async-done(((bf16[14336,1,256]{2,0,1:T(8,128)(2,1)}), bf16[14336,1,1024]{2,0,1:T(8,128)(2,1)}) %all-gather.15.cloned.1.call-update) | async-done | bytes 29360144 | tf_op jit(solution)/shard_map/all_gather | solution.py:48
  3405.0 28.5 fusion.9
  3433.6 439.9 %reduce-scatter.19.cloned.1.call-done = f32[1792,512]{1,0:T(8,128)} async-done(((f32[14336,512]{1,0:T(8,128)}), f32[1792,512]{1,0:T(8,128)}) %reduce-scatter.19.cloned.1.call-update) | async-done | bytes 3670032 | tf_op jit(solution)/shard_map/reduce_scatter | solution.py:38
  3885.2 455.8 %reduce-scatter.15.cloned.1.call-done = f32[1792,512]{1,0:T(8,128)} async-done(((f32[14336,512]{1,0:T(8,128)}), f32[1792,512]{1,0:T(8,128)}) %reduce-scatter.15.cloned.1.call-update) | async-done | bytes 3670032 | tf_op jit(solution)/shard_map/reduce_scatter | solution.py:38
  4351.2 201.2 %all-gather.21.cloned.1.call-done = bf16[14336,512]{1,0:T(8,128)(2,1)} async-done(((bf16[1792,512]{1,0:T(8,128)(2,1)}), bf16[14336,512]{1,0:T(8,128)(2,1)}) %all-gather.21.cloned.1.call-update) | async-done | bytes 14680080 | tf_op jit(solution)/shard_map/all_gather | solution.py:24
  4567.5 110.7 %reduce-scatter.21.cloned.1.call-done = f32[3584,256]{1,0:T(8,128)} async-done(((f32[14336,256]{1,0:T(8,128)}), f32[3584,256]{1,0:T(8,128)}) %reduce-scatter.21.cloned.1.call-update) | async-done | bytes 3670032 | tf_op jit(solution)/shard_map/reduce_scatter | solution.py:32
  4950.2 137.5 %all-gather.23.cloned.1.call-done = bf16[14336,768]{0,1:T(8,128)(2,1)} async-done(((bf16[3584,768]{0,1:T(8,128)(2,1)}), bf16[14336,768]{0,1:T(8,128)(2,1)}) %all-gather.23.cloned.1.call-update) | async-done | bytes 22020112 | tf_op jit(solution)/shard_map/all_gather | solution.py:28
  5087.8 24.6 fusion.361
  5137.3 38.9 fusion.364
  5215.9 360.8 %reduce-scatter.23.cloned.1.call-done = f32[1792,512]{1,0:T(8,128)} async-done(((f32[14336,512]{1,0:T(8,128)}), f32[1792,512]{1,0:T(8,128)}) %reduce-scatter.23.cloned.1.call-update) | async-done | bytes 3670032 | tf_op jit(solution)/shard_map/reduce_scatter | solution.py:38
  (464 shorter events, 708.5 us)
Async XLA Ops:
  7.2 1453.8 %copy-start = (bf16[1024,512]{1,0:T(8,128)(2,1)S(1)}, bf16[1024,512]{1,0:T(8,128)(2,1)}, u32[]{:S(2)}) copy-start(bf16[1024,512]{1,0:T(8,128)(2,1)} %param.62) | copy-start | bytes 3145732
  7.2 217.1 %all-gather.9.cloned.1.call-start = ((), (), s32[]{:S(2)}) async-start(), calls=%async_computation.8 | async-start | bytes 16515072 | tf_op jit(solution)/shard_map/all_gather | solution.py:24
  21.8 526.9 %reduce-scatter.9.cloned.1.call-start = ((), (), s32[]{:S(2)}) async-start(), calls=%async_computation.9 | async-start | bytes 55050240 | tf_op jit(solution)/shard_map/reduce_scatter | solution.py:32
  248.0 530.4 %all-gather.11.cloned.1.call-start = ((), (), s32[]{:S(2)}) async-start(), calls=%async_computation.10 | async-start | bytes 9175040 | tf_op jit(solution)/shard_map/all_gather | solution.py:28
  726.0 531.6 %reduce-scatter.11.cloned.1.call-start = ((), (), s32[]{:S(2)}) async-start(), calls=%async_computation.11 | async-start | bytes 33030144 | tf_op jit(solution)/shard_map/reduce_scatter | solution.py:38
  793.3 464.3 %copy-start.19 = (bf16[1792,512]{1,0:T(8,128)(2,1)S(1)}, bf16[1792,512]{1,0:T(8,128)(2,1)}, u32[]{:S(2)}) copy-start(bf16[1792,512]{1,0:T(8,128)(2,1)} %param.53) | copy-start | bytes 5505028
  793.3 667.7 %all-gather.17.cloned.1.call-start = ((), (), s32[]{:S(2)}) async-start(), calls=%async_computation.16 | async-start | bytes 16515072 | tf_op jit(solution)/shard_map/all_gather | solution.py:24
  793.9 476.3 %copy-start.87 = (f32[512]{0:T(512)S(1)}, f32[512]{0:T(512)}, u32[]{:S(2)}) copy-start(f32[512]{0:T(512)} %param.59) | copy-start | bytes 6148
  793.9 870.2 %all-gather.13.cloned.1.call-start = ((), (), s32[]{:S(2)}) async-start(), calls=%async_computation.12 | async-start | bytes 16515072 | tf_op jit(solution)/shard_map/all_gather | solution.py:24
  1274.0 788.8 %reduce-scatter.17.cloned.1.call-start = ((), (), s32[]{:S(2)}) async-start(), calls=%async_computation.17 | async-start | bytes 73400320 | tf_op jit(solution)/shard_map/reduce_scatter | solution.py:44
  1490.3 1352.6 %reduce-scatter.13.cloned.1.call-start = ((), (), s32[]{:S(2)}) async-start(), calls=%async_computation.13 | async-start | bytes 146800640 | tf_op jit(solution)/shard_map/reduce_scatter | solution.py:44
  1854.4 1367.1 %all-gather.19.cloned.1.call-start = ((), (), s32[]{:S(2)}) async-start(), calls=%async_computation.18 | async-start | bytes 73400320 | tf_op jit(solution)/shard_map/all_gather | solution.py:48
  2867.5 537.5 %all-gather.15.cloned.1.call-start = ((), (), s32[]{:S(2)}) async-start(), calls=%async_computation.14 | async-start | bytes 36700160 | tf_op jit(solution)/shard_map/all_gather | solution.py:48
  2868.1 1005.4 %reduce-scatter.19.cloned.1.call-start = ((), (), s32[]{:S(2)}) async-start(), calls=%async_computation.19 | async-start | bytes 33030144 | tf_op jit(solution)/shard_map/reduce_scatter | solution.py:38
  3332.9 1008.1 %reduce-scatter.15.cloned.1.call-start = ((), (), s32[]{:S(2)}) async-start(), calls=%async_computation.15 | async-start | bytes 33030144 | tf_op jit(solution)/shard_map/reduce_scatter | solution.py:38
  3433.5 440.0 %copy-start.79 = (f32[1792]{0:T(1024)S(1)}, f32[1792]{0:T(1024)}, u32[]{:S(2)}) copy-start(f32[1792]{0:T(1024)} %copy-done.78) | copy-start | bytes 21508
  3433.5 440.0 %copy-start.88 = (f32[512]{0:T(512)S(1)}, f32[512]{0:T(512)}, u32[]{:S(2)}) copy-start(f32[512]{0:T(512)} %param.59) | copy-start | bytes 6148
  3433.5 907.5 %copy-start.27 = (bf16[1792,512]{1,0:T(8,128)(2,1)S(1)}, bf16[1792,512]{1,0:T(8,128)(2,1)}, u32[]{:S(2)}) copy-start(bf16[1792,512]{1,0:T(8,128)(2,1)} %param.63) | copy-start | bytes 5505028
  3433.5 1118.9 %all-gather.21.cloned.1.call-start = ((), (), s32[]{:S(2)}) async-start(), calls=%async_computation.20 | async-start | bytes 16515072 | tf_op jit(solution)/shard_map/all_gather | solution.py:24
  4351.2 327.0 %reduce-scatter.21.cloned.1.call-start = ((), (), s32[]{:S(2)}) async-start(), calls=%async_computation.21 | async-start | bytes 18350080 | tf_op jit(solution)/shard_map/reduce_scatter | solution.py:32
  4566.9 520.8 %all-gather.23.cloned.1.call-start = ((), (), s32[]{:S(2)}) async-start(), calls=%async_computation.22 | async-start | bytes 27525120 | tf_op jit(solution)/shard_map/all_gather | solution.py:28
  4950.2 626.5 %reduce-scatter.23.cloned.1.call-start = ((), (), s32[]{:S(2)}) async-start(), calls=%async_computation.23 | async-start | bytes 33030144 | tf_op jit(solution)/shard_map/reduce_scatter | solution.py:38
  5193.6 383.1 %copy-start.81 = (f32[1792]{0:T(1024)S(1)}, f32[1792]{0:T(1024)}, u32[]{:S(2)}) copy-start(f32[1792]{0:T(1024)} %copy-done.80) | copy-start | bytes 21508
  5193.6 383.1 %copy-start.89 = (f32[512]{0:T(512)S(1)}, f32[512]{0:T(512)}, u32[]{:S(2)}) copy-start(f32[512]{0:T(512)} %param.54) | copy-start | bytes 6148
  (116 other events, 2895.0 us)
Sparse Core Ops, SparseCore 0:
  21.9 202.3 all-gather.8
  248.2 300.5 reduce-scatter.8
  726.1 52.2 all-gather.10
  793.5 464.0 reduce-scatter.10
  1259.9 201.1 all-gather.16
  1463.9 200.1 all-gather.12
  1666.9 395.8 reduce-scatter.16
  2065.4 777.4 reduce-scatter.12
  2867.6 353.8 all-gather.18
  3223.0 181.9 all-gather.14
  3409.4 464.0 reduce-scatter.18
  3877.7 463.2 reduce-scatter.14
  4351.3 201.1 all-gather.20
  4567.0 111.0 reduce-scatter.20
  4950.3 137.4 all-gather.22
  5112.5 464.1 reduce-scatter.22
where the time goes:
time: 5630 us; the launch traced here: 5620 us
  waiting for transfers between devices  4470 us (79%)
  matrix products  629 us (11%)
  local copies, waits for them, and re-layouts  264 us (5%)
  other arithmetic  186 us (3%)
    reduce_scatter x4, waiting for transfers between devices, column_sum(): lax.psum_scatter(term(jnp.int32(0), rows * lax.axis_size('col')), 'col',...  1720 us
    reduce_scatter x2, waiting for transfers between devices, unit_sum(): return lax.psum_scatter(values, 'row', scatter_dimension=2, tiled=True)  988 us
    all_gather x4, waiting for transfers between devices, rows_gather(): return lax.all_gather(values, 'col', axis=0, tiled=True)  761 us
    all_gather x2, waiting for transfers between devices, unit_gather(): return lax.all_gather(values, 'row', axis=2, tiled=True)  425 us
    reduce_scatter x2, waiting for transfers between devices, group_sum(): lax.psum_scatter(term(jnp.int32(0), rows * lax.axis_size('row')), 'row',...  387 us
    all_gather x2, waiting for transfers between devices, group_gather(): return lax.all_gather(values, 'row', axis=0, tiled=True)  190 us
    reshape x1, local copies, waits for them, and re-layouts, local(): jnp.dot(rows_two, gate_up, preferred_element_type=jnp.float32)  116 us
  transfers between devices with their start and end apart: 16, of which 16 were waited for; matrix products, arithmetic and copies ran while one was open for 9% of the time, Pallas kernels for 0%

commit v1 on v0

v1 whole, which is shorter than its diff:
```python
import functools
import jax
import jax.numpy as jnp
from jax import lax
from jax.experimental import pallas as pl
from jax.experimental.pallas import tpu as pltpu
from jax.sharding import Mesh
from jax.sharding import PartitionSpec as P

HD = 64
PROMPT = 2048
CLEN = 256
CONTS = 6
GTOK = 3584
BLK = 256
PBLKS = PROMPT // BLK
BLOCKS = GTOK // BLK
ROWS = 3 * HD
BF = jnp.bfloat16
F32 = jnp.float32
LOW = -1e30
LOG2E = 1.4426950408889634
FACTOR = HD ** (-0.5) * LOG2E
VMEM_LIMIT = 56 * 1024 * 1024

NN = (((1,), (0,)), ((), ()))
NT = (((1,), (1,)), ((), ()))


def mm(a, b, dims=NN):
    return lax.dot_general(a, b, dims, preferred_element_type=F32)


def block_plan(info, block):
    cont = jnp.maximum(block - PBLKS, 0)
    is_cont = block >= PBLKS
    reach = info[cont]
    full = jnp.where(is_cont, reach // BLK, block)
    rest = jnp.where(is_cont, reach - full * BLK, 0)
    limit = jnp.where(is_cont, info[CONTS + cont], BLK)
    masked = 1 + (rest > 0).astype(jnp.int32)
    return full, rest, limit, masked


def local_ids(info, shape, axis):
    return lax.broadcasted_iota(jnp.int32, shape, axis) ^ info[2 * CONTS]


def masked_step(info, block, full, rest, limit, index):
    own = index == 0
    target = jnp.where(own, block, full)
    query_ids = local_ids(info, (1, BLK), 1)
    bound = jnp.where(own, jnp.minimum(query_ids + 1, limit), rest)
    key_ids = local_ids(info, (BLK, BLK), 0)
    return target, key_ids < bound


def columns(block):
    return pl.ds(pl.multiple_of(block * BLK, BLK), BLK)


def forward_kernel(heads, first, info, qkv, knat, out, lse, acc, top, tot):
    block = pl.program_id(0) + first
    full, rest, limit, masked = block_plan(info, block)
    here = columns(block)
    acc[...] = jnp.zeros_like(acc)
    top[...] = jnp.full_like(top, LOW)
    tot[...] = jnp.zeros_like(tot)

    def step(target, allowed):
        span = columns(target)
        for h in range(heads):
            query = qkv[h * ROWS : h * ROWS + HD, here]
            value = qkv[h * ROWS + 2 * HD : (h + 1) * ROWS, span]
            scores = mm(knat[h, span, :], query) * FACTOR
            if allowed is not None:
                scores = jnp.where(allowed, scores, LOW)
            old = top[h : h + 1, :]
            new = jnp.maximum(old, jnp.max(scores, 0, keepdims=True))
            weights = jnp.exp2(scores - new)
            shrink = jnp.exp2(old - new)
            top[h : h + 1, :] = new
            tot[h : h + 1, :] = tot[h : h + 1, :] * shrink + jnp.sum(weights, 0, keepdims=True)
            acc[h] = acc[h] * shrink + mm(value, weights.astype(BF))

    def full_step(index, carry):
        step(index, None)
        return carry

    def mask_step(index, carry):
        target, allowed = masked_step(info, block, full, rest, limit, index)
        step(target, allowed)
        return carry

    lax.fori_loop(0, full, full_step, 0)
    lax.fori_loop(0, masked, mask_step, 0)
    for h in range(heads):
        total = tot[h : h + 1, :]
        out[h * HD : (h + 1) * HD, :] = (acc[h] / total).astype(BF)
        lse[h : h + 1, :] = top[h : h + 1, :] + jnp.log2(total)


def attend_forward(info, qkv, knat, heads, first, count):
    pad = max(8, heads)
    return pl.pallas_call(
        functools.partial(forward_kernel, heads, first),
        grid=(count,),
        in_specs=[
            pl.BlockSpec(memory_space=pltpu.SMEM),
            pl.BlockSpec(qkv.shape, lambda i: (0, 0)),
            pl.BlockSpec(knat.shape, lambda i: (0, 0, 0)),
        ],
        out_specs=[
            pl.BlockSpec((heads * HD, BLK), lambda i: (0, i)),
            pl.BlockSpec((pad, BLK), lambda i: (0, i)),
        ],
        out_shape=[
            jax.ShapeDtypeStruct((heads * HD, count * BLK), BF),
            jax.ShapeDtypeStruct((pad, count * BLK), F32),
        ],
        scratch_shapes=[
            pltpu.VMEM((heads, HD, BLK), F32),
            pltpu.VMEM((pad, BLK), F32),
            pltpu.VMEM((pad, BLK), F32),
        ],
        compiler_params=pltpu.CompilerParams(vmem_limit_bytes=VMEM_LIMIT),
        cost_estimate=pl.CostEstimate(
            flops=heads * count * 6 * BLK * BLK * 1024,
            bytes_accessed=16 << 20,
            transcendentals=heads * count * 6 * BLK * BLK,
        ),
    )(info, qkv, knat)


def backward_kernel(heads, info, qkv, knat, vnat, d_out, heads_out, lse, cosine, sine, d_qkv, inner, d_keys, d_values, d_query):
    block = pl.program_id(0)
    full, rest, limit, masked = block_plan(info, block)
    here = columns(block)

    @pl.when(block == 0)
    def _():
        d_keys[...] = jnp.zeros_like(d_keys)
        d_values[...] = jnp.zeros_like(d_values)
        inner[...] = jnp.zeros_like(inner)

    d_query[...] = jnp.zeros_like(d_query)
    deltas = []
    for h in range(heads):
        rows = slice(h * HD, (h + 1) * HD)
        deltas.append(
            jnp.sum(d_out[rows, here].astype(F32) * heads_out[rows, here].astype(F32), 0, keepdims=True)
        )

    def step(target, allowed):
        span = columns(target)
        for h in range(heads):
            rows = slice(h * HD, (h + 1) * HD)
            query = qkv[h * ROWS : h * ROWS + HD, here]
            key = qkv[h * ROWS + HD : h * ROWS + 2 * HD, span]
            gradient = d_out[rows, here]
            scores = mm(knat[h, span, :], query) * FACTOR - lse[h : h + 1, here]
            if allowed is not None:
                scores = jnp.where(allowed, scores, LOW)
            probs = jnp.exp2(scores)
            d_probs = mm(vnat[h, span, :], gradient)
            d_scores = (probs * (d_probs - deltas[h])).astype(BF)
            d_query[h] += mm(key, d_scores)
            d_keys[rows, span] += mm(query, d_scores, NT)
            d_values[rows, span] += mm(gradient, probs.astype(BF), NT)

    def full_step(index, carry):
        step(index, None)
        return carry

    def mask_step(index, carry):
        target, allowed = masked_step(info, block, full, rest, limit, index)
        step(target, allowed)
        return carry

    lax.fori_loop(0, full, full_step, 0)
    lax.fori_loop(0, masked, mask_step, 0)

    half = HD // 2

    def turn(values, at):
        cos, sin = cosine[:, at], sine[:, at]
        former, latter = values[:half], values[half:]
        return former * cos + latter * sin, latter * cos - former * sin

    share = jnp.zeros((1, BLK), F32)
    for h in range(heads):
        start = h * ROWS
        values = d_query[h] * HD ** (-0.5)
        share += jnp.sum(values * qkv[start : start + HD, here].astype(F32), 0, keepdims=True)
        low, high = turn(values, here)
        d_qkv[start : start + half, here] = low.astype(BF)
        d_qkv[start + half : start + HD, here] = high.astype(BF)
    inner[0:1, here] = share

    @pl.when(block == BLOCKS - 1)
    def _():
        def finish(index, carry):
            at = columns(index)
            share = inner[0:1, at]
            for h in range(heads):
                start = h * ROWS + HD
                rows = slice(h * HD, (h + 1) * HD)
                values = d_keys[rows, at] * HD ** (-0.5)
                share += jnp.sum(values * qkv[start : start + HD, at].astype(F32), 0, keepdims=True)
                low, high = turn(values, at)
                d_qkv[start : start + half, at] = low.astype(BF)
                d_qkv[start + half : start + HD, at] = high.astype(BF)
                start += HD
                values = d_values[rows, at]
                share += jnp.sum(values * qkv[start : start + HD, at].astype(F32), 0, keepdims=True)
                d_qkv[start : start + HD, at] = values.astype(BF)
            inner[0:1, at] = share
            return carry

        lax.fori_loop(0, BLOCKS, finish, 0)


def attend_backward(info, qkv, knat, vnat, d_out, heads_out, lse, cosine, sine, heads):
    whole = lambda a: pl.BlockSpec(a.shape, lambda i, n=len(a.shape): (0,) * n)
    return pl.pallas_call(
        functools.partial(backward_kernel, heads),
        grid=(BLOCKS,),
        in_specs=[pl.BlockSpec(memory_space=pltpu.SMEM)]
        + [whole(a) for a in (qkv, knat, vnat, d_out, heads_out, lse, cosine, sine)],
        out_specs=[
            pl.BlockSpec(qkv.shape, lambda i: (0, 0)),
            pl.BlockSpec((8, GTOK), lambda i: (0, 0)),
        ],
        out_shape=[jax.ShapeDtypeStruct(qkv.shape, BF), jax.ShapeDtypeStruct((8, GTOK), F32)],
        scratch_shapes=[
            pltpu.VMEM((heads * HD, GTOK), F32),
            pltpu.VMEM((heads * HD, GTOK), F32),
            pltpu.VMEM((heads, HD, BLK), F32),
        ],
        compiler_params=pltpu.CompilerParams(vmem_limit_bytes=VMEM_LIMIT),
        cost_estimate=pl.CostEstimate(
            flops=heads * BLOCKS * 6 * BLK * BLK * 2560,
            bytes_accessed=32 << 20,
            transcendentals=heads * BLOCKS * 6 * BLK * BLK,
        ),
    )(info, qkv, knat, vnat, d_out, heads_out, lse, cosine, sine)


EPSILON = 1e-05
THETA = 130000.0
GROUPS = 4
CHUNKS = (4, 4, 3, 3)
ROW = ("x", "c")
TEAM = ("y", "x", "c")
EVERY = ("x", "c", "z", "y")


def flip(values, axis):
    return lax.ppermute(values, axis, [(0, 1), (1, 0)])


def pick(stack, index, axis=0):
    return lax.dynamic_index_in_dim(stack, index, axis, keepdims=False)


def in_order(mine, other, bit, axis):
    return jnp.where(
        bit == 0, jnp.stack([mine, other], axis), jnp.stack([other, mine], axis)
    )


def spread(pieces):
    x, c = lax.axis_index("x"), lax.axis_index("c")
    pieces = pieces.reshape((2, 2) + pieces.shape[1:])
    got = flip(pick(pieces, 1 - x), "x")
    pieces = in_order(pick(pieces, x), got, x, 0)
    got = flip(pick(pieces, 1 - c, 1), "c")
    pieces = in_order(pick(pieces, c, 1), got, c, 1)
    return pieces.reshape((4,) + pieces.shape[2:])


def row_gather(values):
    x, c = lax.axis_index("x"), lax.axis_index("c")
    pair = in_order(values, flip(values, "x"), x, 0)
    four = in_order(pair, flip(pair, "c"), c, 1)
    return four.reshape((4,) + values.shape)


def row_sum(values):
    values = values + flip(values, "x")
    return values + flip(values, "c")


def halves(values):
    middle = values.shape[0] // 2
    return values[:middle], values[middle:]


def team_gather(own):
    from_x, from_y = flip(own, "x"), flip(own, "y")
    former, latter = halves(from_y)[0], halves(from_x)[1]
    corner = jnp.concatenate([flip(former, "x"), flip(latter, "y")], 0)
    found = []
    for piece in (own, from_x, from_y, corner):
        found += [piece, flip(piece, "c")]
    return found


def team_scatter(pieces):
    got = flip(jnp.stack([pieces[k] for k in (1, 3, 5, 7)]), "c")
    sums = [pieces[2 * k].astype(F32) + got[k].astype(F32) for k in range(4)]
    low = [halves(s.astype(BF)) for s in sums[1:]]
    by_x = flip(jnp.stack([low[0][0], low[2][0]]), "x")
    by_y = flip(jnp.stack([low[1][1], low[2][1]]), "y")
    own = halves(sums[0])
    turn_y = flip((halves(sums[2])[0] + by_x[1].astype(F32)).astype(BF), "y")
    turn_x = flip((halves(sums[1])[1] + by_y[1].astype(F32)).astype(BF), "x")
    former = own[0] + by_x[0].astype(F32) + turn_y.astype(F32)
    latter = own[1] + by_y[0].astype(F32) + turn_x.astype(F32)
    return jnp.concatenate([former, latter], 0)


def norm_kernel(places, *refs):
    own, other, (gain, low, share, whole) = refs[:4], refs[4:8], refs[8:]
    half, row, rank = places[0], places[1], places[2]
    mine = pl.program_id(0) // (BLOCKS // 2) == half
    width = own[0].shape[1]

    def place(sources):
        for k, source in enumerate(sources):
            at = pl.multiple_of((row ^ k) * width, width)
            whole[:, pl.ds(at, width)] = source[...]

    @pl.when(mine)
    def _():
        place(own)

    @pl.when(jnp.logical_not(mine))
    def _():
        place(other)

    sub = share.shape[0]
    for k in range(BLK // sub):
        at = pl.multiple_of((rank ^ k) * sub, sub)
        rows = whole[pl.ds(at, sub), :]
        if k == 0:
            share[...] = rows
        if gain is None:
            low[k * sub : (k + 1) * sub, :] = rows
        else:
            wide = rows.astype(F32)
            scale = lax.rsqrt(jnp.sum(wide * wide, 1, keepdims=True) / wide.shape[1] + EPSILON)
            low[k * sub : (k + 1) * sub, :] = (wide * scale * gain[...]).astype(BF)


def plain_kernel(places, *refs):
    norm_kernel(places, *refs[:8], None, *refs[8:])


def assemble(places, pieces, gain, sub):
    per = BLOCKS // 2
    width = pieces[0].shape[1]
    whole = 4 * width

    def own_map(i, places):
        return jnp.where(i // per == places[0], i % per, 0), 0

    def other_map(i, places):
        return jnp.where(i // per == places[0], 0, i % per), 0

    ordered = [pieces[k] for k in range(8)]
    specs = [pl.BlockSpec((BLK, width), own_map)] * 4 + [pl.BlockSpec((BLK, width), other_map)] * 4
    if gain is not None:
        specs = specs + [pl.BlockSpec((1, whole), lambda i, places: (0, 0))]
        ordered = ordered + [gain.reshape(1, whole)]
    return pl.pallas_call(
        plain_kernel if gain is None else norm_kernel,
        grid_spec=pltpu.PrefetchScalarGridSpec(
            num_scalar_prefetch=1,
            grid=(BLOCKS,),
            in_specs=specs,
            out_specs=[
                pl.BlockSpec((BLK, whole), lambda i, places: (i, 0)),
                pl.BlockSpec((sub, whole), lambda i, places: (i, 0)),
            ],
            scratch_shapes=[pltpu.VMEM((BLK, whole), BF)],
        ),
        out_shape=[
            jax.ShapeDtypeStruct((GTOK, whole), BF),
            jax.ShapeDtypeStruct((BLOCKS * sub, whole), BF),
        ],
        compiler_params=pltpu.CompilerParams(vmem_limit_bytes=VMEM_LIMIT),
        cost_estimate=pl.CostEstimate(
            flops=GTOK * whole * 6, bytes_accessed=GTOK * whole * 5, transcendentals=0
        ),
    )(places, *ordered)


def straighten(values, rank):
    sub = values.shape[2]
    count = values.shape[1]
    return jnp.stack([pick(values, j ^ rank, 1) for j in range(count)], 1)


def local(
    quick,
    hidden_in,
    gain_before,
    query_weight,
    key_weight,
    value_weight,
    output_weight,
    gain_middle,
    gate_weight,
    up_weight,
    down_weight,
    cotangent,
    branch_points,
    lengths,
):
    width = hidden_in.shape[1]
    depth = 4 * width
    head_width = query_weight.shape[1]
    heads = head_width // HD
    units = gate_weight.shape[1]
    local_tokens = hidden_in.shape[0]
    team = 4 * lax.axis_size("y")
    sub = BLK // team
    x, c = lax.axis_index("x"), lax.axis_index("c")
    z, y = lax.axis_index("z"), lax.axis_index("y")
    row = 2 * x + c
    rank = 4 * y + row
    order = rank if quick else jnp.int32(0)
    branch_row = pick(branch_points, z)
    length_row = pick(lengths, z)
    info = jnp.concatenate(
        [branch_row, length_row, jnp.stack([order * sub, rank * sub, jnp.int32(0), jnp.int32(0)])]
    ).astype(jnp.int32)

    def join(pieces):
        blocks = pieces[0].shape[0] // sub
        return jnp.stack([p.reshape(blocks, sub, depth) for p in pieces], 1).reshape(-1, depth)

    def token_gather(share):
        if quick:
            return join(team_gather(share))
        blocks = share.shape[0] // sub
        got = lax.all_gather(share.reshape(blocks, sub, depth), TEAM, axis=1, tiled=False)
        return got.reshape(-1, depth)

    def token_scatter(partial):
        parts = partial.reshape(-1, team, sub, depth)
        if quick:
            return team_scatter([parts[:, k].reshape(-1, depth) for k in range(8)])
        parts = lax.psum_scatter(parts, TEAM, scatter_dimension=1, tiled=False)
        return parts.reshape(-1, depth).astype(F32)

    joined = jnp.stack([query_weight, key_weight, value_weight]).transpose(0, 2, 1)
    joined = jnp.concatenate([joined, output_weight[None]], 0)
    if heads % 4 == 0:
        per = heads // 4
        pieces = joined.reshape(4, 4, per * HD, width).transpose(1, 0, 2, 3)
        pieces = spread(pieces)
        pieces = pieces.reshape(4, 4, per, HD, width).transpose(2, 1, 3, 0, 4)
        pieces = pieces.reshape(per, 4 * HD, depth)
        attend_weights = lax.all_gather(pieces, "z", axis=0, tiled=True)
    else:
        pieces = lax.all_gather(joined, "z", axis=0, tiled=False)
        pieces = spread(pieces).reshape(4, 4, heads, HD, width).transpose(2, 1, 3, 0, 4)
        attend_weights = pieces.reshape(heads, 4 * HD, depth)
    join_weight = attend_weights[:, :ROWS].reshape(heads * ROWS, depth)
    out_weight = attend_weights[:, ROWS:].reshape(heads * HD, depth)

    def unit_rows(weight):
        pieces = spread(weight.reshape(4, units // 4, width))
        pieces = pieces.transpose(1, 0, 2).reshape(units // 4, depth)
        return lax.all_gather(pieces, "z", axis=0, tiled=True)

    gains = row_gather(jnp.stack([gain_before, gain_middle])).transpose(1, 0, 2).reshape(2, depth)
    gain_one, gain_two = gains[0], gains[1]

    places = jnp.stack([y, row, rank]).astype(jnp.int32)
    if quick:
        low_one, residual = assemble(places, team_gather(hidden_in), gain_one, sub)
        upstream_rows, upstream = assemble(places, team_gather(cotangent), None, sub)
    else:

        def full(values):
            values = lax.all_gather(values, "y", axis=0, tiled=True)
            return lax.all_gather(values, ROW, axis=1, tiled=True)

        def share_of(values):
            return pick(values.reshape(BLOCKS, team, sub, depth), rank, 1).reshape(-1, depth)

        hidden_rows = full(hidden_in)
        upstream_rows = full(cotangent)
        residual, upstream = share_of(hidden_rows), share_of(upstream_rows)
        wide = hidden_rows.astype(F32)
        scale = lax.rsqrt(jnp.mean(wide * wide, -1, keepdims=True) + EPSILON)
        low_one = (wide * scale * gain_one).astype(BF)

    gate_rows = unit_rows(gate_weight.T)
    up_rows = unit_rows(up_weight.T)
    down_rows = unit_rows(down_weight)
    gate_up_rows = jnp.concatenate([gate_rows, up_rows], 0)

    ids = jnp.arange(GTOK, dtype=jnp.int32)
    block_ids, slot_ids = ids // BLK, (ids % BLK) ^ (order * sub)
    starts = jnp.concatenate([jnp.arange(PBLKS, dtype=jnp.int32) * BLK, branch_row])
    positions = jnp.repeat(starts, BLK) + slot_ids
    frequency = THETA ** (-2.0 * jnp.arange(HD // 2, dtype=F32) / HD)
    angles = positions.astype(F32)[None, :] * frequency[:, None]
    cosine, sine = jnp.cos(angles), jnp.sin(angles)
    raw = mm(join_weight, low_one, NT).reshape(heads, 3, HD, GTOK)
    former, latter = raw[:, :2, : HD // 2], raw[:, :2, HD // 2 :]
    turned = jnp.concatenate([former * cosine - latter * sine, latter * cosine + former * sine], 2)
    qkv = jnp.concatenate([turned, raw[:, 2:]], 1).astype(BF)
    natural = qkv[:, 1:].transpose(1, 0, 3, 2)
    keys, values = natural[0], natural[1]
    qkv = qkv.reshape(heads * ROWS, GTOK)

    heads_parts, lse_parts, low_parts, d_low_parts, hidden_parts, d_unit_parts = [], [], [], [], [], []
    d_attention_parts, d_head_parts, out_parts = [], [], []
    middle_local = jnp.zeros((depth,), F32)
    squares = jnp.zeros((3,), F32)
    first = 0
    for count in CHUNKS:
        span = slice(first * BLK, (first + count) * BLK)
        shares = slice(first * sub, (first + count) * sub)
        head_part, lse = attend_forward(info, qkv, keys, heads, first, count)
        heads_parts.append(head_part)
        lse_parts.append(lse)
        partial = mm(head_part, out_weight, (((0,), (0,)), ((), ()))).astype(BF)
        attention = token_scatter(partial)
        middle = residual[shares].astype(F32) + attention
        scale_two = lax.rsqrt(jnp.mean(middle * middle, -1, keepdims=True) + EPSILON)
        norm_two = middle * scale_two
        low_two = token_gather((norm_two * gain_two).astype(BF))
        low_parts.append(low_two)
        gate = mm(low_two, gate_rows, NT)
        up = mm(low_two, up_rows, NT)
        sigma = jax.nn.sigmoid(gate)
        hidden = (gate * sigma * up).astype(BF)
        hidden_parts.append(hidden)
        d_hidden = mm(upstream_rows[span], down_rows, NT)
        d_gate = (d_hidden * up * sigma * (1.0 + gate * (1.0 - sigma))).astype(BF)
        d_up = (d_hidden * (gate * sigma)).astype(BF)
        d_units = jnp.concatenate([d_gate, d_up], 1)
        d_unit_parts.append(d_units)
        d_two = token_scatter(mm(d_units, gate_up_rows).astype(BF))
        middle_local += jnp.sum(d_two * norm_two, 0)
        scaled_two = d_two * gain_two
        inner_two = jnp.mean(scaled_two * norm_two, -1, keepdims=True)
        d_middle = upstream[shares].astype(F32) + scale_two * (scaled_two - norm_two * inner_two)
        d_attention = token_gather(d_middle.astype(BF))
        d_attention_parts.append(d_attention)
        d_head_parts.append(mm(out_weight, d_attention, NT).astype(BF))
        mixed = token_scatter(mm(hidden, down_rows).astype(BF))
        layer_out = (middle + mixed).astype(BF)
        out_parts.append(layer_out)
        here = first + jnp.arange(count, dtype=jnp.int32)
        bound = jnp.where(here < PBLKS, BLK, jnp.take(length_row, jnp.maximum(here - PBLKS, 0)))
        slots = rank * sub + jnp.arange(sub, dtype=jnp.int32)
        valid = (slots[None, :] < bound[:, None]).astype(F32).reshape(-1)
        wide = layer_out.astype(F32)
        squares += jnp.stack(
            [jnp.sum(valid * jnp.sum(v * v, -1)) for v in (wide, attention, d_middle)]
        )
        first += count

    low_two = jnp.concatenate(low_parts, 0)
    hidden = jnp.concatenate(hidden_parts, 0)
    d_units = jnp.concatenate(d_unit_parts, 0)
    d_attention = jnp.concatenate(d_attention_parts, 0)
    d_heads = jnp.concatenate(d_head_parts, 1)
    heads_out = jnp.concatenate(heads_parts, 1)
    lse = jnp.concatenate(lse_parts, 1)

    TN = (((0,), (0,)), ((), ()))

    def home(grad):
        part = lax.psum_scatter(grad, "z", scatter_dimension=0, tiled=True)
        part = part.reshape(part.shape[0], 4, width).transpose(1, 0, 2)
        return spread(part).reshape(-1, width)

    unit_grads = mm(d_units, low_two, TN).astype(BF)
    gate_grad = home(unit_grads[:units]).T.astype(F32)
    up_grad = home(unit_grads[units:]).T.astype(F32)
    down_grad = home(mm(hidden, upstream_rows, TN).astype(BF)).astype(F32)

    d_qkv, inner = attend_backward(
        info, qkv, keys, values, d_heads, heads_out, lse, cosine, sine, heads
    )
    partial = mm(d_qkv, join_weight, TN).astype(BF)
    join_grad = mm(d_qkv, low_one)
    before_local = jnp.sum(join_grad * join_weight.astype(F32), 0) / gain_one
    out_grad = mm(heads_out, d_attention)
    attend_grad = jnp.concatenate(
        [join_grad.reshape(heads, ROWS, depth), out_grad.reshape(heads, HD, depth)], 1
    ).astype(BF)
    if heads % 4 == 0:
        part = lax.psum_scatter(attend_grad, "z", scatter_dimension=0, tiled=True)
        part = part.reshape(heads // 4, 4, HD, 4, width).transpose(3, 1, 0, 2, 4)
        part = spread(part).transpose(1, 0, 2, 3, 4).reshape(4, head_width, width)
    else:
        part = attend_grad.reshape(heads, 4, HD, 4, width).transpose(3, 1, 0, 2, 4)
        part = spread(part.reshape(4, 4, heads * HD, width))
        part = lax.psum_scatter(part, "z", scatter_dimension=0, tiled=False)
    part = part.astype(F32)
    query_grad, key_grad, value_grad, output_grad = part[0].T, part[1].T, part[2].T, part[3]

    parts = partial.reshape(BLOCKS, team, sub, depth)
    inner = inner[0].reshape(BLOCKS, team, sub)
    d_middle = d_attention.reshape(BLOCKS, team, sub, depth)
    layer_out = jnp.concatenate(out_parts, 0)
    if quick:
        parts = straighten(parts, rank).reshape(2, -1, 4, width)
        pieces = []
        for k in range(8):
            piece = lax.dynamic_slice(
                parts,
                (y ^ (k >> 2), jnp.int32(0), row ^ (k & 3), jnp.int32(0)),
                (1, local_tokens, 1, width),
            )
            pieces.append(piece.reshape(local_tokens, width))
        d_one = team_scatter(pieces)
        inner = straighten(inner, rank).reshape(2, local_tokens)
        inner = row_sum(inner + flip(inner, "y"))
        inner = pick(inner, y)
        d_middle = lax.dynamic_slice(
            d_middle.reshape(2, BLOCKS // 2, team, sub, 4, width),
            (y, 0, 0, 0, row, 0),
            (1, BLOCKS // 2, team, sub, 1, width),
        ).reshape(BLOCKS // 2, team, sub, width)
        d_middle = straighten(d_middle, rank).reshape(local_tokens, width).astype(F32)
        layer_out = layer_out.reshape(2, local_tokens // team, 4, width).transpose(0, 2, 1, 3)
        layer_out = lax.all_to_all(
            layer_out.reshape(team, local_tokens // team, width), TEAM, 0, 0, tiled=True
        )
        layer_out = layer_out.reshape(team, BLOCKS // 2, sub, width).transpose(1, 0, 2, 3)
        layer_out = layer_out.reshape(local_tokens, width)
    else:
        d_one = lax.psum_scatter(
            parts.reshape(GTOK, depth), "y", scatter_dimension=0, tiled=True
        )
        d_one = lax.psum_scatter(d_one, ROW, scatter_dimension=1, tiled=True).astype(F32)
        inner = lax.psum(inner.reshape(GTOK), TEAM)
        inner = lax.dynamic_slice(inner, (y * local_tokens,), (local_tokens,))
        corner = (y * local_tokens, row * width)
        d_middle = lax.dynamic_slice(
            d_middle.reshape(GTOK, depth), corner, (local_tokens, width)
        ).astype(F32)
        layer_out = lax.all_gather(
            layer_out.reshape(BLOCKS, sub, depth), TEAM, axis=1, tiled=False
        ).reshape(GTOK, depth)
        layer_out = lax.dynamic_slice(layer_out, corner, (local_tokens, width))
    wide = hidden_in.astype(F32)
    scale_one = lax.rsqrt(row_sum(jnp.sum(wide * wide, -1)) / depth + EPSILON)[:, None]
    norm_one = wide * scale_one
    input_grad = d_middle + scale_one * (d_one * gain_before - norm_one * (inner / depth)[:, None])

    sums = lax.psum(jnp.concatenate([before_local, middle_local, squares]), EVERY)
    before_grad = lax.dynamic_slice(sums, (row * width,), (width,))
    middle_grad = lax.dynamic_slice(sums, (depth + row * width,), (width,))
    valid_count = (lengths.shape[0] * PROMPT + jnp.sum(lengths)).astype(F32)
    rms_values = jnp.sqrt(sums[2 * depth :] / (valid_count * depth))
    return (
        layer_out,
        input_grad,
        before_grad,
        query_grad,
        key_grad,
        value_grad,
        output_grad,
        middle_grad,
        gate_grad,
        up_grad,
        down_grad,
        rms_values,
    )


def solution(mesh):
    split = mesh.shape["col"] // GROUPS
    grid = Mesh(mesh.devices.reshape(2, 2, GROUPS, split), ("x", "c", "z", "y"))
    row, col = ("x", "c"), ("z", "y")
    return jax.shard_map(
        functools.partial(local, split == 2),
        mesh=grid,
        in_specs=(
            P(col, row),
            P(row),
            P(row, col),
            P(row, col),
            P(row, col),
            P(col, row),
            P(row),
            P(row, col),
            P(row, col),
            P(col, row),
            P(col, row),
            P(),
            P(),
        ),
        out_specs=(
            P(col, row),
            P(col, row),
            P(row),
            P(row, col),
            P(row, col),
            P(row, col),
            P(col, row),
            P(row),
            P(row, col),
            P(row, col),
            P(col, row),
            P(),
        ),
        check_vma=False,
    )
```

time: 5630 us -> 1690 us (0.30)
  waiting for transfers between devices: 4470 us -> 406 us
  matrix products: 629 us -> 324 us
  Pallas kernels: 0 us -> 268 us
  starting transfers between devices: 1.51 us -> 137 us
    reduce_scatter x8 -> x4, waiting for transfers between devices: 3100 us -> 0.03 us  [the longest x3 0.02 us: home(): part = lax.psum_scatter(grad, 'z', scatter_dimension=0, tiled=True)]
    all_gather x8 -> x4, waiting for transfers between devices: 1380 us -> 0.03 us  [the longest x1 0.02 us: local(): attend_weights = lax.all_gather(pieces, 'z', axis=0, tiled=True)]
    ppermute x0 -> x168, waiting for transfers between devices: none -> 406 us  [flip(): return lax.ppermute(values, axis, [(0, 1), (1, 0)])]
    pallas_call x0 -> x7, Pallas kernels: none -> 268 us  [the longest x1 118 us: attend_backward(): pl.pallas_call(functools.partial(backward_kernel, heads), grid=(BLOCKS,),...]
    dot_general x47 -> x34, matrix products: 557 us -> 324 us  [mm(): return lax.dot_general(a, b, dims, preferred_element_type=F32)]
    ppermute x0 -> x168, starting transfers between devices: none -> 132 us  [flip(): return lax.ppermute(values, axis, [(0, 1), (1, 0)])]
    reshape x1 -> x13, local copies, waits for them, and re-layouts: 116 us -> 43.1 us  [the longest x1 24.5 us: local(): parts = straighten(parts, rank).reshape(2, -1, 4, width)]
    sub x7 -> x0, matrix products: 72.9 us -> none  [block_forward(): weights = jnp.exp(shifted - peak)]
  transfers between devices with their start and end apart: 16 -> 177, of which waited for: 16 -> 70; matrix products, arithmetic and copies ran while one was open for 9% -> 46% of each run, Pallas kernels for 0% -> 16%
where the time goes in v1:
time: 1690 us; the launch traced here: 1680 us
  waiting for transfers between devices  406 us (24%)
  matrix products  324 us (19%)
  local copies, waits for them, and re-layouts  305 us (18%)
  Pallas kernels  268 us (16%)
  other arithmetic  180 us (11%)
  starting transfers between devices  137 us (8%)
  blocking collectives  44 us (3%)
  between operations  19.2 us (1%)
    ppermute x168, waiting for transfers between devices, flip(): return lax.ppermute(values, axis, [(0, 1), (1, 0)])  406 us
    dot_general x34, matrix products, mm(): return lax.dot_general(a, b, dims, preferred_element_type=F32)  324 us
    ppermute x168, starting transfers between devices, flip(): return lax.ppermute(values, axis, [(0, 1), (1, 0)])  132 us
    pallas_call x1, Pallas kernels, attend_backward(): pl.pallas_call(functools.partial(backward_kernel, heads), grid=(BLOCKS,),...  118 us
    pallas_call x4, Pallas kernels, attend_forward(): pl.pallas_call(functools.partial(forward_kernel, heads, first), grid=(cou...  114 us
    unnamed x434, local copies, waits for them, and re-layouts  66 us
    psum x1, blocking collectives, local(): lax.psum(jnp.concatenate([before_local, middle_local, squares]), EVERY)  44 us
    dynamic_slice x1, local copies, waits for them, and re-layouts, local(): lax.dynamic_slice(parts, (y ^ k >> 2, jnp.int32(0), row ^ k & 3, jnp.int3...  38.1 us
  transfers between devices with their start and end apart: 177, of which 70 were waited for; matrix products, arithmetic and copies ran while one was open for 46% of the time, Pallas kernels for 16%

profile of v1, /device:TPU:0, one launch (start us, length us, event | category | flops | bytes accessed | tf_op | source)
XLA Modules:
  0.0 1681.7 jit_solution(5062813665818076573)
XLA Ops:
  13.9 11.9 collective-permute-done.10
  34.4 12.2 collective-permute-done.25
  72.8 24.8 %collective-permute-done.3.refs_4_ = bf16[1792,512]{1,0:T(8,128)(2,1)} collective-permute-done((bf16[1792,512]{1,0:T(8,128)(2,1)S(1)}, bf16[1792,512]{1,0:T(8,128)(2,1)}, u32[]{:S(2)}, u32[]{:S(2)}) %collective-permute-start.3) | collective-permute-done | bytes 1835040 | tf_op jit(solution)/shard_map/ppermute | solution.py:259
  114.1 65.9 %collective-permute-done.8 = f32[2,512]{1,0:T(2,128)S(1)} collective-permute-done((f32[2,512]{1,0:T(2,128)S(1)}, f32[2,512]{1,0:T(2,128)S(1)}, u32[]{:S(2)}, u32[]{:S(2)}) %collective-permute-start.8) | collective-permute-done | bytes 4128 | tf_op jit(solution)/shard_map/ppermute | solution.py:259
  188.3 14.0 collective-permute-done.6
  243.2 17.2 %shard_map.225 = (bf16[3584,2048]{1,0:T(8,128)(2,1)}, bf16[448,2048]{1,0:T(8,128)(2,1)}) custom-call(s32[3]{0:T(128)} %pad_add_fusion.places, bf16[1792,512]{1,0:T(8,128)(2,1)} %refs_0_.3, bf16[1792,512]{1,0:T(8,128)(2,1)} %collective-permute-done.90.refs_1_, bf16[1792,512]{1,0:T(8,128)(2,1)} %collective-permute-done.91.refs_2_, ...), custom_call_target="tpu_custom_call" | custom-call | flops 44040192 | bytes 36700160 | tf_op jit(solution)/shard_map/pallas_call | solution.py:376
  260.4 18.6 %shard_map.220 = (bf16[3584,2048]{1,0:T(8,128)(2,1)}, bf16[448,2048]{1,0:T(8,128)(2,1)}) custom-call(s32[3]{0:T(128)} %pad_add_fusion.places, bf16[1792,512]{1,0:T(8,128)(2,1)} %refs_0_.2, bf16[1792,512]{1,0:T(8,128)(2,1)} %collective-permute-done.refs_1_, bf16[1792,512]{1,0:T(8,128)(2,1)} %collective-permute-done.1.refs_2_, ...), custom_call_target="tpu_custom_call" | custom-call | flops 44040192 | bytes 36700160 | tf_op jit(solution)/shard_map/pallas_call | solution.py:376
  283.1 25.6 %fusion.23 = f32[4,3,64,3584]{2,3,0,1:T(8,128)S(1)} fusion(bf16[3584,2048]{1,0:T(8,128)(2,1)} %get-tuple-element.29, bf16[4,3,64,2048]{3,2,1,0:T(8,128)(2,1)S(1)} %bitcast.1550), kind=kOutput, calls=%fused_computation.30 | convolution fusion | flops 11274289152 | bytes 28835840 | tf_op jit(solution)/shard_map/dot_general | solution.py:31
  354.8 34.7 %shard_map.222 = (bf16[256,1024]{1,0:T(8,128)(2,1)}, f32[8,1024]{1,0:T(8,128)}) custom-call(s32[16]{0:T(128)} %concatenate.170.info, bf16[768,3584]{1,0:T(8,128)(2,1)} %bitcast.1522, bf16[4,3584,64]{2,1,0:T(8,128)(2,1)} %get-tuple-element.165.knat), custom_call_target="tpu_custom_call" | custom-call | flops 6442450944 | bytes 16777216 | tf_op jit(solution)/shard_map/pallas_call | solution.py:105
  389.5 16.2 shard_map.221
  405.6 27.7 %shard_map.224 = (bf16[256,768]{1,0:T(8,128)(2,1)}, f32[8,768]{1,0:T(8,128)}) custom-call(s32[16]{0:T(128)} %concatenate.170.info, bf16[768,3584]{1,0:T(8,128)(2,1)} %bitcast.1524, bf16[4,3584,64]{2,1,0:T(8,128)(2,1)} %get-tuple-element.165.knat), custom_call_target="tpu_custom_call" | custom-call | flops 4831838208 | bytes 16777216 | tf_op jit(solution)/shard_map/pallas_call | solution.py:105
  433.3 35.1 %shard_map.223 = (bf16[256,768]{1,0:T(8,128)(2,1)}, f32[8,768]{1,0:T(8,128)}) custom-call(s32[16]{0:T(128)} %concatenate.170.info, bf16[768,3584]{1,0:T(8,128)(2,1)} %bitcast.1525, bf16[4,3584,64]{2,1,0:T(8,128)(2,1)} %get-tuple-element.165.knat), custom_call_target="tpu_custom_call" | custom-call | flops 4831838208 | bytes 16777216 | tf_op jit(solution)/shard_map/pallas_call | solution.py:105
  666.4 14.1 fusion.58
  862.7 18.4 %fusion.52 = bf16[1024,2048]{1,0:T(8,128)(2,1)} fusion(bf16[3584,2048]{1,0:T(8,128)(2,1)S(1)} %bitcast.1725, bf16[768,1024]{1,0:T(8,128)(2,1)} %copy-done.153, bf16[768,1024]{1,0:T(8,128)(2,1)} %copy-done.152, bf16[1024,1024]{1,0:T(8,128)(2,1)} %get-tuple-element.159, bf16[1024,1024]{1,0:T(8,128)(2,1)} %get-tuple-element.156), kind=kOutput, calls=%fused_computation.71 | convolution fusion | flops 15063842816 | bytes 26214400 | tf_op jit(solution)/shard_map/dot_general | solution.py:31
  888.2 84.1 %fusion.25 = bf16[2048,2048]{1,0:T(8,128)(2,1)} fusion(bf16[768,2048]{1,0:T(8,128)(2,1)} %bitcast.1715, bf16[768,2048]{1,0:T(8,128)(2,1)} %bitcast.1718, bf16[1024,2048]{1,0:T(8,128)(2,1)} %bitcast.1711, bf16[1024,2048]{1,0:T(8,128)(2,1)} %bitcast.1708, bf16[768,1024]{1,0:T(8,128)(2,1)} %get-tuple-element.172, bf16[768,1024]{1,0:T(8,128)(2,1)} %get-tuple-element.171, ...), kind=kOutput, calls=%fused_computation.34 | convolution fusion | flops 30245126144 | bytes 37748736 | tf_op jit(solution)/shard_map/dot_general | solution.py:31
  1159.7 118.2 %shard_map.226 = (bf16[768,3584]{1,0:T(8,128)(2,1)}, f32[8,3584]{1,0:T(8,128)}) custom-call(s32[16]{0:T(128)} %concatenate.170.info, bf16[768,3584]{1,0:T(8,128)(2,1)} %bitcast.1526, bf16[4,3584,64]{2,1,0:T(8,128)(2,1)} %get-tuple-element.165.knat, bf16[4,3584,64]{2,1,0:T(8,128)(2,1)} %get-tuple-element.164.vnat, ...), custom_call_target="tpu_custom_call" | custom-call | flops 56371445760 | bytes 33554432 | tf_op jit(solution)/shard_map/pallas_call | solution.py:225
  1277.9 14.8 convolution_convert_fusion
  1303.3 24.5 %reshape.999 = bf16[2,1792,4,512]{3,2,1,0:T(4,128)(2,1)} reshape(bf16[14,8,32,2048]{3,2,1,0:T(8,128)(2,1)} %dynamic-slice_dynamic-update-slice_fusion) | data formatting | bytes 29360128 | tf_op jit(solution)/shard_map/reshape | solution.py:617
  1327.8 38.1 %constant_dynamic-slice_fusion.21 = (bf16[1,1792,1,512]{3,2,1,0:T(2,128)(2,1)}, bf16[1,1792,1,512]{3,2,1,0:T(2,128)(2,1)}, bf16[1,1792,1,512]{3,2,1,0:T(2,128)(2...) fusion(bf16[2,1792,4,512]{3,2,1,0:T(4,128)(2,1)} %reshape.999, ...), kind=kLoop, calls=%fused_computation.735 | loop fusion | bytes 29360152 | tf_op jit(solution)/shard_map/dynamic_slice | solution.py:620
  1371.9 17.8 %fusion.203 = (bf16[768,2048]{1,0:T(8,128)(2,1)}, f32[2048]{0:T(1024)S(1)}) fusion(bf16[4,192,2048]{2,1,0:T(8,128)(2,1)S(1)} %copy-done.49, bf16[768,3584]{1,0:T(8,128)(2,1)} %get-tuple-element.40, bf16[3584,2048]{1,0:T(8,128)(2,1)} %get-tuple-element.29), kind=kOutput, calls=%fused_computation.847 | convolution fusion | flops 11280578560 | bytes 26484736 | tf_op jit(solution)/shard_map/dot_general | solution.py:31
  1389.7 30.8 %pad_maximum_fusion = bf16[3584,2048]{1,0:T(8,128)(2,1)S(1)} fusion(bf16[768,2048]{1,0:T(8,128)(2,1)S(1)} %bitcast.1547, bf16[768,2048]{1,0:T(8,128)(2,1)S(1)} %bitcast.1549, bf16[1024,2048]{1,0:T(8,128)(2,1)S(1)} %bitcast.1528, bf16[1024,2048]{1,0:T(8,128)(2,1)S(1)} %bitcast.1530), kind=kLoop, calls=%fused_computation.6 | loop fusion | flops 58720256 | bytes 29360128 | tf_op jit(solution)/shard_map/concatenate | solution.py:574
  1456.1 24.6 %reshape_reshape.19 = bf16[2,7,8,32,4,512]{5,4,3,2,1,0:T(4,128)(2,1)} reshape(bf16[3584,2048]{1,0:T(8,128)(2,1)} %copy-done.5) | data formatting | bytes 29360128 | tf_op jit(solution)/shard_map/reshape;reshape | solution.py:631
  1498.1 44.0 %psum.7 = f32[4099]{0:T(1024)S(1)} all-reduce(f32[4099]{0:T(1024)S(1)} %pad_maximum_fusion.54), channel_id=1, replica_groups=mesh['x'=2,'c'=2,'z'=4,'y'=2] {'x','c','z','y'}, use_global_device_ids=true, to_apply=%region_38.41 | all-reduce | flops 4099 | bytes 32792 | tf_op jit(solution)/shard_map/psum | solution.py:662
  1601.9 34.6 %collective-permute-done.160 = bf16[2,4,1,64,512]{4,3,0,1,2:T(8,128)(2,1)S(1)} collective-permute-done((bf16[2,4,1,64,512]{4,3,0,1,2:T(8,128)(2,1)S(1)}, bf16[2,4,1,64,512]{4,3,0,1,2:T(8,128)(2,1)S(1)}, u32[]{:S(2)}, u32[]{:S(2)}) %collective-permute-start.160) | collective-permute-done | bytes 524320 | tf_op jit(solution)/shard_map/ppermute | solution.py:259
  (1166 shorter events, 894.6 us)
Async XLA Ops:
  7.2 271.8 %all-gather.5.cloned.1.call-start = ((), (), s32[]{:S(2)}) async-start(), calls=%async_computation.5 | async-start | bytes 5242880 | tf_op jit(solution)/shard_map/all_gather | solution.py:466
  30.9 458.6 %all-gather.7.cloned.1.call-start = ((), (), s32[]{:S(2)}) async-start(), calls=%async_computation.6 | async-start | bytes 5242880 | tf_op jit(solution)/shard_map/all_gather | solution.py:477
  50.0 444.1 %all-gather.9.cloned.1.call-start = ((), (), s32[]{:S(2)}) async-start(), calls=%async_computation.7 | async-start | bytes 5242880 | tf_op jit(solution)/shard_map/all_gather | solution.py:477
  69.0 113.2 %collective-permute-start.93 = (bf16[1792,512]{1,0:T(8,128)(2,1)}, bf16[1792,512]{1,0:T(8,128)(2,1)}, u32[]{:S(2)}, u32[]{:S(2)}) collective-permute-start(bf16[1792,512]{1,0:T(8,128)(2,1)} %refs_0_.3), channel_id=1, source_target_pairs={{0,1},{1,0},{2,3},{3,2},{4,5},{5,4},{6,7},{7,6},{8,9},{9,8},{10,11... | collective-permute-start | bytes 5505032 | tf_op jit(solution)/shard_map/ppermute | solution.py:259
  70.5 111.2 %collective-permute-start.91 = (bf16[1792,512]{1,0:T(8,128)(2,1)}, bf16[1792,512]{1,0:T(8,128)(2,1)}, u32[]{:S(2)}, u32[]{:S(2)}) collective-permute-start(bf16[1792,512]{1,0:T(8,128)(2,1)} %refs_0_.3), channel_id=1, source_target_pairs={{0,16},{16,0},{1,17},{17,1},{2,18},{18,2},{3,19},{19,3},{4,20},{20... | collective-permute-start | bytes 5505032 | tf_op jit(solution)/shard_map/ppermute | solution.py:259
  72.2 527.1 %all-gather.11.cloned.1.call-start = ((), (), s32[]{:S(2)}) async-start(), calls=%async_computation.8 | async-start | bytes 5242880 | tf_op jit(solution)/shard_map/all_gather | solution.py:477
  99.8 84.7 %collective-permute-start.5 = (bf16[896,512]{1,0:T(8,128)(2,1)}, bf16[896,512]{1,0:T(8,128)(2,1)}, u32[]{:S(2)}, u32[]{:S(2)}) collective-permute-start(bf16[896,512]{1,0:T(8,128)(2,1)} %slice.1433), channel_id=1, source_target_pairs={{0,16},{16,0},{1,17},{17,1},{2,18},{18,2},{3,19},{19,3},{4,20},{20... | collective-permute-start | bytes 2752520 | tf_op jit(solution)/shard_map/ppermute | solution.py:259
  102.3 79.4 %collective-permute-start.29 = (bf16[2,256,512]{1,2,0:T(8,128)(2,1)}, bf16[2,256,512]{1,2,0:T(8,128)(2,1)S(1)}, u32[]{:S(2)}, u32[]{:S(2)}) collective-permute-start(bf16[2,256,512]{1,2,0:T(8,128)(2,1)} %bitcast.1682), channel_id=1, source_target_pairs={{0,16},{16,0},{1,17},{17,1},{2,18},{18,2},{3,19},{19,3},{4,20},{20... | collective-permute-start | bytes 1572872 | tf_op jit(solution)/shard_map/ppermute | solution.py:259
  110.2 69.8 %collective-permute-start.8 = (f32[2,512]{1,0:T(2,128)S(1)}, f32[2,512]{1,0:T(2,128)S(1)}, u32[]{:S(2)}, u32[]{:S(2)}) collective-permute-start(f32[2,512]{1,0:T(2,128)S(1)} %get-tuple-element.446), channel_id=1, source_target_pairs={{0,16},{16,0},{1,17},{17,1},{2,18},{18,2},{3,19},{19,3},{4,20},{20... | collective-permute-start | bytes 12296 | tf_op jit(solution)/shard_map/ppermute | solution.py:259
  242.9 1299.3 %reduce-scatter.11.cloned.1.call-start = ((), (), s32[]{:S(2)}) async-start(), calls=%async_computation.12 | async-start | bytes 5242880 | tf_op jit(solution)/shard_map/reduce_scatter | solution.py:582
  622.5 69.9 %collective-permute-start.124 = (bf16[4,96,2048]{2,1,0:T(8,128)(2,1)}, bf16[4,96,2048]{2,1,0:T(8,128)(2,1)}, u32[]{:S(2)}, u32[]{:S(2)}) collective-permute-start(bf16[4,96,2048]{2,1,0:T(8,128)(2,1)} %pad_maximum_fusion.17), channel_id=1, source_target_pairs={{0,8},{8,0},{1,9},{9,1},{2,10},{10,2},{3,11},{11,3},{4,12},{12,4},... | collective-permute-start | bytes 4718600 | tf_op jit(solution)/shard_map/ppermute | solution.py:259
  629.4 68.7 %collective-permute-start.67 = (bf16[4,96,2048]{2,1,0:T(8,128)(2,1)}, bf16[4,96,2048]{2,1,0:T(8,128)(2,1)}, u32[]{:S(2)}, u32[]{:S(2)}) collective-permute-start(bf16[4,96,2048]{2,1,0:T(8,128)(2,1)} %pad_maximum_fusion.14), channel_id=1, source_target_pairs={{0,8},{8,0},{1,9},{9,1},{2,10},{10,2},{3,11},{11,3},{4,12},{12,4},... | collective-permute-start | bytes 4718600 | tf_op jit(solution)/shard_map/ppermute | solution.py:259
  684.5 93.1 %collective-permute-start.98 = (bf16[4,128,2048]{2,1,0:T(8,128)(2,1)S(1)}, bf16[4,128,2048]{2,1,0:T(8,128)(2,1)}, u32[]{:S(2)}, u32[]{:S(2)}) collective-permute-start(bf16[4,128,2048]{2,1,0:T(8,128)(2,1)S(1)} %pad_maximum_fusion.7), channel_id=1, source_target_pairs={{0,8},{8,0},{1,9},{9,1},{2,10},{10,2},{3,11},{11,3},{4,12},{12,4},... | collective-permute-start | bytes 6291464 | tf_op jit(solution)/shard_map/ppermute | solution.py:259
  692.2 90.3 %collective-permute-start.31 = (bf16[4,128,2048]{2,1,0:T(8,128)(2,1)S(1)}, bf16[4,128,2048]{2,1,0:T(8,128)(2,1)S(1)}, u32[]{:S(2)}, u32[]{:S(2)}) collective-permute-start(bf16[4,128,2048]{2,1,0:T(8,128)(2,1)S(1)} %pad_maximum_fusion.4), channel_id=1, source_target_pairs={{0,8},{8,0},{1,9},{9,1},{2,10},{10,2},{3,11},{11,3},{4,12},{12,4},... | collective-permute-start | bytes 6291464 | tf_op jit(solution)/shard_map/ppermute | solution.py:259
  818.5 62.7 %collective-permute-start.85 = (bf16[4,96,2048]{2,1,0:T(8,128)(2,1)}, bf16[4,96,2048]{2,1,0:T(8,128)(2,1)S(1)}, u32[]{:S(2)}, u32[]{:S(2)}) collective-permute-start(bf16[4,96,2048]{2,1,0:T(8,128)(2,1)} %pad_maximum_fusion.16), channel_id=1, source_target_pairs={{0,8},{8,0},{1,9},{9,1},{2,10},{10,2},{3,11},{11,3},{4,12},{12,4},... | collective-permute-start | bytes 4718600 | tf_op jit(solution)/shard_map/ppermute | solution.py:259
  818.5 160.1 %collective-permute-start.137 = (bf16[4,96,2048]{2,1,0:T(8,128)(2,1)}, bf16[4,96,2048]{2,1,0:T(8,128)(2,1)}, u32[]{:S(2)}, u32[]{:S(2)}) collective-permute-start(bf16[4,96,2048]{2,1,0:T(8,128)(2,1)} %pad_maximum_fusion.18), channel_id=1, source_target_pairs={{0,8},{8,0},{1,9},{9,1},{2,10},{10,2},{3,11},{11,3},{4,12},{12,4},... | collective-permute-start | bytes 4718600 | tf_op jit(solution)/shard_map/ppermute | solution.py:259
  881.1 669.6 %reduce-scatter.9.cloned.1.call-start = ((), (), s32[]{:S(2)}) async-start(), calls=%async_computation.11 | async-start | bytes 5242880 | tf_op jit(solution)/shard_map/reduce_scatter | solution.py:582
  885.4 97.3 %collective-permute-start.88 = (bf16[2,48,2048]{2,1,0:T(8,128)(2,1)}, bf16[2,48,2048]{2,1,0:T(8,128)(2,1)}, u32[]{:S(2)}, u32[]{:S(2)}) collective-permute-start(bf16[2,48,2048]{2,1,0:T(8,128)(2,1)} %pad_maximum_fusion.48), channel_id=1, source_target_pairs={{0,1},{1,0},{2,3},{3,2},{4,5},{5,4},{6,7},{7,6},{8,9},{9,8},{10,11... | collective-permute-start | bytes 1179656 | tf_op jit(solution)/shard_map/ppermute | solution.py:259
  886.9 98.3 %collective-permute-start.86 = (bf16[2,48,2048]{2,1,0:T(8,128)(2,1)}, bf16[2,48,2048]{2,1,0:T(8,128)(2,1)}, u32[]{:S(2)}, u32[]{:S(2)}) collective-permute-start(bf16[2,48,2048]{2,1,0:T(8,128)(2,1)} %pad_maximum_fusion.47), channel_id=1, source_target_pairs={{0,16},{16,0},{1,17},{17,1},{2,18},{18,2},{3,19},{19,3},{4,20},{20... | collective-permute-start | bytes 1179656 | tf_op jit(solution)/shard_map/ppermute | solution.py:259
  978.5 579.3 %reduce-scatter.7.cloned.1.call-start = ((), (), s32[]{:S(2)}) async-start(), calls=%async_computation.10 | async-start | bytes 5242880 | tf_op jit(solution)/shard_map/reduce_scatter | solution.py:582
  1018.5 574.6 %reduce-scatter.5.cloned.1.call-start = ((), (), s32[]{:S(2)}) async-start(), calls=%async_computation.9 | async-start | bytes 5242880 | tf_op jit(solution)/shard_map/reduce_scatter | solution.py:602
  1128.9 303.3 %collective-permute-start.150 = (f32[1792]{0:T(1024)}, f32[1792]{0:T(1024)}, u32[]{:S(2)}, u32[]{:S(2)}) collective-permute-start(f32[1792]{0:T(1024)} %fusion.61), channel_id=1, source_target_pairs={{0,16},{16,0},{1,17},{17,1},{2,18},{18,2},{3,19},{19,3},{4,20},{20... | collective-permute-start | bytes 21512 | tf_op jit(solution)/shard_map/ppermute | solution.py:259
  1371.7 194.3 %collective-permute-start.152 = (bf16[4,1792,512]{2,1,0:T(8,128)(2,1)}, bf16[4,1792,512]{2,1,0:T(8,128)(2,1)}, u32[]{:S(2)}, u32[]{:S(2)}) collective-permute-start(bf16[4,1792,512]{2,1,0:T(8,128)(2,1)} %pad_maximum_fusion.1), channel_id=1, source_target_pairs={{0,8},{8,0},{1,9},{9,1},{2,10},{10,2},{3,11},{11,3},{4,12},{12,4},... | collective-permute-start | bytes 22020104 | tf_op jit(solution)/shard_map/ppermute | solution.py:259
  1443.5 144.3 %all-to-all-start = ((bf16[8,224,512]{2,1,0:T(8,128)(2,1)}), bf16[8,224,512]{2,1,0:T(8,128)(2,1)S(1)}, u32[]{:S(2)}, u32[]{:S(2)}) async-start(bf16[8,224,512]{2,1,0:T(8,128)(2,1)} %bitcast.1521), calls=%async_computation | async-start | bytes 3670016 | tf_op jit(solution)/shard_map/all_to_all | solution.py:637
  (319 other events, 4793.2 us)
Sparse Core Ops, SparseCore 0:
  31.0 82.2 all-gather.4
  114.9 79.0 all-gather.6
  195.6 78.7 all-gather.8
  275.8 78.7 all-gather.10
  881.2 79.3 reduce-scatter.10
  978.6 79.0 reduce-scatter.8
  1060.0 77.2 reduce-scatter.6
  1430.4 81.9 reduce-scatter.4

commit v2 on v1

v2 whole, which is shorter than its diff:
```python
import functools
import jax
import jax.numpy as jnp
from jax import lax
from jax.experimental import pallas as pl
from jax.experimental.pallas import tpu as pltpu
from jax.sharding import Mesh
from jax.sharding import PartitionSpec as P

HD = 64
PROMPT = 2048
CLEN = 256
CONTS = 6
GTOK = 3584
BLK = 256
PBLKS = PROMPT // BLK
BLOCKS = GTOK // BLK
ROWS = 3 * HD
BF = jnp.bfloat16
F32 = jnp.float32
LOW = -1e30
LOG2E = 1.4426950408889634
FACTOR = HD ** (-0.5) * LOG2E
VMEM_LIMIT = 56 * 1024 * 1024

NN = (((1,), (0,)), ((), ()))
NT = (((1,), (1,)), ((), ()))
TN = (((0,), (0,)), ((), ()))


def mm(a, b, dims=NN):
    return lax.dot_general(a, b, dims, preferred_element_type=F32)


def block_plan(info, block):
    cont = jnp.maximum(block - PBLKS, 0)
    is_cont = block >= PBLKS
    reach = info[cont]
    full = jnp.where(is_cont, reach // BLK, block)
    rest = jnp.where(is_cont, reach - full * BLK, 0)
    limit = jnp.where(is_cont, info[CONTS + cont], BLK)
    masked = 1 + (rest > 0).astype(jnp.int32)
    return full, rest, limit, masked


def local_ids(info, shape, axis):
    return lax.broadcasted_iota(jnp.int32, shape, axis) ^ info[2 * CONTS]


def masked_step(info, block, full, rest, limit, index):
    own = index == 0
    target = jnp.where(own, block, full)
    query_ids = local_ids(info, (1, BLK), 1)
    bound = jnp.where(own, jnp.minimum(query_ids + 1, limit), rest)
    key_ids = local_ids(info, (BLK, BLK), 0)
    return target, key_ids < bound


def columns(block):
    return pl.ds(pl.multiple_of(block * BLK, BLK), BLK)


def forward_kernel(heads, first, info, qkv, knat, out, lse, acc, top, tot):
    block = pl.program_id(0) + first
    full, rest, limit, masked = block_plan(info, block)
    here = columns(block)
    acc[...] = jnp.zeros_like(acc)
    top[...] = jnp.full_like(top, LOW)
    tot[...] = jnp.zeros_like(tot)

    def step(target, allowed, wide=1):
        span = pl.ds(pl.multiple_of(target * BLK, BLK), wide * BLK)
        weights, shrinks = [], []
        scores = [
            mm(knat[h, span, :], qkv[h * ROWS : h * ROWS + HD, here]) for h in range(heads)
        ]
        for h in range(heads):
            score = scores[h] * FACTOR
            if allowed is not None:
                score = jnp.where(allowed, score, LOW)
            old = top[h : h + 1, :]
            new = jnp.maximum(old, jnp.max(score, 0, keepdims=True))
            weight = jnp.exp2(score - new)
            shrink = jnp.exp2(old - new)
            top[h : h + 1, :] = new
            tot[h : h + 1, :] = tot[h : h + 1, :] * shrink + jnp.sum(weight, 0, keepdims=True)
            weights.append(weight.astype(BF))
            shrinks.append(shrink)
        for h in range(heads):
            value = qkv[h * ROWS + 2 * HD : (h + 1) * ROWS, span]
            acc[h] = acc[h] * shrinks[h] + mm(value, weights[h])

    def full_step(index, carry):
        step(index, None)
        return carry

    def mask_step(index, carry):
        target, allowed = masked_step(info, block, full, rest, limit, index)
        step(target, allowed)
        return carry

    def wide_step(index, carry):
        step(index * 4, None, 4)
        return carry

    lax.fori_loop(0, full // 4, wide_step, 0)
    lax.fori_loop(full // 4 * 4, full, full_step, 0)
    lax.fori_loop(0, masked, mask_step, 0)
    for h in range(heads):
        total = tot[h : h + 1, :]
        out[h * HD : (h + 1) * HD, :] = (acc[h] / total).astype(BF)
        lse[h : h + 1, :] = top[h : h + 1, :] + jnp.log2(total)


def attend_forward(info, qkv, knat, heads, first, count):
    pad = max(8, heads)
    return pl.pallas_call(
        functools.partial(forward_kernel, heads, first),
        grid=(count,),
        in_specs=[
            pl.BlockSpec(memory_space=pltpu.SMEM),
            pl.BlockSpec(qkv.shape, lambda i: (0, 0)),
            pl.BlockSpec(knat.shape, lambda i: (0, 0, 0)),
        ],
        out_specs=[
            pl.BlockSpec((heads * HD, BLK), lambda i: (0, i)),
            pl.BlockSpec((pad, BLK), lambda i: (0, i)),
        ],
        out_shape=[
            jax.ShapeDtypeStruct((heads * HD, count * BLK), BF),
            jax.ShapeDtypeStruct((pad, count * BLK), F32),
        ],
        scratch_shapes=[
            pltpu.VMEM((heads, HD, BLK), F32),
            pltpu.VMEM((pad, BLK), F32),
            pltpu.VMEM((pad, BLK), F32),
        ],
        compiler_params=pltpu.CompilerParams(vmem_limit_bytes=VMEM_LIMIT),
        cost_estimate=pl.CostEstimate(
            flops=heads * count * 6 * BLK * BLK * 2560,
            bytes_accessed=16 << 20,
            transcendentals=heads * count * 6 * BLK * BLK,
        ),
    )(info, qkv, knat)


def turn(values, cosine, sine, at):
    half = HD // 2
    cos, sin = cosine[:, at], sine[:, at]
    former, latter = values[:half], values[half:]
    return former * cos + latter * sin, latter * cos - former * sin


def backward_kernel(heads, first, final, info, qkv, knat, vnat, d_out, heads_out, lse, cosine, sine, *refs):
    if final:
        d_old_keys, d_old_values, d_old_query, old_inner, d_qkv, inner, d_keys, d_values, d_query = refs
    else:
        d_keys, d_values, d_turned, share_out, d_query = refs
    block = pl.program_id(0) + first
    full, rest, limit, masked = block_plan(info, block)
    here = columns(block)
    there = columns(pl.program_id(0))

    @pl.when(pl.program_id(0) == 0)
    def _():
        if final:
            d_keys[...] = d_old_keys[...]
            d_values[...] = d_old_values[...]
            inner[...] = jnp.zeros_like(inner)
        else:
            d_keys[...] = jnp.zeros_like(d_keys)
            d_values[...] = jnp.zeros_like(d_values)

    d_query[...] = jnp.zeros_like(d_query)
    deltas = []
    for h in range(heads):
        rows = slice(h * HD, (h + 1) * HD)
        deltas.append(
            jnp.sum(d_out[rows, there].astype(F32) * heads_out[rows, here].astype(F32), 0, keepdims=True)
        )

    def step(target, allowed, wide=1):
        span = pl.ds(pl.multiple_of(target * BLK, BLK), wide * BLK)
        for first in range(0, heads, 4):
            team = range(first, min(first + 4, heads))
            scores = [
                mm(knat[h, span, :], qkv[h * ROWS : h * ROWS + HD, here]) for h in team
            ]
            d_probs = [
                mm(vnat[h, span, :], d_out[h * HD : (h + 1) * HD, there]) for h in team
            ]
            low_probs, d_scores = [], []
            for h, score, d_prob in zip(team, scores, d_probs):
                score = score * FACTOR - lse[h : h + 1, here]
                if allowed is not None:
                    score = jnp.where(allowed, score, LOW)
                probs = jnp.exp2(score)
                low_probs.append(probs.astype(BF))
                d_scores.append((probs * (d_prob - deltas[h])).astype(BF))
            for h, low, d_score in zip(team, low_probs, d_scores):
                rows = slice(h * HD, (h + 1) * HD)
                query = qkv[h * ROWS : h * ROWS + HD, here]
                key = qkv[h * ROWS + HD : h * ROWS + 2 * HD, span]
                d_query[h] += mm(key, d_score)
                d_keys[rows, span] += mm(query, d_score, NT)
                d_values[rows, span] += mm(d_out[rows, there], low, NT)

    def full_step(index, carry):
        step(index, None)
        return carry

    def mask_step(index, carry):
        target, allowed = masked_step(info, block, full, rest, limit, index)
        step(target, allowed)
        return carry

    def wide_step(index, carry):
        step(index * 2, None, 2)
        return carry

    lax.fori_loop(0, full // 2, wide_step, 0)
    lax.fori_loop(full // 2 * 2, full, full_step, 0)
    lax.fori_loop(0, masked, mask_step, 0)

    half = HD // 2
    share = jnp.zeros((1, BLK), F32)
    for h in range(heads):
        start = h * ROWS
        values = d_query[h] * HD ** (-0.5)
        share += jnp.sum(values * qkv[start : start + HD, here].astype(F32), 0, keepdims=True)
        low, high = turn(values, cosine, sine, here)
        if final:
            d_qkv[start : start + half, here] = low.astype(BF)
            d_qkv[start + half : start + HD, here] = high.astype(BF)
        else:
            d_turned[h * HD : h * HD + half, :] = low.astype(BF)
            d_turned[h * HD + half : (h + 1) * HD, :] = high.astype(BF)
    if not final:
        share_out[0:1, :] = share
        return
    inner[0:1, here] = share

    @pl.when(block == PBLKS - 1)
    def _():
        inner[:, PROMPT:] = old_inner[...]
        for h in range(heads):
            d_qkv[h * ROWS : h * ROWS + HD, PROMPT:] = d_old_query[h * HD : (h + 1) * HD, :]

        def finish(index, carry):
            at = columns(index)
            share = inner[0:1, at]
            for h in range(heads):
                start = h * ROWS + HD
                rows = slice(h * HD, (h + 1) * HD)
                values = d_keys[rows, at] * HD ** (-0.5)
                share += jnp.sum(values * qkv[start : start + HD, at].astype(F32), 0, keepdims=True)
                low, high = turn(values, cosine, sine, at)
                d_qkv[start : start + half, at] = low.astype(BF)
                d_qkv[start + half : start + HD, at] = high.astype(BF)
                start += HD
                values = d_values[rows, at]
                share += jnp.sum(values * qkv[start : start + HD, at].astype(F32), 0, keepdims=True)
                d_qkv[start : start + HD, at] = values.astype(BF)
            inner[0:1, at] = share
            return carry

        lax.fori_loop(0, BLOCKS, finish, 0)


def attend_backward(info, operands, heads, before=None):
    whole = lambda a: pl.BlockSpec(a.shape, lambda i, n=len(a.shape): (0,) * n)
    final = before is not None
    operands = tuple(operands) + (tuple(before) if final else ())
    sums = jax.ShapeDtypeStruct((heads * HD, GTOK), F32)
    rest = GTOK - PROMPT
    if final:
        shapes = [jax.ShapeDtypeStruct((heads * ROWS, GTOK), BF), jax.ShapeDtypeStruct((8, GTOK), F32)]
        specs = [whole(a) for a in shapes]
        scratch = [pltpu.VMEM(sums.shape, F32), pltpu.VMEM(sums.shape, F32)]
    else:
        shapes = [sums, sums, jax.ShapeDtypeStruct((heads * HD, rest), BF), jax.ShapeDtypeStruct((8, rest), F32)]
        specs = [whole(sums), whole(sums)]
        specs += [
            pl.BlockSpec((heads * HD, BLK), lambda i: (0, i)),
            pl.BlockSpec((8, BLK), lambda i: (0, i)),
        ]
        scratch = []
    return pl.pallas_call(
        functools.partial(backward_kernel, heads, 0 if final else PBLKS, final),
        grid=(PBLKS if final else CONTS,),
        in_specs=[pl.BlockSpec(memory_space=pltpu.SMEM)] + [whole(a) for a in operands],
        out_specs=specs,
        out_shape=shapes,
        scratch_shapes=scratch + [pltpu.VMEM((heads, HD, BLK), F32)],
        compiler_params=pltpu.CompilerParams(vmem_limit_bytes=VMEM_LIMIT),
        cost_estimate=pl.CostEstimate(
            flops=heads * BLOCKS * 3 * BLK * BLK * 4096,
            bytes_accessed=32 << 20,
            transcendentals=heads * BLOCKS * 3 * BLK * BLK,
        ),
    )(info, *operands)


def project_kernel(heads, weight, low, cosine, sine, qkv, knat, vnat):
    raw = mm(weight[...], low[...], NT)
    half = HD // 2
    cos, sin = cosine[...], sine[...]
    for h in range(heads):
        for part in range(2):
            start = h * ROWS + part * HD
            former, latter = raw[start : start + half], raw[start + half : start + HD]
            turned = jnp.concatenate(
                [former * cos - latter * sin, latter * cos + former * sin], 0
            )
            qkv[start : start + HD, :] = turned.astype(BF)
            if part:
                knat[h] = turned.T.astype(BF)
        start = h * ROWS + 2 * HD
        value = raw[start : start + HD]
        qkv[start : start + HD, :] = value.astype(BF)
        vnat[h] = value.T.astype(BF)


def project(weight, low, cosine, sine, heads):
    depth = weight.shape[1]
    natural = jax.ShapeDtypeStruct((heads, GTOK, HD), BF)
    return pl.pallas_call(
        functools.partial(project_kernel, heads),
        grid=(BLOCKS,),
        in_specs=[
            pl.BlockSpec(weight.shape, lambda i: (0, 0)),
            pl.BlockSpec((BLK, depth), lambda i: (i, 0)),
            pl.BlockSpec((HD // 2, BLK), lambda i: (0, i)),
            pl.BlockSpec((HD // 2, BLK), lambda i: (0, i)),
        ],
        out_specs=[pl.BlockSpec((heads * ROWS, BLK), lambda i: (0, i))]
        + [pl.BlockSpec((heads, BLK, HD), lambda i: (0, i, 0))] * 2,
        out_shape=[jax.ShapeDtypeStruct((heads * ROWS, GTOK), BF), natural, natural],
        compiler_params=pltpu.CompilerParams(vmem_limit_bytes=VMEM_LIMIT),
        cost_estimate=pl.CostEstimate(
            flops=2 * GTOK * depth * heads * ROWS, bytes_accessed=3 * GTOK * depth, transcendentals=0
        ),
    )(weight, low, cosine, sine)


EPSILON = 1e-05
THETA = 130000.0
GROUPS = 4
CHUNKS = ((8, 3), (11, 3), (0, 4), (4, 4))
ROW = ("x", "c")
TEAM = ("y", "x", "c")
EVERY = ("x", "c", "z", "y")


def after(values, *earlier):
    return lax.optimization_barrier((values, earlier))[0]


def flip(values, axis):
    return lax.ppermute(values, axis, [(0, 1), (1, 0)])


def send(values, axis):
    if axis == "z1":
        return lax.ppermute(values, "z", [(0, 1), (1, 0), (2, 3), (3, 2)])
    if axis == "z2":
        return lax.ppermute(values, "z", [(0, 2), (1, 3), (2, 0), (3, 1)])
    return flip(values, axis)


def pick(stack, index, axis=0):
    return lax.dynamic_index_in_dim(stack, index, axis, keepdims=False)


def in_order(mine, other, bit, axis):
    return jnp.where(
        bit == 0, jnp.stack([mine, other], axis), jnp.stack([other, mine], axis)
    )


def spread_steps(pieces):
    x, c = lax.axis_index("x"), lax.axis_index("c")
    pieces = pieces.reshape((2, 2) + pieces.shape[1:])
    (got,) = yield [(pick(pieces, 1 - x), "x")]
    pieces = in_order(pick(pieces, x), got, x, 0)
    (got,) = yield [(pick(pieces, 1 - c, 1), "c")]
    pieces = in_order(pick(pieces, c, 1), got, c, 1)
    return pieces.reshape((4,) + pieces.shape[2:])


def complete(steps):
    try:
        wanted = next(steps)
        while True:
            wanted = steps.send([flip(*w) for w in wanted])
    except StopIteration as end:
        return end.value


def spread(pieces):
    return complete(spread_steps(pieces))


class Lines:
    def __init__(self):
        self.wanted = {}
        self.flying = {}
        self.results = {}
        self.last = []
        self.extra = []

    def start(self, name, steps):
        self.wanted[name] = (steps, next(steps))

    def launch(self, name):
        steps, wanted = self.wanted.pop(name)
        wanted = [(after(v, *self.last) if self.last else v, axis) for v, axis in wanted]
        self.extra += [v for v, _ in wanted]
        self.flying[name] = (steps, [send(v, axis) for v, axis in wanted])

    def land(self, name):
        steps, got = self.flying.pop(name)
        self.proceed(name, steps, after(got, *self.last))

    def proceed(self, name, steps, got):
        try:
            self.wanted[name] = (steps, steps.send(got))
        except StopIteration as end:
            self.results[name] = end.value
            value = end.value[-1] if isinstance(end.value, list) else end.value
            if value is not None:
                self.extra.append(value)

    def tick(self, large, *names):
        if large is None:
            for name in names:
                steps, wanted = self.wanted.pop(name)
                wanted = [(after(v, *self.last) if self.last else v, axis) for v, axis in wanted]
                self.proceed(name, steps, [send(*w) for w in wanted])
            return None
        sent = {}
        for name in names:
            steps, wanted = self.wanted.pop(name)
            sent[name] = (steps, [(after(v, *self.last) if self.last else v, axis) for v, axis in wanted])
        operands = [v for _, part in sent.values() for v, _ in part]
        done = large(self.last + self.extra + operands)
        self.extra = []
        self.last = [done[0] if isinstance(done, (tuple, list)) else done]
        for name, (steps, wanted) in sent.items():
            self.proceed(name, steps, after([send(*w) for w in wanted], *self.last))
        return done


def row_gather(values):
    x, c = lax.axis_index("x"), lax.axis_index("c")
    pair = in_order(values, flip(values, "x"), x, 0)
    four = in_order(pair, flip(pair, "c"), c, 1)
    return four.reshape((4,) + values.shape)


def row_sum(values):
    values = values + flip(values, "x")
    return values + flip(values, "c")


def halves(values):
    middle = values.shape[0] // 2
    return values[:middle], values[middle:]


def place_steps(own):
    from_x, from_y, from_c = yield [(own, "x"), (own, "y"), (own, "c")]
    former, latter, by_x, by_y = yield [
        (halves(from_y)[0], "x"),
        (halves(from_x)[1], "y"),
        (from_x, "c"),
        (from_y, "c"),
    ]
    corner = jnp.concatenate([former, latter], 0)
    (other,) = yield [(corner, "c")]
    return [own, from_c, from_x, by_x, from_y, by_y, corner, other]


def gather_steps(own):
    from_x, from_y = yield [(own, "x"), (own, "y")]
    former, latter = yield [(halves(from_y)[0], "x"), (halves(from_x)[1], "y")]
    four = jnp.concatenate([own, from_x, from_y, former, latter], 0)
    (other,) = yield [(four, "c")]
    return [four, other]


def sum_steps(keep, send):
    (got,) = yield [(send, "c")]
    sums = [halves(keep[k].astype(F32) + got[k].astype(F32)) for k in range(4)]
    to_x = jnp.stack([sums[1][0], sums[3][0]]).astype(BF)
    to_y = jnp.stack([sums[2][1], sums[3][1]]).astype(BF)
    by_x, by_y = yield [(to_x, "x"), (to_y, "y")]
    over_y = (sums[2][0] + by_x[1].astype(F32)).astype(BF)
    over_x = (sums[1][1] + by_y[1].astype(F32)).astype(BF)
    former = sums[0][0] + by_x[0].astype(F32)
    latter = sums[0][1] + by_y[0].astype(F32)
    by_y, by_x = yield [(over_y, "y"), (over_x, "x")]
    return jnp.concatenate([former + by_y.astype(F32), latter + by_x.astype(F32)], 0)


def norm_kernel(mode, heads, places, *refs):
    own, other, refs = refs[:4], refs[4:8], refs[8:]
    if mode:
        gain, weight, cosine, sine, low, share, qkv, knat, vnat, whole = refs
    else:
        low, share, whole = refs
    half, row, rank = places[0], places[1], places[2]
    mine = pl.program_id(0) // (BLOCKS // 2) == half
    width = own[0].shape[1]

    def place(sources):
        for k, source in enumerate(sources):
            at = pl.multiple_of((row ^ k) * width, width)
            whole[:, pl.ds(at, width)] = source[...]

    @pl.when(mine)
    def _():
        place(own)

    @pl.when(jnp.logical_not(mine))
    def _():
        place(other)

    sub = share.shape[0]
    for k in range(BLK // sub):
        at = pl.multiple_of((rank ^ k) * sub, sub)
        rows = whole[pl.ds(at, sub), :]
        if k == 0:
            share[...] = rows
        if not mode:
            low[k * sub : (k + 1) * sub, :] = rows
        else:
            wide = rows.astype(F32)
            scale = lax.rsqrt(jnp.sum(wide * wide, 1, keepdims=True) / wide.shape[1] + EPSILON)
            low[k * sub : (k + 1) * sub, :] = (wide * scale * gain[...]).astype(BF)
    if mode:
        project_kernel(heads, weight, low, cosine, sine, qkv, knat, vnat)


def assemble(places, pieces, gain, sub, projection=(), heads=0):
    per = BLOCKS // 2
    width = pieces[0].shape[1]
    whole = 4 * width
    mode = gain is not None

    def own_map(i, places):
        return jnp.where(i // per == places[0], i % per, 0), 0

    def other_map(i, places):
        return jnp.where(i // per == places[0], 0, i % per), 0

    operands = list(pieces)
    specs = [pl.BlockSpec((BLK, width), own_map)] * 4 + [pl.BlockSpec((BLK, width), other_map)] * 4
    outs = [pl.BlockSpec((BLK, whole), lambda i, p: (i, 0)), pl.BlockSpec((sub, whole), lambda i, p: (i, 0))]
    shapes = [jax.ShapeDtypeStruct((GTOK, whole), BF), jax.ShapeDtypeStruct((BLOCKS * sub, whole), BF)]
    flops = 0
    if mode:
        table = pl.BlockSpec((HD // 2, BLK), lambda i, p: (0, i))
        specs += [pl.BlockSpec((1, whole), lambda i, p: (0, 0))]
        specs += [pl.BlockSpec(projection[0].shape, lambda i, p: (0, 0)), table, table]
        operands += [gain.reshape(1, whole), *projection]
        outs += [pl.BlockSpec((heads * ROWS, BLK), lambda i, p: (0, i))]
        outs += [pl.BlockSpec((heads, BLK, HD), lambda i, p: (0, i, 0))] * 2
        natural = jax.ShapeDtypeStruct((heads, GTOK, HD), BF)
        shapes += [jax.ShapeDtypeStruct((heads * ROWS, GTOK), BF), natural, natural]
        flops = 2 * GTOK * whole * heads * ROWS
    return pl.pallas_call(
        functools.partial(norm_kernel, mode, heads),
        grid_spec=pltpu.PrefetchScalarGridSpec(
            num_scalar_prefetch=1,
            grid=(BLOCKS,),
            in_specs=specs,
            out_specs=outs,
            scratch_shapes=[pltpu.VMEM((BLK, whole), BF)],
        ),
        out_shape=shapes,
        compiler_params=params(),
        cost_estimate=cost(flops + GTOK * whole * 6, GTOK * whole * 5),
    )(places, *operands)


def straighten(values, rank):
    count = values.shape[1]
    return jnp.stack([pick(values, j ^ rank, 1) for j in range(count)], 1)


def whole_spec(shape):
    return pl.BlockSpec(shape, lambda *i, n=len(shape): (0,) * n)


def cost(flops, bytes_accessed, transcendentals=0):
    return pl.CostEstimate(
        flops=int(flops), bytes_accessed=int(bytes_accessed), transcendentals=int(transcendentals)
    )


def params():
    return pltpu.CompilerParams(vmem_limit_bytes=VMEM_LIMIT)


def split_kernel(pairs, form, sub, *refs):
    keep, send = refs[2 * pairs :]
    total = mm(refs[0][...], refs[1][...], form)
    for p in range(1, pairs):
        total += mm(refs[2 * p][...], refs[2 * p + 1][...], form)
    low = total.astype(BF)
    for b in range(low.shape[0] // BLK):
        for k in range(8):
            target = send if k % 2 else keep
            start = b * BLK + k * sub
            target[k // 2, b * sub : (b + 1) * sub, :] = low[start : start + sub]


def split_product(pairs, form):
    width = pairs[0][1].shape[1]
    rows = pairs[0][0].shape[1 if form == TN else 0]
    depth = pairs[0][1].shape[0]
    tile = 512
    sub = BLK // 8
    specs, operands = [], []
    for left, right in pairs:
        specs += [whole_spec(left.shape), pl.BlockSpec((depth, tile), lambda j: (0, j))]
        operands += [left, right]
    shape = (4, rows // 8, width)
    return pl.pallas_call(
        functools.partial(split_kernel, len(pairs), form, sub),
        grid=(width // tile,),
        in_specs=specs,
        out_specs=[pl.BlockSpec((4, rows // 8, tile), lambda j: (0, 0, j))] * 2,
        out_shape=[jax.ShapeDtypeStruct(shape, BF)] * 2,
        compiler_params=params(),
        cost_estimate=cost(
            2 * rows * depth * width * len(pairs),
            2 * (rows * width + (rows + width) * depth * len(pairs)),
        ),
    )(*operands)


def mix_kernel(parts, sub, *refs):
    weight, keep, send = refs[parts:]
    at = 0
    for left in refs[:parts]:
        low = mm(left[...], weight[...]).astype(BF)
        for b in range(low.shape[0] // BLK):
            for k in range(8):
                target = send if k % 2 else keep
                start = b * BLK + k * sub
                target[k // 2, at : at + sub, :] = low[start : start + sub]
            at += sub


def mix_product(parts, weight):
    width = weight.shape[1]
    rows = sum(a.shape[0] for a in parts)
    tile = 256
    return pl.pallas_call(
        functools.partial(mix_kernel, len(parts), BLK // 8),
        grid=(width // tile,),
        in_specs=[whole_spec(a.shape) for a in parts]
        + [pl.BlockSpec((weight.shape[0], tile), lambda j: (0, j))],
        out_specs=[pl.BlockSpec((4, rows // 8, tile), lambda j: (0, 0, j))] * 2,
        out_shape=[jax.ShapeDtypeStruct((4, rows // 8, width), BF)] * 2,
        compiler_params=params(),
        cost_estimate=cost(2 * rows * weight.size, 2 * (rows * width + rows * weight.shape[0])),
    )(*parts, weight)


def join_rows(pieces, target):
    if len(pieces) == 1:
        target[...] = pieces[0][...]
        return
    blocks = target.shape[0] // BLK
    sub = BLK // 8
    for b in range(blocks):
        for k in range(8):
            start = b * BLK + k * sub
            source = ((k // 2) * blocks + b) * sub
            target[start : start + sub, :] = pieces[k % 2][source : source + sub, :]


def unit_kernel(count, *refs):
    pieces, (gates, ups, low, gate_out, up_out, hidden) = refs[:count], refs[count:]

    @pl.when(pl.program_id(0) == 0)
    def _():
        join_rows(pieces, low)

    rows = low[...]
    gate = mm(rows, gates[...], NT)
    up = mm(rows, ups[...], NT)
    gate_out[...] = gate.astype(BF)
    up_out[...] = up.astype(BF)
    hidden[...] = (gate * jax.nn.sigmoid(gate) * up).astype(BF)


def unit_products(pieces, gates, ups):
    rows = sum(p.shape[0] for p in pieces)
    units, depth = gates.shape
    tile = min(units, 256)
    weight = pl.BlockSpec((tile, depth), lambda j: (j, 0))
    result = pl.BlockSpec((rows, tile), lambda j: (0, j))
    return pl.pallas_call(
        functools.partial(unit_kernel, len(pieces)),
        grid=(units // tile,),
        in_specs=[whole_spec(p.shape) for p in pieces] + [weight, weight],
        out_specs=[whole_spec((rows, depth)), result, result, result],
        out_shape=[jax.ShapeDtypeStruct((rows, depth), BF)]
        + [jax.ShapeDtypeStruct((rows, units), BF)] * 3,
        compiler_params=params(),
        cost_estimate=cost(4 * rows * depth * units, 4 * depth * (rows + units), rows * units),
    )(*pieces, gates, ups)


def unit_grad_kernel(upstream, downs, gate_in, up_in, d_gate, d_up):
    d_hidden = mm(upstream[...], downs[...], NT)
    gate, up = gate_in[...].astype(F32), up_in[...].astype(F32)
    sigma = jax.nn.sigmoid(gate)
    silu = gate * sigma
    d_gate[...] = (d_hidden * up * (sigma + silu * (1.0 - sigma))).astype(BF)
    d_up[...] = (d_hidden * silu).astype(BF)


def unit_grads(upstream, first, rows, downs, gate, up):
    units, depth = downs.shape
    tile = min(units, 256)
    result = pl.BlockSpec((rows, tile), lambda j: (0, j))
    return pl.pallas_call(
        unit_grad_kernel,
        grid=(units // tile,),
        in_specs=[
            pl.BlockSpec((pl.Element(rows), pl.Element(depth)), lambda j: (first, 0)),
            pl.BlockSpec((tile, depth), lambda j: (j, 0)),
            result,
            result,
        ],
        out_specs=[result, result],
        out_shape=[jax.ShapeDtypeStruct((rows, units), BF)] * 2,
        compiler_params=params(),
        cost_estimate=cost(2 * rows * depth * units, 4 * depth * (rows + units), rows * units),
    )(upstream, downs, gate, up)


def head_kernel(count, *refs):
    pieces, (weight, joined, result) = refs[:count], refs[count:]
    join_rows(pieces, joined)
    result[...] = mm(weight[...], joined[...], NT).astype(BF)


def head_product(pieces, weight):
    depth = weight.shape[1]
    rows = sum(p.shape[0] for p in pieces)
    return pl.pallas_call(
        functools.partial(head_kernel, len(pieces)),
        out_shape=[
            jax.ShapeDtypeStruct((rows, depth), BF),
            jax.ShapeDtypeStruct((weight.shape[0], rows), BF),
        ],
        compiler_params=params(),
        cost_estimate=cost(2 * rows * depth * weight.shape[0], 4 * rows * depth),
    )(*pieces, weight)


def grad_kernel(parts, form, starts, *refs):
    rights = refs[parts:-1]
    total = None
    for p in range(parts):
        left = refs[p][...]
        if starts:
            count = left.shape[0]
            right = rights[0][starts[p] : starts[p] + count, :]
        else:
            right = rights[p][...]
        term = mm(left, right, form)
        total = term if total is None else total + term
    refs[-1][...] = total.astype(BF)


def grad_product(lefts, rights, form=TN, starts=()):
    rows = lefts[0].shape[1 if form == TN else 0]
    width = rights[0].shape[1]
    tile = 512
    tokens = sum(r.shape[0] for r in rights)
    return pl.pallas_call(
        functools.partial(grad_kernel, len(lefts), form, starts),
        grid=(width // tile,),
        in_specs=[whole_spec(a.shape) for a in lefts]
        + [pl.BlockSpec((b.shape[0], tile), lambda j: (0, j)) for b in rights],
        out_specs=pl.BlockSpec((rows, tile), lambda j: (0, j)),
        out_shape=jax.ShapeDtypeStruct((rows, width), BF),
        compiler_params=params(),
        cost_estimate=cost(2 * rows * width * tokens, 2 * tokens * (rows + width)),
    )(*lefts, *rights)


def last_kernel(places, d_qkv, weight, keep, send, whole):
    row, rank = places[1], places[2]
    sub = BLK // 8
    width = keep.shape[2]
    whole[...] = mm(d_qkv[...], weight[...], TN).astype(BF)
    for k in range(8):
        at = pl.ds(pl.multiple_of((rank ^ k) * sub, sub), sub)
        for j in range(4):
            target = send if j % 2 else keep
            source = pl.ds(pl.multiple_of((row ^ j) * width, width), width)
            target[j // 2, at, :] = whole[k * sub : (k + 1) * sub, source]


def last_product(places, d_qkv, weight):
    depth = weight.shape[1]
    per = BLOCKS // 2

    def out_map(i, places):
        return ((i // per) ^ places[0], i % per, 0)

    return pl.pallas_call(
        last_kernel,
        grid_spec=pltpu.PrefetchScalarGridSpec(
            num_scalar_prefetch=1,
            grid=(BLOCKS,),
            in_specs=[
                pl.BlockSpec((d_qkv.shape[0], BLK), lambda i, places: (0, i)),
                pl.BlockSpec(weight.shape, lambda i, places: (0, 0)),
            ],
            out_specs=[pl.BlockSpec((2, BLK, depth // 4), out_map)] * 2,
            scratch_shapes=[pltpu.VMEM((BLK, depth), BF)],
        ),
        out_shape=[jax.ShapeDtypeStruct((4, GTOK // 2, depth // 4), BF)] * 2,
        compiler_params=params(),
        cost_estimate=cost(2 * GTOK * depth * d_qkv.shape[0], 2 * GTOK * depth),
    )(places, d_qkv, weight)


def columns_of(values, count, width):
    return jnp.stack([values[..., k * width : (k + 1) * width] for k in range(count)])


def local(
    quick,
    hidden_in,
    gain_before,
    query_weight,
    key_weight,
    value_weight,
    output_weight,
    gain_middle,
    gate_weight,
    up_weight,
    down_weight,
    cotangent,
    branch_points,
    lengths,
):
    width = hidden_in.shape[1]
    depth = 4 * width
    head_width = query_weight.shape[1]
    heads = head_width // HD
    units = gate_weight.shape[1]
    local_tokens = hidden_in.shape[0]
    team = 4 * lax.axis_size("y")
    sub = BLK // team
    x, c = lax.axis_index("x"), lax.axis_index("c")
    z, y = lax.axis_index("z"), lax.axis_index("y")
    row = 2 * x + c
    rank = 4 * y + row
    order = rank if quick else jnp.int32(0)
    branch_row = pick(branch_points, z)
    length_row = pick(lengths, z)
    info = jnp.concatenate([branch_row, length_row, jnp.stack([order * sub])]).astype(jnp.int32)
    places = jnp.stack([y, row, rank]).astype(jnp.int32)

    def full_gather(share):
        blocks = share.shape[0] // sub
        got = lax.all_gather(share.reshape(blocks, sub, depth), TEAM, axis=1, tiled=False)
        return [got.reshape(-1, depth)]

    def full_scatter(partial):
        parts = partial.reshape(-1, team, sub, depth)
        parts = lax.psum_scatter(parts, TEAM, scatter_dimension=1, tiled=False)
        return parts.reshape(-1, depth).astype(F32)

    lines = Lines()
    tick = lines.tick

    joined = jnp.stack([query_weight.T, key_weight.T, value_weight.T, output_weight])
    if heads % 4 == 0:
        per = heads // 4
        pieces = joined.reshape(4, 4, per * HD, width).transpose(1, 0, 2, 3)
        if quick:
            from_y = flip(hidden_in, "y")
            lines.start("heads", spread_steps(pieces))
            tick(None, "heads")
            from_x = flip(after(hidden_in, lines.wanted["heads"][1][0][0]), "x")
            tick(None, "heads")
            pieces = lines.results["heads"]
        else:
            pieces = spread(pieces)
        pieces = jnp.concatenate([pieces[k] for k in range(4)], -1)
        pieces = pieces.reshape(4, per, HD, depth).transpose(1, 0, 2, 3).reshape(per, 4 * HD, depth)
        attend_weights = lax.all_gather(pieces, "z", axis=0, tiled=True)
    else:
        pieces = lax.all_gather(joined, "z", axis=0, tiled=False)
        pieces = spread(pieces).reshape(4, 4, heads, HD, width).transpose(2, 1, 3, 0, 4)
        attend_weights = pieces.reshape(heads, 4 * HD, depth)
    join_weight = attend_weights[:, :ROWS].reshape(heads * ROWS, depth)
    out_weight = attend_weights[:, ROWS:].reshape(heads * HD, depth)

    def unit_rows(weight):
        pieces = yield from spread_steps(weight.reshape(4, units // 4, width))
        pieces = jnp.concatenate([pieces[k] for k in range(4)], 1)
        if quick:
            lines.extra.append(pieces)
        return [lax.all_gather(pieces, "z", axis=0, tiled=True), pieces]

    gains = row_gather(after(jnp.stack([gain_before, gain_middle]), pieces))
    gains = gains.transpose(1, 0, 2).reshape(2, depth)
    gain_one, gain_two = gains[0], gains[1]

    ids = jnp.arange(GTOK, dtype=jnp.int32)
    slot_ids = (ids % BLK) ^ (order * sub)
    starts = jnp.concatenate([jnp.arange(PBLKS, dtype=jnp.int32) * BLK, branch_row])
    positions = jnp.repeat(starts, BLK) + slot_ids
    frequency = THETA ** (-2.0 * jnp.arange(HD // 2, dtype=F32) / HD)
    angles = positions.astype(F32)[None, :] * frequency[:, None]
    cosine, sine = jnp.cos(angles), jnp.sin(angles)

    steps = range(len(CHUNKS))
    ordered = sorted(steps, key=lambda k: CHUNKS[k][0])
    rows_of = [count * BLK for _, count in CHUNKS]
    shares = [slice(first * sub, (first + count) * sub) for first, count in CHUNKS]
    starts = tuple(first * BLK for first, _ in CHUNKS)
    conts = [k for k in ordered if CHUNKS[k][0] >= PBLKS]
    prompts = [k for k in ordered if CHUNKS[k][0] < PBLKS]
    attentions, middles, scales, norms, d_middles, notes = ({} for _ in range(6))
    attended, d_heads = {}, {}

    def to_middle(k, attention):
        middle = residual[shares[k]].astype(F32) + attention
        scale_two = lax.rsqrt(jnp.mean(middle * middle, -1, keepdims=True) + EPSILON)
        norm_two = middle * scale_two
        attentions[k], middles[k], scales[k], norms[k] = attention, middle, scale_two, norm_two
        return (norm_two * gain_two).astype(BF)

    def to_d_middle(k, d_two):
        notes[k] = jnp.sum(d_two * norms[k], 0)
        scaled_two = d_two * gain_two
        inner_two = jnp.mean(scaled_two * norms[k], -1, keepdims=True)
        d_middle = upstream[shares[k]].astype(F32) + scales[k] * (scaled_two - norms[k] * inner_two)
        d_middles[k] = d_middle
        return d_middle.astype(BF)

    def backward(parts, ties, before=None):
        d_out = jnp.concatenate([d_heads[k] for k in parts], 1)
        heads_out = jnp.concatenate([heads_parts[k] for k in ordered], 1)
        lse = jnp.concatenate([lse_parts[k] for k in ordered], 1)
        source = after(qkv, *ties) if ties else qkv
        operands = (source, keys, values, d_out, heads_out, lse, cosine, sine)
        return attend_backward(info, operands, heads, before)

    def total(grad):
        return lax.psum_scatter(grad, "z", scatter_dimension=0, tiled=True)

    def home_steps(part):
        part = yield from spread_steps(columns_of(part, 4, width))
        return part.reshape(-1, width)

    def outcome(mixed, join_grad):
        layer_out = (jnp.concatenate([middles[k] for k in ordered], 0) + mixed).astype(BF)
        here = jnp.arange(BLOCKS, dtype=jnp.int32)
        bound = jnp.where(here < PBLKS, BLK, jnp.take(length_row, jnp.maximum(here - PBLKS, 0)))
        slots = rank * sub + jnp.arange(sub, dtype=jnp.int32)
        valid = (slots[None, :] < bound[:, None]).astype(F32).reshape(-1)

        def square_sum(part, weights):
            return jnp.sum(weights * jnp.sum(part * part, -1))

        squares = jnp.stack(
            [square_sum(layer_out.astype(F32), valid)]
            + [
                sum(square_sum(parts[k], valid[shares[k]]) for k in steps)
                for parts in (attentions, d_middles)
            ]
        )
        before_local = jnp.sum(join_grad * join_weight.astype(F32), 0) / gain_one
        middle_local = sum(notes[k] for k in steps)
        return layer_out, jnp.concatenate([before_local, middle_local, squares])

    heads_parts, lse_parts, lows, gates, ups, hiddens = ([] for _ in range(6))
    gate_parts, up_parts = [], []
    if quick:
        former, latter = flip(halves(from_y)[0], "x"), flip(halves(from_x)[1], "y")
        corner = jnp.concatenate([former, latter], 0)
        four = [hidden_in, from_x, from_y, corner]
        hidden_pieces = [p for piece in four for p in (piece, flip(piece, "c"))]
        lines.start("gate", unit_rows(after(gate_weight, corner).T))
        lines.start("up", unit_rows(up_weight.T))
        lines.start("down", unit_rows(down_weight))
        lines.start("late", place_steps(after(cotangent, corner)))
        lines.launch("late")
        low_one, residual, qkv, keys, values = tick(
            lambda ties: assemble(
                places,
                after(hidden_pieces, *ties),
                gain_one,
                sub,
                (join_weight, cosine, sine),
                heads,
            ),
            "gate",
        )

        def forward_line(k, partial):
            low = to_middle(k, (yield from sum_steps(*partial)))
            return (yield from gather_steps(low))

        def attend(k, *names):
            def large(ties):
                return attend_forward(info, after(qkv, *ties), keys, heads, *CHUNKS[k])

            head_part, lse = tick(large, *names)
            heads_parts.append(head_part)
            lse_parts.append(lse)
            partial = split_product([(head_part, out_weight)], TN)
            lines.last = [partial[0]]
            lines.start(k, forward_line(k, partial))

        attend(0, "gate", "up")
        lines.land("late")
        attend(1, 0, "late")
        attend(2, 0, 1, "up", "late")
        attend(3, 0, 1, 2)
        gate_rows, up_rows = lines.results["gate"][0], lines.results["up"][0]
        upstream_rows, upstream = tick(
            lambda ties: assemble(places, after(lines.results["late"], *ties), None, sub), 0, 1, 3
        )

        def unit(k, *names):
            def large(ties):
                return unit_products(after(lines.results[k], *ties), gate_rows, up_rows)

            low, gate, up, hidden = tick(large, *names)
            lows.append(low)
            gates.append(gate)
            ups.append(up)
            hiddens.append(hidden)

        tick(None, 0, 2, "down")
        tick(None, 0, 1, 2, "down")
        down_rows = lines.results["down"][0]
        unit(0, 1, 3)
        tick(None, 1, 2)
        unit(1, 2, 3)
        tick(None, 2, 3)
        unit(2, 3)
        tick(None, 3)
        unit(3)
        down_grad = tick(lambda ties: grad_product(hiddens, [after(upstream_rows, *ties)], TN, starts))
        down_sum = total(down_grad)

        def backward_line(k, partial):
            low = to_d_middle(k, (yield from sum_steps(*partial)))
            pieces = yield from gather_steps(low)
            attended[k], d_heads[k] = head_product(pieces, out_weight)
            return d_heads[k]

        def unit_grad(k, first, second):
            def large(ties):
                source = after(gates[k], *ties)
                return unit_grads(upstream_rows, starts[k], rows_of[k], down_rows, source, ups[k])

            d_gate, d_up = tick(large, *first)
            gate_parts.append(d_gate)
            up_parts.append(d_up)

            def more(ties):
                return split_product([(after(d_gate, *ties), gate_rows), (d_up, up_rows)], NN)

            lines.start(k, backward_line(k, tick(more, *second)))

        unit_grad(0, (), ())
        unit_grad(1, (0,), (0,))
        unit_grad(2, (0, 1), (0, 1))
        unit_grad(3, (0, 1, 2), (0, 1, 2))
        def summed(values, axes):
            for axis in axes:
                (got,) = yield [(values, axis)]
                values = values + got
            return values

        gate_grad = tick(lambda ties: grad_product(after(gate_parts, *ties), lows), 1, 2, 3)
        gate_sum = total(gate_grad)
        mixed = tick(
            lambda ties: mix_product(after([hiddens[k] for k in ordered], *ties), down_rows),
            1,
            2,
            3,
        )
        lines.start("mixed", sum_steps(*mixed))
        before = tick(lambda ties: backward(conts, ties), 2, 3, "mixed")
        lines.start("down", home_steps(down_sum))
        up_grad = tick(lambda ties: grad_product(after(up_parts, *ties), lows), 2, 3, "down")
        up_sum = total(up_grad)
        tick(None, 3)
        tick(None, 3)
        lines.start("gate", home_steps(gate_sum))
        d_qkv, inner = tick(lambda ties: backward(prompts, ties, before), "mixed", "down", "gate")
        inner = straighten(inner[0].reshape(BLOCKS, team, sub), rank).reshape(GTOK)
        lines.start("inner", summed(inner, ("x", "c", "y")))
        lines.start("up", home_steps(up_sum))
        own, other = tick(
            lambda ties: last_product(places, after(d_qkv, *ties), join_weight),
            "mixed",
            "gate",
            "inner",
        )
        lines.start("last", sum_steps(own, other))
        join_grad = tick(lambda ties: mm(d_qkv, after(low_one, *ties)), "last", "up", "inner")
        join_sum = total(join_grad.astype(BF))
        mixed = lines.results["mixed"]
        layer_out, sums = outcome(mixed, join_grad)
        lines.start("sums", summed(sums, ("x", "y", "c", "z1", "z2")))
        tick(None, "sums")
        tick(None, "sums")
        out_grad = tick(
            lambda ties: grad_product(
                after([heads_parts[k] for k in ordered], *ties), [attended[k] for k in ordered], NN
            ),
            "last",
            "inner",
            "up",
        )
        tick(None, "last", "sums")
        tick(None, "sums")
        tick(None, "sums")
        d_one, inner, sums = (lines.results[n] for n in ("last", "inner", "sums"))
        gate_grad, up_grad, down_grad = (lines.results[n] for n in ("gate", "up", "down"))
    else:

        def full(values):
            values = lax.all_gather(values, "y", axis=0, tiled=True)
            return lax.all_gather(values, ROW, axis=1, tiled=True)

        def share_of(values):
            return pick(values.reshape(BLOCKS, team, sub, depth), rank, 1).reshape(-1, depth)

        gate_rows = complete(unit_rows(gate_weight.T))[0]
        up_rows = complete(unit_rows(up_weight.T))[0]
        down_rows = complete(unit_rows(down_weight))[0]
        hidden_rows = full(hidden_in)
        upstream_rows = full(cotangent)
        residual, upstream = share_of(hidden_rows), share_of(upstream_rows)
        wide = hidden_rows.astype(F32)
        scale = lax.rsqrt(jnp.mean(wide * wide, -1, keepdims=True) + EPSILON)
        low_one = (wide * scale * gain_one).astype(BF)
        qkv, keys, values = project(join_weight, low_one, cosine, sine, heads)
        for k in steps:
            head_part, lse = attend_forward(info, qkv, keys, heads, *CHUNKS[k])
            heads_parts.append(head_part)
            lse_parts.append(lse)
            low = to_middle(k, full_scatter(mm(head_part, out_weight, TN).astype(BF)))
            low, gate, up, hidden = unit_products(full_gather(low), gate_rows, up_rows)
            lows.append(low)
            hiddens.append(hidden)
            d_gate, d_up = unit_grads(upstream_rows, starts[k], rows_of[k], down_rows, gate, up)
            gate_parts.append(d_gate)
            up_parts.append(d_up)
            partial = (mm(d_gate, gate_rows) + mm(d_up, up_rows)).astype(BF)
            low = to_d_middle(k, full_scatter(partial))
            attended[k], d_heads[k] = head_product(full_gather(low), out_weight)
        gate_sum, up_sum = total(grad_product(gate_parts, lows)), total(grad_product(up_parts, lows))
        down_sum = total(grad_product(hiddens, [upstream_rows], TN, starts))
        mixed = full_scatter(
            jnp.concatenate([mm(hiddens[k], down_rows).astype(BF) for k in ordered], 0)
        )
        d_qkv, inner = backward(prompts, [], backward(conts, []))
        partial = mm(d_qkv, join_weight, TN).astype(BF)
        join_grad = mm(d_qkv, low_one)
        out_grad = grad_product([heads_parts[k] for k in ordered], [attended[k] for k in ordered], NN)
        layer_out, sums = outcome(mixed, join_grad)
        sums = lax.psum(sums, EVERY)
        gate_grad, up_grad, down_grad = (
            complete(home_steps(part)) for part in (gate_sum, up_sum, down_sum)
        )

    attended = [attended[k] for k in ordered]
    gate_grad, up_grad = gate_grad.T.astype(F32), up_grad.T.astype(F32)
    down_grad = down_grad.astype(F32)
    if heads % 4 == 0:
        part = join_sum if quick else total(join_grad.astype(BF))
        part = part.reshape(heads // 4, 3, HD, depth)
        out_part = total(out_grad).reshape(heads // 4, 1, HD, depth)
        part = jnp.concatenate([part, out_part], 1).transpose(1, 0, 2, 3)
        part = spread(columns_of(part.reshape(4, heads // 4 * HD, depth), 4, width))
        part = part.transpose(1, 0, 2, 3).reshape(4, head_width, width)
    else:
        part = jnp.concatenate(
            [join_grad.astype(BF).reshape(heads, 3, HD, depth), out_grad.reshape(heads, 1, HD, depth)], 1
        ).transpose(1, 0, 2, 3)
        part = spread(columns_of(part.reshape(4, heads * HD, depth), 4, width))
        part = lax.psum_scatter(part, "z", scatter_dimension=0, tiled=False)
    query_grad, key_grad, value_grad = (part[k].T.astype(F32) for k in range(3))
    output_grad = part[3].astype(F32)

    if quick:
        half = local_tokens
        inner = pick(inner.reshape(2, half), y)
        d_middle = jnp.concatenate(
            [lax.dynamic_slice_in_dim(a, row * width, width, 1) for a in attended], 0
        )
        d_middle = pick(d_middle.reshape(2, BLOCKS // 2, team, sub, width), y)
        d_middle = straighten(d_middle, rank).reshape(half, width).astype(F32)
        rows = half // team
        layer_out = jnp.stack(
            [
                layer_out[h * rows : (h + 1) * rows, k * width : (k + 1) * width]
                for h in range(2)
                for k in range(4)
            ]
        )
        layer_out = lax.all_to_all(layer_out, TEAM, 0, 0, tiled=True)
        layer_out = layer_out.reshape(team, BLOCKS // 2, sub, width).transpose(1, 0, 2, 3)
        layer_out = layer_out.reshape(half, width)
    else:
        d_one = lax.psum_scatter(partial, "y", scatter_dimension=0, tiled=True)
        d_one = lax.psum_scatter(d_one, ROW, scatter_dimension=1, tiled=True).astype(F32)
        inner = lax.psum(inner[0], TEAM)
        inner = lax.dynamic_slice(inner, (y * local_tokens,), (local_tokens,))
        corner = (y * local_tokens, row * width)
        d_middle = lax.dynamic_slice(
            jnp.concatenate(attended, 0), corner, (local_tokens, width)
        ).astype(F32)
        layer_out = lax.all_gather(
            layer_out.reshape(BLOCKS, sub, depth), TEAM, axis=1, tiled=False
        ).reshape(GTOK, depth)
        layer_out = lax.dynamic_slice(layer_out, corner, (local_tokens, width))
    wide = hidden_in.astype(F32)
    scale_one = lax.rsqrt(row_sum(jnp.sum(wide * wide, -1)) / depth + EPSILON)[:, None]
    norm_one = wide * scale_one
    input_grad = d_middle + scale_one * (d_one * gain_before - norm_one * (inner / depth)[:, None])

    before_grad = lax.dynamic_slice(sums, (row * width,), (width,))
    middle_grad = lax.dynamic_slice(sums, (depth + row * width,), (width,))
    valid_count = (lengths.shape[0] * PROMPT + jnp.sum(lengths)).astype(F32)
    rms_values = jnp.sqrt(sums[2 * depth :] / (valid_count * depth))
    return (
        layer_out,
        input_grad,
        before_grad,
        query_grad,
        key_grad,
        value_grad,
        output_grad,
        middle_grad,
        gate_grad,
        up_grad,
        down_grad,
        rms_values,
    )


def solution(mesh):
    split = mesh.shape["col"] // GROUPS
    grid = Mesh(mesh.devices.reshape(2, 2, GROUPS, split), ("x", "c", "z", "y"))
    row, col = ("x", "c"), ("z", "y")
    return jax.shard_map(
        functools.partial(local, split == 2),
        mesh=grid,
        in_specs=(
            P(col, row),
            P(row),
            P(row, col),
            P(row, col),
            P(row, col),
            P(col, row),
            P(row),
            P(row, col),
            P(row, col),
            P(col, row),
            P(col, row),
            P(),
            P(),
        ),
        out_specs=(
            P(col, row),
            P(col, row),
            P(row),
            P(row, col),
            P(row, col),
            P(row, col),
            P(col, row),
            P(row),
            P(row, col),
            P(row, col),
            P(col, row),
            P(),
        ),
        check_vma=False,
    )
```

time: 1690 us -> 1190 us (0.70)
  matrix products: 324 us -> 17.7 us
  Pallas kernels: 268 us -> 490 us
  local copies, waits for them, and re-layouts: 305 us -> 141 us
  waiting for transfers between devices: 406 us -> 273 us
  other arithmetic: 180 us -> 127 us
  blocking collectives: 44 us -> 0 us
  starting transfers between devices: 137 us -> 108 us
    dot_general x34 -> x1, matrix products: 324 us -> 17.7 us  [mm(): return lax.dot_general(a, b, dims, preferred_element_type=F32)]
    pallas_call x3 -> x30, Pallas kernels: 154 us -> 429 us  [the longest x2 89.3 us: attend_backward(): pl.pallas_call(functools.partial(backward_kernel, heads, 0 if final else...]
    ppermute x168 -> x132, waiting for transfers between devices: 406 us -> 259 us  [flip(): return lax.ppermute(values, axis, [(0, 1), (1, 0)])]
    pallas_call x4, Pallas kernels: 114 us -> 60.8 us  [attend_forward(): pl.pallas_call(functools.partial(forward_kernel, heads, first), grid=(cou...]
    psum x1 -> x0, blocking collectives: 44 us -> none  [local(): lax.psum(jnp.concatenate([before_local, middle_local, squares]), EVERY)]
    reshape x12 -> x2, local copies, waits for them, and re-layouts: 43 us -> 0.09 us  [the longest x1 0.08 us: local(): inner = straighten(inner[0].reshape(BLOCKS, team, sub), rank).reshape(GTOK)]
    dynamic_slice x1 -> x4, local copies, waits for them, and re-layouts: 38.1 us -> 6.98 us  [local(): lax.dynamic_slice_in_dim(a, row * width, width, 1)]
    ppermute x168 -> x132, starting transfers between devices: 132 us -> 101 us  [flip(): return lax.ppermute(values, axis, [(0, 1), (1, 0)])]
  transfers between devices with their start and end apart: 177 -> 144, of which waited for: 70 -> 31; matrix products, arithmetic and copies ran while one was open for 46% -> 22% of each run, Pallas kernels for 16% -> 40%
where the time goes in v2:
time: 1190 us; the launch traced here: 1180 us
  Pallas kernels  490 us (41%)
  waiting for transfers between devices  273 us (23%)
  local copies, waits for them, and re-layouts  141 us (12%)
  other arithmetic  127 us (11%)
  starting transfers between devices  108 us (9%)
  between operations  22.5 us (2%)
  matrix products  17.7 us (1%)
    ppermute x132, waiting for transfers between devices, flip(): return lax.ppermute(values, axis, [(0, 1), (1, 0)])  259 us
    ppermute x132, starting transfers between devices, flip(): return lax.ppermute(values, axis, [(0, 1), (1, 0)])  101 us
    pallas_call x2, Pallas kernels, attend_backward(): pl.pallas_call(functools.partial(backward_kernel, heads, 0 if final else...  89.3 us
    pallas_call x4, Pallas kernels, grad_product(): pl.pallas_call(functools.partial(grad_kernel, len(lefts), form, starts),...  74.4 us
    pallas_call x8, Pallas kernels, split_product(): pl.pallas_call(functools.partial(split_kernel, len(pairs), form, sub), gr...  67.6 us
    unnamed x254, local copies, waits for them, and re-layouts  62.2 us
    pallas_call x4, Pallas kernels, attend_forward(): pl.pallas_call(functools.partial(forward_kernel, heads, first), grid=(cou...  60.8 us
    pallas_call x4, Pallas kernels, unit_products(): pl.pallas_call(functools.partial(unit_kernel, len(pieces)), grid=(units /...  51.1 us
  transfers between devices with their start and end apart: 144, of which 31 were waited for; matrix products, arithmetic and copies ran while one was open for 22% of the time, Pallas kernels for 40%

profile of v2, /device:TPU:0, one launch (start us, length us, event | category | flops | bytes accessed | tf_op | source)
XLA Modules:
  0.0 1178.5 jit_solution(6323324541938670393)
XLA Ops:
  14.7 11.9 %collective-permute-done.1 = bf16[2,4,64,512]{3,2,0,1:T(8,128)(2,1)S(1)} collective-permute-done((bf16[2,4,64,512]{3,2,0,1:T(8,128)(2,1)S(1)}, bf16[2,4,64,512]{3,2,0,1:T(8,128)(2,1)S(1)}, u32[]{:S(2)}, u32[]{:S(2)}) %collective-permute-start.1) | collective-permute-done | bytes 524320 | tf_op jit(solution)/shard_map/ppermute | solution.py:360
  35.6 37.5 %collective-permute-done.4.refs_4_ = bf16[1792,512]{1,0:T(8,128)(2,1)} collective-permute-done((bf16[1792,512]{1,0:T(8,128)(2,1)S(1)}, bf16[1792,512]{1,0:T(8,128)(2,1)}, u32[]{:S(2)}, u32[]{:S(2)}) %collective-permute-start.4) | collective-permute-done | bytes 1835040 | tf_op jit(solution)/shard_map/ppermute | solution.py:360
  126.1 26.9 %shard_map.220 = (bf16[3584,2048]{1,0:T(8,128)(2,1)}, bf16[448,2048]{1,0:T(8,128)(2,1)}, bf16[768,3584]{1,0:T(8,128)(2,1)}, bf16[4,3584,64]{2,1,0:T(8,128)(2,1)}, bf16[4,3584,64]{2,1,0:T(8,128)(2,1)}) custom-call(s32[3]{0:T(128)} %pad_add_fusion.places, bf16[1792,512]{1,0:T(8,128)(2,1)} %refs_0_, bf16[1792,512]{1,0:T(8,128)(2,1)} %collective-permute-done.refs_1_, ...), custom_call_target="tpu_custom_call" | custom-call | flops 11318329344 | bytes 36700160 | tf_op jit(solution)/shard_map/pallas_call | solution.py:572
  153.0 19.0 %collective-permute-done.12 = bf16[2,256,512]{2,1,0:T(8,128)(2,1)S(1)} collective-permute-done((bf16[2,256,512]{2,1,0:T(8,128)(2,1)}, bf16[2,256,512]{2,1,0:T(8,128)(2,1)S(1)}, u32[]{:S(2)}, u32[]{:S(2)}) %collective-permute-start.12) | collective-permute-done | bytes 524320 | tf_op jit(solution)/shard_map/ppermute | solution.py:360
  172.4 15.5 %shard_map.221 = (bf16[256,768]{1,0:T(8,128)(2,1)}, f32[8,768]{1,0:T(8,128)}) custom-call(s32[13]{0:T(128)} %pad_add_fusion.2.info, bf16[768,3584]{1,0:T(8,128)(2,1)} %get-tuple-element.621.qkv, bf16[4,3584,64]{2,1,0:T(8,128)(2,1)} %get-tuple-element.361.knat), custom_call_target="tpu_custom_call" | custom-call | flops 12079595520 | bytes 16777216 | tf_op jit(solution)/shard_map/pallas_call | solution.py:117
  205.5 16.5 %shard_map.223 = (bf16[256,768]{1,0:T(8,128)(2,1)}, f32[8,768]{1,0:T(8,128)}) custom-call(s32[13]{0:T(128)} %pad_add_fusion.2.info, bf16[768,3584]{1,0:T(8,128)(2,1)} %get-tuple-element.621.qkv, bf16[4,3584,64]{2,1,0:T(8,128)(2,1)} %get-tuple-element.361.knat), custom_call_target="tpu_custom_call" | custom-call | flops 12079595520 | bytes 16777216 | tf_op jit(solution)/shard_map/pallas_call | solution.py:117
  276.0 17.6 %shard_map.227 = (bf16[256,1024]{1,0:T(8,128)(2,1)}, f32[8,1024]{1,0:T(8,128)}) custom-call(s32[13]{0:T(128)} %pad_add_fusion.2.info, bf16[768,3584]{1,0:T(8,128)(2,1)} %get-tuple-element.621.qkv, bf16[4,3584,64]{2,1,0:T(8,128)(2,1)} %get-tuple-element.361.knat), custom_call_target="tpu_custom_call" | custom-call | flops 16106127360 | bytes 16777216 | tf_op jit(solution)/shard_map/pallas_call | solution.py:117
  306.4 17.2 %shard_map.229 = (bf16[3584,2048]{1,0:T(8,128)(2,1)}, bf16[448,2048]{1,0:T(8,128)(2,1)}) custom-call(s32[3]{0:T(128)} %pad_add_fusion.places, bf16[1792,512]{1,0:T(8,128)(2,1)} %refs_0_.1, bf16[1792,512]{1,0:T(8,128)(2,1)} %collective-permute-done.16.refs_1_, bf16[1792,512]{1,0:T(8,128)(2,1)} %collective-permute-done.14.refs_2_, ...), custom_call_target="tpu_custom_call" | custom-call | flops 44040192 | bytes 36700160 | tf_op jit(solution)/shard_map/pallas_call | solution.py:572
  443.9 13.5 %collective-permute-done.62 = bf16[128,2048]{1,0:T(8,128)(2,1)S(1)} collective-permute-done((bf16[128,2048]{1,0:T(8,128)(2,1)}, bf16[128,2048]{1,0:T(8,128)(2,1)S(1)}, u32[]{:S(2)}, u32[]{:S(2)}) %collective-permute-start.62) | collective-permute-done | bytes 524320 | tf_op jit(solution)/shard_map/ppermute | solution.py:360
  463.6 14.1 %shard_map.232 = (bf16[1024,2048]{1,0:T(8,128)(2,1)}, bf16[1024,1024]{1,0:T(8,128)(2,1)}, bf16[1024,1024]{1,0:T(8,128)(2,1)}, bf16[1024,1024]{1,0:T(8,128)(2,1)}) custom-call(bf16[512,2048]{1,0:T(8,128)(2,1)} %constant_dynamic-update-slice_fusion.14.refs_0_, bf16[512,2048]{1,0:T(8,128)(2,1)} %collective-permute-done.60.refs_1_, ...), custom_call_target="tpu_custom_call" | custom-call | flops 8589934592 | bytes 16777216 | tf_op jit(solution)/shard_map/pallas_call | solution.py:707
  482.2 13.9 %shard_map.233 = (bf16[1024,2048]{1,0:T(8,128)(2,1)}, bf16[1024,1024]{1,0:T(8,128)(2,1)}, bf16[1024,1024]{1,0:T(8,128)(2,1)}, bf16[1024,1024]{1,0:T(8,128)(2,1)}) custom-call(bf16[512,2048]{1,0:T(8,128)(2,1)} %copy-done.72, bf16[512,2048]{1,0:T(8,128)(2,1)} %collective-permute-done.65.refs_1_, ...), custom_call_target="tpu_custom_call" | custom-call | flops 8589934592 | bytes 16777216 | tf_op jit(solution)/shard_map/pallas_call | solution.py:707
  496.1 21.3 %shard_map.234 = bf16[1024,2048]{1,0:T(8,128)(2,1)} custom-call(bf16[768,1024]{1,0:T(8,128)(2,1)} %get-tuple-element.574.refs_0_.refs_2_, bf16[768,1024]{1,0:T(8,128)(2,1)} %get-tuple-element.575.refs_1_.refs_3_, bf16[1024,1024]{1,0:T(8,128)(2,1)} %get-tuple-element.572.refs_2_.refs_0_, bf16[1024,1024]{1,0:T(8,128)(2,1)} %get-tuple-element.573.refs_3_.refs_1_, ...), custom_call_target="tpu_custom_call" | custom-call | flops 15032385536 | bytes 22020096 | tf_op jit(solution)/shard_map/pallas_call | solution.py:788
  599.0 13.3 %shard_map.240 = (bf16[4,128,2048]{2,1,0:T(8,128)(2,1)}, bf16[4,128,2048]{2,1,0:T(8,128)(2,1)}) custom-call(bf16[1024,1024]{1,0:T(8,128)(2,1)} %get-tuple-element.561.refs_0_.refs_2_, bf16[1024,2048]{1,0:T(8,128)(2,1)} %all-gather.7.cloned.1.call-done.refs_2_.refs_1_, bf16[1024,1024]{1,0:T(8,128)(2,1)} %get-tuple-element.606.refs_2_, ...), custom_call_target="tpu_custom_call" | custom-call | flops 8589934592 | bytes 16777216 | tf_op jit(solution)/shard_map/pallas_call | solution.py:630
  641.0 13.4 %shard_map.242 = (bf16[4,128,2048]{2,1,0:T(8,128)(2,1)}, bf16[4,128,2048]{2,1,0:T(8,128)(2,1)}) custom-call(bf16[1024,1024]{1,0:T(8,128)(2,1)} %get-tuple-element.562.refs_0_.refs_3_, bf16[1024,2048]{1,0:T(8,128)(2,1)} %all-gather.7.cloned.1.call-done.refs_2_.refs_1_, bf16[1024,1024]{1,0:T(8,128)(2,1)} %get-tuple-element.607.refs_2_.refs_3_, ...), custom_call_target="tpu_custom_call" | custom-call | flops 8589934592 | bytes 16777216 | tf_op jit(solution)/shard_map/pallas_call | solution.py:630
  666.4 21.6 %shard_map.244 = bf16[1024,2048]{1,0:T(8,128)(2,1)} custom-call(bf16[768,1024]{1,0:T(8,128)(2,1)} %get-tuple-element.559.refs_0_, bf16[768,1024]{1,0:T(8,128)(2,1)} %get-tuple-element.560.refs_0_.refs_1_, bf16[1024,1024]{1,0:T(8,128)(2,1)} %get-tuple-element.561.refs_0_.refs_2_, bf16[1024,1024]{1,0:T(8,128)(2,1)} %get-tuple-element.562.refs_0_.refs_3_, ...), custom_call_target="tpu_custom_call" | custom-call | flops 15032385536 | bytes 22020096 | tf_op jit(solution)/shard_map/pallas_call | solution.py:788
  703.2 21.6 %shard_map.245 = (bf16[4,448,2048]{2,1,0:T(8,128)(2,1)}, bf16[4,448,2048]{2,1,0:T(8,128)(2,1)}) custom-call(bf16[1024,1024]{1,0:T(8,128)(2,1)} %get-tuple-element.572.refs_2_.refs_0_, bf16[1024,1024]{1,0:T(8,128)(2,1)} %get-tuple-element.573.refs_3_.refs_1_, bf16[768,1024]{1,0:T(8,128)(2,1)} %get-tuple-element.574.refs_0_.refs_2_, ...), custom_call_target="tpu_custom_call" | custom-call | flops 15032385536 | bytes 22020096 | tf_op jit(solution)/shard_map/pallas_call | solution.py:661
  741.0 46.8 %shard_map.247 = (f32[256,3584]{1,0:T(8,128)}, f32[256,3584]{1,0:T(8,128)}, bf16[256,1536]{1,0:T(8,128)(2,1)}, f32[8,1536]{1,0:T(8,128)}) custom-call(s32[13]{0:T(128)} %pad_add_fusion.2.info, bf16[768,3584]{1,0:T(8,128)(2,1)} %get-tuple-element.621.qkv, bf16[4,3584,64]{2,1,0:T(8,128)(2,1)} %get-tuple-element.361.knat, ...), custom_call_target="tpu_custom_call" | custom-call | flops 45097156608 | bytes 33554432 | tf_op jit(solution)/shard_map/pallas_call | solution.py:288
  799.4 22.0 %shard_map.248 = bf16[1024,2048]{1,0:T(8,128)(2,1)} custom-call(bf16[768,1024]{1,0:T(8,128)(2,1)} %get-tuple-element.604.refs_2_.refs_0_, bf16[768,1024]{1,0:T(8,128)(2,1)} %get-tuple-element.605.refs_2_.refs_1_, bf16[1024,1024]{1,0:T(8,128)(2,1)} %get-tuple-element.606.refs_2_, bf16[1024,1024]{1,0:T(8,128)(2,1)} %get-tuple-element.607.refs_2_.refs_3_, ...), custom_call_target="tpu_custom_call" | custom-call | flops 15032385536 | bytes 22020096 | tf_op jit(solution)/shard_map/pallas_call | solution.py:788
  893.2 42.5 %shard_map.251 = (bf16[768,3584]{1,0:T(8,128)(2,1)}, f32[8,3584]{1,0:T(8,128)}) custom-call(s32[13]{0:T(128)} %pad_add_fusion.2.info, bf16[768,3584]{1,0:T(8,128)(2,1)} %get-tuple-element.621.qkv, bf16[4,3584,64]{2,1,0:T(8,128)(2,1)} %get-tuple-element.361.knat, bf16[4,3584,64]{2,1,0:T(8,128)(2,1)} %get-tuple-element.590.vnat, ...), custom_call_target="tpu_custom_call" | custom-call | flops 45097156608 | bytes 33554432 | tf_op jit(solution)/shard_map/pallas_call | solution.py:288
  944.2 20.9 %shard_map.252 = (bf16[4,1792,512]{2,1,0:T(8,128)(2,1)}, bf16[4,1792,512]{2,1,0:T(8,128)(2,1)}) custom-call(s32[3]{0:T(128)} %pad_add_fusion.places, bf16[768,3584]{1,0:T(8,128)(2,1)} %get-tuple-element.635.d_qkv, bf16[768,2048]{1,0:T(8,128)(2,1)} %bitcast.420), custom_call_target="tpu_custom_call" | custom-call | flops 11274289152 | bytes 14680064 | tf_op jit(solution)/shard_map/pallas_call | solution.py:820
  971.2 17.7 %fusion.107 = (bf16[768,2048]{1,0:T(8,128)(2,1)}, f32[2048]{0:T(1024)S(1)}) fusion(bf16[4,192,2048]{2,1,0:T(8,128)(2,1)S(1)} %copy-done.34, bf16[768,3584]{1,0:T(8,128)(2,1)} %get-tuple-element.635.d_qkv, bf16[3584,2048]{1,0:T(8,128)(2,1)} %get-tuple-element.649), kind=kOutput, calls=%fused_computation.499 | convolution fusion | flops 11280578560 | bytes 26484736 | tf_op jit(solution)/shard_map/dot_general | solution.py:32
  996.6 29.2 %collective-permute-done.122 = bf16[2,256,512]{2,1,0:T(8,128)(2,1)S(1)} collective-permute-done((bf16[2,256,512]{2,1,0:T(8,128)(2,1)S(1)}, bf16[2,256,512]{2,1,0:T(8,128)(2,1)S(1)}, u32[]{:S(2)}, u32[]{:S(2)}) %collective-permute-start.122) | collective-permute-done | bytes 524320 | tf_op jit(solution)/shard_map/ppermute | solution.py:360
  1073.9 35.5 %collective-permute-done.126 = f32[4099]{0:T(1024)S(1)} collective-permute-done((f32[4099]{0:T(1024)S(1)}, f32[4099]{0:T(1024)S(1)}, u32[]{:S(2)}, u32[]{:S(2)}) %collective-permute-start.126) | collective-permute-done | bytes 16428 | tf_op jit(solution)/shard_map/ppermute | solution.py:360
  1138.0 21.0 %collective-permute-done.131 = bf16[2,4,64,512]{3,2,0,1:T(8,128)(2,1)} collective-permute-done((bf16[2,4,64,512]{3,2,0,1:T(8,128)(2,1)}, bf16[2,4,64,512]{3,2,0,1:T(8,128)(2,1)}, u32[]{:S(2)}, u32[]{:S(2)}) %collective-permute-start.131) | collective-permute-done | bytes 524320 | tf_op jit(solution)/shard_map/ppermute | solution.py:360
  (849 shorter events, 625.5 us)
Async XLA Ops:
  7.2 114.9 %all-gather.5.cloned.1.call-start = ((), (), s32[]{:S(2)}) async-start(), calls=%async_computation.6 | async-start | bytes 5242880 | tf_op jit(solution)/shard_map/all_gather | solution.py:904
  30.1 360.7 %all-gather.7.cloned.1.call-start = ((), (), s32[]{:S(2)}) async-start(), calls=%async_computation.7 | async-start | bytes 5242880 | tf_op jit(solution)/shard_map/all_gather | solution.py:917
  34.2 84.8 %collective-permute-start = (bf16[1792,512]{1,0:T(8,128)(2,1)S(1)}, bf16[1792,512]{1,0:T(8,128)(2,1)}, u32[]{:S(2)}, u32[]{:S(2)}) collective-permute-start(bf16[1792,512]{1,0:T(8,128)(2,1)S(1)} %copy-done.21), channel_id=1, source_target_pairs={{0,8},{8,0},{1,9},{9,1},{2,10},{10,2},{3,11},{11,3},{4,12},{12,4},... | collective-permute-start | bytes 5505032 | tf_op jit(solution)/shard_map/ppermute | solution.py:360
  118.4 80.5 %collective-permute-start.14 = (bf16[1792,512]{1,0:T(8,128)(2,1)}, bf16[1792,512]{1,0:T(8,128)(2,1)}, u32[]{:S(2)}, u32[]{:S(2)}) collective-permute-start(bf16[1792,512]{1,0:T(8,128)(2,1)} %refs_0_.1), channel_id=1, source_target_pairs={{0,16},{16,0},{1,17},{17,1},{2,18},{18,2},{3,19},{19,3},{4,20},{20... | collective-permute-start | bytes 5505032 | tf_op jit(solution)/shard_map/ppermute | solution.py:360
  118.9 80.0 %collective-permute-start.15 = (bf16[1792,512]{1,0:T(8,128)(2,1)}, bf16[1792,512]{1,0:T(8,128)(2,1)S(1)}, u32[]{:S(2)}, u32[]{:S(2)}) collective-permute-start(bf16[1792,512]{1,0:T(8,128)(2,1)} %refs_0_.1), channel_id=1, source_target_pairs={{0,1},{1,0},{2,3},{3,2},{4,5},{5,4},{6,7},{7,6},{8,9},{9,8},{10,11... | collective-permute-start | bytes 5505032 | tf_op jit(solution)/shard_map/ppermute | solution.py:360
  120.6 78.4 %collective-permute-start.16 = (bf16[1792,512]{1,0:T(8,128)(2,1)}, bf16[1792,512]{1,0:T(8,128)(2,1)}, u32[]{:S(2)}, u32[]{:S(2)}) collective-permute-start(bf16[1792,512]{1,0:T(8,128)(2,1)} %refs_0_.1), channel_id=1, source_target_pairs={{0,8},{8,0},{1,9},{9,1},{2,10},{10,2},{3,11},{11,3},{4,12},{12,4},... | collective-permute-start | bytes 5505032 | tf_op jit(solution)/shard_map/ppermute | solution.py:360
  189.2 201.7 %all-gather.9.cloned.1.call-start = ((), (), s32[]{:S(2)}) async-start(), calls=%async_computation.8 | async-start | bytes 5242880 | tf_op jit(solution)/shard_map/all_gather | solution.py:917
  265.7 61.1 %collective-permute-start.23 = (bf16[4,128,2048]{2,1,0:T(8,128)(2,1)}, bf16[4,128,2048]{2,1,0:T(8,128)(2,1)}, u32[]{:S(2)}, u32[]{:S(2)}) collective-permute-start(bf16[4,128,2048]{2,1,0:T(8,128)(2,1)} %get-tuple-element.390), channel_id=1, source_target_pairs={{0,8},{8,0},{1,9},{9,1},{2,10},{10,2},{3,11},{11,3},{4,12},{12,4},... | collective-permute-start | bytes 6291464 | tf_op jit(solution)/shard_map/ppermute | solution.py:360
  267.1 262.0 %all-gather.11.cloned.1.call-start = ((), (), s32[]{:S(2)}) async-start(), calls=%async_computation.9 | async-start | bytes 5242880 | tf_op jit(solution)/shard_map/all_gather | solution.py:917
  304.8 78.6 %collective-permute-start.37 = (bf16[4,128,2048]{2,1,0:T(8,128)(2,1)}, bf16[4,128,2048]{2,1,0:T(8,128)(2,1)}, u32[]{:S(2)}, u32[]{:S(2)}) collective-permute-start(bf16[4,128,2048]{2,1,0:T(8,128)(2,1)} %get-tuple-element.415), channel_id=1, source_target_pairs={{0,8},{8,0},{1,9},{9,1},{2,10},{10,2},{3,11},{11,3},{4,12},{12,4},... | collective-permute-start | bytes 6291464 | tf_op jit(solution)/shard_map/ppermute | solution.py:360
  443.9 353.1 %reduce-scatter.6.cloned.1.call-start = ((), (), s32[]{:S(2)}) async-start(), calls=%async_computation.10 | async-start | bytes 5242880 | tf_op jit(solution)/shard_map/reduce_scatter | solution.py:965
  552.4 322.5 %reduce-scatter.8.cloned.1.call-start = ((), (), s32[]{:S(2)}) async-start(), calls=%async_computation.11 | async-start | bytes 5242880 | tf_op jit(solution)/shard_map/reduce_scatter | solution.py:965
  691.4 276.5 %reduce-scatter.10.cloned.1.call-start = ((), (), s32[]{:S(2)}) async-start(), calls=%async_computation.12 | async-start | bytes 5242880 | tf_op jit(solution)/shard_map/reduce_scatter | solution.py:965
  734.1 53.8 %collective-permute-start.98 = (bf16[64,2048]{1,0:T(8,128)(2,1)}, bf16[64,2048]{1,0:T(8,128)(2,1)}, u32[]{:S(2)}, u32[]{:S(2)}) collective-permute-start(bf16[64,2048]{1,0:T(8,128)(2,1)} %slice.1178), channel_id=1, source_target_pairs={{0,1},{1,0},{2,3},{3,2},{4,5},{5,4},{6,7},{7,6},{8,9},{9,8},{10,11... | collective-permute-start | bytes 786440 | tf_op jit(solution)/shard_map/ppermute | solution.py:360
  737.1 140.1 %collective-permute-start.91 = (bf16[4,448,2048]{2,1,0:T(8,128)(2,1)}, bf16[4,448,2048]{2,1,0:T(8,128)(2,1)}, u32[]{:S(2)}, u32[]{:S(2)}) collective-permute-start(bf16[4,448,2048]{2,1,0:T(8,128)(2,1)} %get-tuple-element.578), channel_id=1, source_target_pairs={{0,8},{8,0},{1,9},{9,1},{2,10},{10,2},{3,11},{11,3},{4,12},{12,4},... | collective-permute-start | bytes 22020104 | tf_op jit(solution)/shard_map/ppermute | solution.py:360
  790.0 71.1 %collective-permute-start.103 = (bf16[512,2048]{1,0:T(8,128)(2,1)S(1)}, bf16[512,2048]{1,0:T(8,128)(2,1)}, u32[]{:S(2)}, u32[]{:S(2)}) collective-permute-start(bf16[512,2048]{1,0:T(8,128)(2,1)S(1)} %constant_dynamic-update-slice_fusion.42.refs_0_), channel_id=1, source_target_pairs={{0,8},{8,0},{1,9},{9,1},{2,10},{10,2},{3,11},{11,3},{4,12},{12,4},... | collective-permute-start | bytes 6291464 | tf_op jit(solution)/shard_map/ppermute | solution.py:360
  851.1 278.8 %reduce-scatter.12.cloned.1.call-start = ((), (), s32[]{:S(2)}) async-start(), calls=%async_computation.13 | async-start | bytes 3932160 | tf_op jit(solution)/shard_map/reduce_scatter | solution.py:965
  877.2 59.7 %collective-permute-start.113 = (bf16[2,256,512]{2,1,0:T(8,128)(2,1)}, bf16[2,256,512]{2,1,0:T(8,128)(2,1)}, u32[]{:S(2)}, u32[]{:S(2)}) collective-permute-start(bf16[2,256,512]{2,1,0:T(8,128)(2,1)} %get-tuple-element.620), channel_id=1, source_target_pairs={{0,16},{16,0},{1,17},{17,1},{2,18},{18,2},{3,19},{19,3},{4,20},{20... | collective-permute-start | bytes 1572872 | tf_op jit(solution)/shard_map/ppermute | solution.py:360
  967.7 68.6 %collective-permute-start.116 = (bf16[4,1792,512]{2,1,0:T(8,128)(2,1)}, bf16[4,1792,512]{2,1,0:T(8,128)(2,1)}, u32[]{:S(2)}, u32[]{:S(2)}) collective-permute-start(bf16[4,1792,512]{2,1,0:T(8,128)(2,1)} %get-tuple-element.644), channel_id=1, source_target_pairs={{0,8},{8,0},{1,9},{9,1},{2,10},{10,2},{3,11},{11,3},{4,12},{12,4},... | collective-permute-start | bytes 22020104 | tf_op jit(solution)/shard_map/ppermute | solution.py:360
  996.4 72.8 %collective-permute-start.112 = (bf16[2,256,512]{2,1,0:T(8,128)(2,1)}, bf16[2,256,512]{2,1,0:T(8,128)(2,1)}, u32[]{:S(2)}, u32[]{:S(2)}) collective-permute-start(bf16[2,256,512]{2,1,0:T(8,128)(2,1)} %get-tuple-element.619), channel_id=1, source_target_pairs={{0,8},{8,0},{1,9},{9,1},{2,10},{10,2},{3,11},{11,3},{4,12},{12,4},... | collective-permute-start | bytes 1572872 | tf_op jit(solution)/shard_map/ppermute | solution.py:360
  1046.7 76.3 %collective-permute-start.120 = (bf16[2,896,512]{2,1,0:T(8,128)(2,1)}, bf16[2,896,512]{2,1,0:T(8,128)(2,1)}, u32[]{:S(2)}, u32[]{:S(2)}) collective-permute-start(bf16[2,896,512]{2,1,0:T(8,128)(2,1)} %pad_maximum_fusion.5), channel_id=1, source_target_pairs={{0,1},{1,0},{2,3},{3,2},{4,5},{5,4},{6,7},{7,6},{8,9},{9,8},{10,11... | collective-permute-start | bytes 5505032 | tf_op jit(solution)/shard_map/ppermute | solution.py:360
  1047.6 75.4 %collective-permute-start.119 = (bf16[2,896,512]{2,1,0:T(8,128)(2,1)}, bf16[2,896,512]{2,1,0:T(8,128)(2,1)}, u32[]{:S(2)}, u32[]{:S(2)}) collective-permute-start(bf16[2,896,512]{2,1,0:T(8,128)(2,1)} %pad_maximum_fusion.4), channel_id=1, source_target_pairs={{0,16},{16,0},{1,17},{17,1},{2,18},{18,2},{3,19},{19,3},{4,20},{20... | collective-permute-start | bytes 5505032 | tf_op jit(solution)/shard_map/ppermute | solution.py:360
  1049.5 66.3 %all-to-all-start = ((bf16[8,224,512]{2,1,0:T(8,128)(2,1)}), bf16[8,224,512]{2,1,0:T(8,128)(2,1)S(1)}, u32[]{:S(2)}, u32[]{:S(2)}) async-start(bf16[8,224,512]{2,1,0:T(8,128)(2,1)} %fusion.78), calls=%async_computation.2 | async-start | bytes 3670016 | tf_op jit(solution)/shard_map/all_to_all | solution.py:1224
  1053.1 76.7 %reduce-scatter.14.cloned.1.call-start = ((), (), s32[]{:S(2)}) async-start(), calls=%async_computation.14 | async-start | bytes 1310720 | tf_op jit(solution)/shard_map/reduce_scatter | solution.py:965
  (216 other events, 4339.0 us)
Sparse Core Ops, SparseCore 0:
  30.3 82.2 all-gather.4
  189.3 82.9 all-gather.6
  273.9 79.2 all-gather.8
  444.0 85.0 all-gather.10
  552.5 75.4 reduce-scatter.5
  691.5 75.5 reduce-scatter.7
  851.2 77.8 reduce-scatter.9
  989.1 60.9 reduce-scatter.11
  1062.7 28.7 reduce-scatter.13

commit v3 on v2

--- a/solution.py
+++ b/solution.py
@@ -430,6 +430,8 @@
             value = end.value[-1] if isinstance(end.value, list) else end.value
             if value is not None:
                 self.extra.append(value)
+            if name == "mixed":
+                self.extra += list(got)
 
     def tick(self, large, *names):
         if large is None:
@@ -795,6 +797,34 @@
         compiler_params=params(),
         cost_estimate=cost(2 * rows * width * tokens, 2 * tokens * (rows + width)),
     )(*lefts, *rights)
+
+
+def join_kernel(d_qkv, low, weight, grad, share):
+    total = mm(d_qkv[...], low[...])
+    grad[...] = total.astype(BF)
+    sums = jnp.sum(total * weight[...].astype(F32), 0, keepdims=True)
+    share[...] = jnp.broadcast_to(sums, share.shape)
+
+
+def join_product(d_qkv, low, weight):
+    rows, width = weight.shape
+    tile = 512
+    return pl.pallas_call(
+        join_kernel,
+        grid=(width // tile,),
+        in_specs=[
+            whole_spec(d_qkv.shape),
+            pl.BlockSpec((low.shape[0], tile), lambda j: (0, j)),
+            pl.BlockSpec((rows, tile), lambda j: (0, j)),
+        ],
+        out_specs=[
+            pl.BlockSpec((rows, tile), lambda j: (0, j)),
+            pl.BlockSpec((8, tile), lambda j: (0, j)),
+        ],
+        out_shape=[jax.ShapeDtypeStruct((rows, width), BF), jax.ShapeDtypeStruct((8, width), F32)],
+        compiler_params=params(),
+        cost_estimate=cost(2 * rows * width * low.shape[0], 2 * low.shape[0] * (rows + width)),
+    )(d_qkv, low, weight)
 
 
 def last_kernel(places, d_qkv, weight, keep, send, whole):
@@ -886,6 +916,13 @@
     lines = Lines()
     tick = lines.tick
 
+    def unit_rows(weight):
+        pieces = yield from spread_steps(weight.reshape(4, units // 4, width))
+        pieces = jnp.concatenate([pieces[k] for k in range(4)], 1)
+        if quick:
+            lines.extra.append(pieces)
+        return [lax.all_gather(pieces, "z", axis=0, tiled=True), pieces]
+
     joined = jnp.stack([query_weight.T, key_weight.T, value_weight.T, output_weight])
     if heads % 4 == 0:
         per = heads // 4
@@ -894,8 +931,11 @@
             from_y = flip(hidden_in, "y")
             lines.start("heads", spread_steps(pieces))
             tick(None, "heads")
-            from_x = flip(after(hidden_in, lines.wanted["heads"][1][0][0]), "x")
+            lines.start("gate", unit_rows(after(gate_weight, lines.wanted["heads"][1][0][0]).T))
             tick(None, "heads")
+            tick(None, "gate")
+            from_x = flip(after(hidden_in, lines.wanted["gate"][1][0][0]), "x")
+            tick(None, "gate")
             pieces = lines.results["heads"]
         else:
             pieces = spread(pieces)
@@ -909,13 +949,6 @@
     join_weight = attend_weights[:, :ROWS].reshape(heads * ROWS, depth)
     out_weight = attend_weights[:, ROWS:].reshape(heads * HD, depth)
 
-    def unit_rows(weight):
-        pieces = yield from spread_steps(weight.reshape(4, units // 4, width))
-        pieces = jnp.concatenate([pieces[k] for k in range(4)], 1)
-        if quick:
-            lines.extra.append(pieces)
-        return [lax.all_gather(pieces, "z", axis=0, tiled=True), pieces]
-
     gains = row_gather(after(jnp.stack([gain_before, gain_middle]), pieces))
     gains = gains.transpose(1, 0, 2).reshape(2, depth)
     gain_one, gain_two = gains[0], gains[1]
@@ -968,8 +1001,11 @@
         part = yield from spread_steps(columns_of(part, 4, width))
         return part.reshape(-1, width)
 
-    def outcome(mixed, join_grad):
-        layer_out = (jnp.concatenate([middles[k] for k in ordered], 0) + mixed).astype(BF)
+    def squares_one():
+        wide = hidden_in.astype(F32)
+        return jnp.sum(wide * wide, -1)
+
+    def outcome(layer_out, share):
         here = jnp.arange(BLOCKS, dtype=jnp.int32)
         bound = jnp.where(here < PBLKS, BLK, jnp.take(length_row, jnp.maximum(here - PBLKS, 0)))
         slots = rank * sub + jnp.arange(sub, dtype=jnp.int32)
@@ -985,9 +1021,9 @@
                 for parts in (attentions, d_middles)
             ]
         )
-        before_local = jnp.sum(join_grad * join_weight.astype(F32), 0) / gain_one
+        before_local = share / gain_one
         middle_local = sum(notes[k] for k in steps)
-        return layer_out, jnp.concatenate([before_local, middle_local, squares])
+        return jnp.concatenate([before_local, middle_local, squares])
 
     heads_parts, lse_parts, lows, gates, ups, hiddens = ([] for _ in range(6))
     gate_parts, up_parts = [], []
@@ -996,7 +1032,6 @@
         corner = jnp.concatenate([former, latter], 0)
         four = [hidden_in, from_x, from_y, corner]
         hidden_pieces = [p for piece in four for p in (piece, flip(piece, "c"))]
-        lines.start("gate", unit_rows(after(gate_weight, corner).T))
         lines.start("up", unit_rows(up_weight.T))
         lines.start("down", unit_rows(down_weight))
         lines.start("late", place_steps(after(cotangent, corner)))
@@ -1010,7 +1045,7 @@
                 (join_weight, cosine, sine),
                 heads,
             ),
-            "gate",
+            "up",
         )
 
         def forward_line(k, partial):
@@ -1028,10 +1063,10 @@
             lines.last = [partial[0]]
             lines.start(k, forward_line(k, partial))
 
-        attend(0, "gate", "up")
+        attend(0, "up")
         lines.land("late")
         attend(1, 0, "late")
-        attend(2, 0, 1, "up", "late")
+        attend(2, 0, 1, "down", "late")
         attend(3, 0, 1, 2)
         gate_rows, up_rows = lines.results["gate"][0], lines.results["up"][0]
         upstream_rows, upstream = tick(
@@ -1048,15 +1083,23 @@
             ups.append(up)
             hiddens.append(hidden)
 
-        tick(None, 0, 2, "down")
-        tick(None, 0, 1, 2, "down")
+        def gathered(k):
+            lines.last = [lines.wanted[k][1][0][0]]
+            tick(None, k)
+
+        tick(None, 0, "down")
         down_rows = lines.results["down"][0]
-        unit(0, 1, 3)
+        gathered(0)
+        unit(0, 1, 2)
         tick(None, 1, 2)
+        gathered(1)
         unit(1, 2, 3)
         tick(None, 2, 3)
+        gathered(2)
+        lines.extra.append(down_rows)
         unit(2, 3)
         tick(None, 3)
+        gathered(3)
         unit(3)
         down_grad = tick(lambda ties: grad_product(hiddens, [after(upstream_rows, *ties)], TN, starts))
         down_sum = total(down_grad)
@@ -1101,11 +1144,12 @@
         )
         lines.start("mixed", sum_steps(*mixed))
         before = tick(lambda ties: backward(conts, ties), 2, 3, "mixed")
+        lines.start("scale", summed(squares_one(), ("x", "c")))
+        up_grad = tick(lambda ties: grad_product(after(up_parts, *ties), lows), 2, 3, "scale")
+        up_sum = total(up_grad)
+        tick(None, 3, "scale")
+        tick(None, 3)
         lines.start("down", home_steps(down_sum))
-        up_grad = tick(lambda ties: grad_product(after(up_parts, *ties), lows), 2, 3, "down")
-        up_sum = total(up_grad)
-        tick(None, 3)
-        tick(None, 3)
         lines.start("gate", home_steps(gate_sum))
         d_qkv, inner = tick(lambda ties: backward(prompts, ties, before), "mixed", "down", "gate")
         inner = straighten(inner[0].reshape(BLOCKS, team, sub), rank).reshape(GTOK)
@@ -1114,17 +1158,30 @@
         own, other = tick(
             lambda ties: last_product(places, after(d_qkv, *ties), join_weight),
             "mixed",
+            "down",
             "gate",
             "inner",
         )
         lines.start("last", sum_steps(own, other))
-        join_grad = tick(lambda ties: mm(d_qkv, after(low_one, *ties)), "last", "up", "inner")
-        join_sum = total(join_grad.astype(BF))
         mixed = lines.results["mixed"]
-        layer_out, sums = outcome(mixed, join_grad)
-        lines.start("sums", summed(sums, ("x", "y", "c", "z1", "z2")))
-        tick(None, "sums")
-        tick(None, "sums")
+        layer_out = (jnp.concatenate([middles[k] for k in ordered], 0) + mixed).astype(BF)
+        rows = local_tokens // team
+        layer_pieces = jnp.stack(
+            [
+                layer_out[h * rows : (h + 1) * rows, k * width : (k + 1) * width]
+                for h in range(2)
+                for k in range(4)
+            ]
+        )
+        lines.extra.append(layer_pieces)
+        layer_pieces = lax.all_to_all(layer_pieces, TEAM, 0, 0, tiled=True)
+        join_grad, share = tick(
+            lambda ties: join_product(after(d_qkv, *ties), low_one, join_weight),
+            "last",
+            "up",
+            "inner",
+        )
+        join_sum = total(join_grad)
         out_grad = tick(
             lambda ties: grad_product(
                 after([heads_parts[k] for k in ordered], *ties), [attended[k] for k in ordered], NN
@@ -1133,10 +1190,18 @@
             "inner",
             "up",
         )
-        tick(None, "last", "sums")
-        tick(None, "sums")
-        tick(None, "sums")
+        turned = lines.wanted["last"][1][0][0]
+        sums = outcome(after(layer_out, out_grad), share[0])
+        lines.start("sums", summed(after(sums, turned), ("c", "z1", "z2", "x", "y")))
+        tick(None, "last")
+        for _ in range(5):
+            tick(None, "sums")
         d_one, inner, sums = (lines.results[n] for n in ("last", "inner", "sums"))
+        join_sum, up_home = after((join_sum, lines.results["up"]), turned)
+        lines.results["up"] = up_home
+        lines.results["gate"], lines.results["down"], attended, layer_pieces, inner = after(
+            (lines.results["gate"], lines.results["down"], attended, layer_pieces, inner), out_grad
+        )
         gate_grad, up_grad, down_grad = (lines.results[n] for n in ("gate", "up", "down"))
     else:
 
@@ -1178,10 +1243,10 @@
         )
         d_qkv, inner = backward(prompts, [], backward(conts, []))
         partial = mm(d_qkv, join_weight, TN).astype(BF)
-        join_grad = mm(d_qkv, low_one)
+        join_grad, share = join_product(d_qkv, low_one, join_weight)
         out_grad = grad_product([heads_parts[k] for k in ordered], [attended[k] for k in ordered], NN)
-        layer_out, sums = outcome(mixed, join_grad)
-        sums = lax.psum(sums, EVERY)
+        layer_out = (jnp.concatenate([middles[k] for k in ordered], 0) + mixed).astype(BF)
+        sums = lax.psum(outcome(layer_out, share[0]), EVERY)
         gate_grad, up_grad, down_grad = (
             complete(home_steps(part)) for part in (gate_sum, up_sum, down_sum)
         )
@@ -1190,15 +1255,15 @@
     gate_grad, up_grad = gate_grad.T.astype(F32), up_grad.T.astype(F32)
     down_grad = down_grad.astype(F32)
     if heads % 4 == 0:
-        part = join_sum if quick else total(join_grad.astype(BF))
-        part = part.reshape(heads // 4, 3, HD, depth)
-        out_part = total(out_grad).reshape(heads // 4, 1, HD, depth)
-        part = jnp.concatenate([part, out_part], 1).transpose(1, 0, 2, 3)
-        part = spread(columns_of(part.reshape(4, heads // 4 * HD, depth), 4, width))
-        part = part.transpose(1, 0, 2, 3).reshape(4, head_width, width)
+        part = join_sum if quick else total(join_grad)
+        part = part.reshape(heads // 4, 3, HD, depth).transpose(1, 0, 2, 3)
+        part = spread(columns_of(part.reshape(3, heads // 4 * HD, depth), 4, width))
+        part = part.transpose(1, 0, 2, 3).reshape(3, head_width, width)
+        out_part = spread(columns_of(total(out_grad), 4, width)).reshape(1, head_width, width)
+        part = jnp.concatenate([part, out_part], 0)
     else:
         part = jnp.concatenate(
-            [join_grad.astype(BF).reshape(heads, 3, HD, depth), out_grad.reshape(heads, 1, HD, depth)], 1
+            [join_grad.reshape(heads, 3, HD, depth), out_grad.reshape(heads, 1, HD, depth)], 1
         ).transpose(1, 0, 2, 3)
         part = spread(columns_of(part.reshape(4, heads * HD, depth), 4, width))
         part = lax.psum_scatter(part, "z", scatter_dimension=0, tiled=False)
@@ -1213,16 +1278,7 @@
         )
         d_middle = pick(d_middle.reshape(2, BLOCKS // 2, team, sub, width), y)
         d_middle = straighten(d_middle, rank).reshape(half, width).astype(F32)
-        rows = half // team
-        layer_out = jnp.stack(
-            [
-                layer_out[h * rows : (h + 1) * rows, k * width : (k + 1) * width]
-                for h in range(2)
-                for k in range(4)
-            ]
-        )
-        layer_out = lax.all_to_all(layer_out, TEAM, 0, 0, tiled=True)
-        layer_out = layer_out.reshape(team, BLOCKS // 2, sub, width).transpose(1, 0, 2, 3)
+        layer_out = layer_pieces.reshape(team, BLOCKS // 2, sub, width).transpose(1, 0, 2, 3)
         layer_out = layer_out.reshape(half, width)
     else:
         d_one = lax.psum_scatter(partial, "y", scatter_dimension=0, tiled=True)
@@ -1238,7 +1294,8 @@
         ).reshape(GTOK, depth)
         layer_out = lax.dynamic_slice(layer_out, corner, (local_tokens, width))
     wide = hidden_in.astype(F32)
-    scale_one = lax.rsqrt(row_sum(jnp.sum(wide * wide, -1)) / depth + EPSILON)[:, None]
+    row_squares = lines.results["scale"] if quick else row_sum(squares_one())
+    scale_one = lax.rsqrt(row_squares / depth + EPSILON)[:, None]
     norm_one = wide * scale_one
     input_grad = d_middle + scale_one * (d_one * gain_before - norm_one * (inner / depth)[:, None])
 

time: 1190 us -> 1090 us (0.916)
  waiting for transfers between devices: 273 us -> 158 us
  other arithmetic: 127 us -> 147 us
  matrix products: 17.7 us -> 0 us
  Pallas kernels: 490 us -> 504 us
  starting transfers between devices: 108 us -> 122 us
    ppermute x132 -> x134, waiting for transfers between devices: 259 us -> 153 us  [flip(): return lax.ppermute(values, axis, [(0, 1), (1, 0)])]
    dot_general x1 -> x0, matrix products: 17.7 us -> none  [mm(): return lax.dot_general(a, b, dims, preferred_element_type=F32)]
    pallas_call x0 -> x1, Pallas kernels: none -> 17.1 us  [join_product(): pl.pallas_call(join_kernel, grid=(width // tile,), in_specs=[whole_spec(d...]
    unnamed x254 -> x258, local copies, waits for them, and re-layouts: 62.2 us -> 54.9 us
    ppermute x132 -> x134, starting transfers between devices: 101 us -> 106 us  [flip(): return lax.ppermute(values, axis, [(0, 1), (1, 0)])]
  transfers between devices with their start and end apart: 144 -> 146, of which waited for: 31 -> 34; matrix products, arithmetic and copies ran while one was open for 22% -> 24% of each run, Pallas kernels for 40% -> 41%
where the time goes in v3:
time: 1090 us
  Pallas kernels  504 us (46%)
  waiting for transfers between devices  158 us (14%)
  other arithmetic  147 us (13%)
  local copies, waits for them, and re-layouts  133 us (12%)
  starting transfers between devices  122 us (11%)
  between operations  22.4 us (2%)
    ppermute x134, waiting for transfers between devices, flip(): return lax.ppermute(values, axis, [(0, 1), (1, 0)])  153 us
    ppermute x134, starting transfers between devices, flip(): return lax.ppermute(values, axis, [(0, 1), (1, 0)])  106 us
    pallas_call x2, Pallas kernels, attend_backward(): pl.pallas_call(functools.partial(backward_kernel, heads, 0 if final else...  87.9 us
    pallas_call x4, Pallas kernels, grad_product(): pl.pallas_call(functools.partial(grad_kernel, len(lefts), form, starts),...  74.3 us
    pallas_call x8, Pallas kernels, split_product(): pl.pallas_call(functools.partial(split_kernel, len(pairs), form, sub), gr...  67.6 us
    pallas_call x4, Pallas kernels, attend_forward(): pl.pallas_call(functools.partial(forward_kernel, heads, first), grid=(cou...  59.1 us
    unnamed x258, local copies, waits for them, and re-layouts  54.9 us
    pallas_call x4, Pallas kernels, unit_products(): pl.pallas_call(functools.partial(unit_kernel, len(pieces)), grid=(units /...  51.2 us
  transfers between devices with their start and end apart: 146, of which 34 were waited for; matrix products, arithmetic and copies ran while one was open for 24% of the time, Pallas kernels for 41%

profile of v3, /device:TPU:0, one launch (start us, length us, event | category | flops | bytes accessed | tf_op | source)
XLA Modules:
  0.0 1086.5 jit_solution(6029304459407121433)
XLA Ops:
  14.7 11.9 %collective-permute-done.2 = bf16[2,4,64,512]{3,2,0,1:T(8,128)(2,1)S(1)} collective-permute-done((bf16[2,4,64,512]{3,2,0,1:T(8,128)(2,1)S(1)}, bf16[2,4,64,512]{3,2,0,1:T(8,128)(2,1)S(1)}, u32[]{:S(2)}, u32[]{:S(2)}) %collective-permute-start.2) | collective-permute-done | bytes 524320 | tf_op jit(solution)/shard_map/ppermute | solution.py:360
  57.1 21.5 %collective-permute-done.refs_4_ = bf16[1792,512]{1,0:T(8,128)(2,1)} collective-permute-done((bf16[1792,512]{1,0:T(8,128)(2,1)S(1)}, bf16[1792,512]{1,0:T(8,128)(2,1)}, u32[]{:S(2)}, u32[]{:S(2)}) %collective-permute-start) | collective-permute-done | bytes 1835040 | tf_op jit(solution)/shard_map/ppermute | solution.py:360
  81.0 11.5 %collective-permute-done.4.refs_2_ = bf16[1792,512]{1,0:T(8,128)(2,1)} collective-permute-done((bf16[1792,512]{1,0:T(8,128)(2,1)S(1)}, bf16[1792,512]{1,0:T(8,128)(2,1)}, u32[]{:S(2)}, u32[]{:S(2)}) %collective-permute-start.4) | collective-permute-done | bytes 1835040 | tf_op jit(solution)/shard_map/ppermute | solution.py:360
  134.7 27.0 %shard_map.220 = (bf16[3584,2048]{1,0:T(8,128)(2,1)}, bf16[448,2048]{1,0:T(8,128)(2,1)}, bf16[768,3584]{1,0:T(8,128)(2,1)}, bf16[4,3584,64]{2,1,0:T(8,128)(2,1)}, bf16[4,3584,64]{2,1,0:T(8,128)(2,1)}) custom-call(s32[3]{0:T(128)} %pad_add_fusion.places, bf16[1792,512]{1,0:T(8,128)(2,1)} %refs_0_, bf16[1792,512]{1,0:T(8,128)(2,1)} %collective-permute-done.9.refs_1_, ...), custom_call_target="tpu_custom_call" | custom-call | flops 11318329344 | bytes 36700160 | tf_op jit(solution)/shard_map/pallas_call | solution.py:574
  162.0 16.1 %shard_map.221 = (bf16[256,768]{1,0:T(8,128)(2,1)}, f32[8,768]{1,0:T(8,128)}) custom-call(s32[13]{0:T(128)} %pad_add_fusion.1.info, bf16[768,3584]{1,0:T(8,128)(2,1)} %get-tuple-element.633.qkv, bf16[4,3584,64]{2,1,0:T(8,128)(2,1)} %get-tuple-element.373.knat), custom_call_target="tpu_custom_call" | custom-call | flops 12079595520 | bytes 16777216 | tf_op jit(solution)/shard_map/pallas_call | solution.py:117
  192.5 14.7 %shard_map.223 = (bf16[256,768]{1,0:T(8,128)(2,1)}, f32[8,768]{1,0:T(8,128)}) custom-call(s32[13]{0:T(128)} %pad_add_fusion.1.info, bf16[768,3584]{1,0:T(8,128)(2,1)} %get-tuple-element.633.qkv, bf16[4,3584,64]{2,1,0:T(8,128)(2,1)} %get-tuple-element.373.knat), custom_call_target="tpu_custom_call" | custom-call | flops 12079595520 | bytes 16777216 | tf_op jit(solution)/shard_map/pallas_call | solution.py:117
  222.0 11.2 %shard_map.225 = (bf16[256,1024]{1,0:T(8,128)(2,1)}, f32[8,1024]{1,0:T(8,128)}) custom-call(s32[13]{0:T(128)} %pad_add_fusion.1.info, bf16[768,3584]{1,0:T(8,128)(2,1)} %get-tuple-element.633.qkv, bf16[4,3584,64]{2,1,0:T(8,128)(2,1)} %get-tuple-element.373.knat), custom_call_target="tpu_custom_call" | custom-call | flops 16106127360 | bytes 16777216 | tf_op jit(solution)/shard_map/pallas_call | solution.py:117
  249.6 17.1 %shard_map.227 = (bf16[256,1024]{1,0:T(8,128)(2,1)}, f32[8,1024]{1,0:T(8,128)}) custom-call(s32[13]{0:T(128)} %pad_add_fusion.1.info, bf16[768,3584]{1,0:T(8,128)(2,1)} %get-tuple-element.633.qkv, bf16[4,3584,64]{2,1,0:T(8,128)(2,1)} %get-tuple-element.373.knat), custom_call_target="tpu_custom_call" | custom-call | flops 16106127360 | bytes 16777216 | tf_op jit(solution)/shard_map/pallas_call | solution.py:117
  280.2 17.4 %shard_map.229 = (bf16[3584,2048]{1,0:T(8,128)(2,1)}, bf16[448,2048]{1,0:T(8,128)(2,1)}) custom-call(s32[3]{0:T(128)} %pad_add_fusion.places, bf16[1792,512]{1,0:T(8,128)(2,1)} %refs_0_.1, bf16[1792,512]{1,0:T(8,128)(2,1)} %collective-permute-done.8.refs_1_, bf16[1792,512]{1,0:T(8,128)(2,1)} %collective-permute-done.6.refs_2_, ...), custom_call_target="tpu_custom_call" | custom-call | flops 44040192 | bytes 36700160 | tf_op jit(solution)/shard_map/pallas_call | solution.py:574
  327.6 11.8 %shard_map.230 = (bf16[768,2048]{1,0:T(8,128)(2,1)}, bf16[768,1024]{1,0:T(8,128)(2,1)}, bf16[768,1024]{1,0:T(8,128)(2,1)}, bf16[768,1024]{1,0:T(8,128)(2,1)}) custom-call(bf16[384,2048]{1,0:T(8,128)(2,1)} %constant_dynamic-update-slice_fusion.4.refs_0_, bf16[384,2048]{1,0:T(8,128)(2,1)} %collective-permute-done.38.refs_1_, ...), custom_call_target="tpu_custom_call" | custom-call | flops 6442450944 | bytes 14680064 | tf_op jit(solution)/shard_map/pallas_call | solution.py:709
  363.6 11.4 %shard_map.231 = (bf16[768,2048]{1,0:T(8,128)(2,1)}, bf16[768,1024]{1,0:T(8,128)(2,1)}, bf16[768,1024]{1,0:T(8,128)(2,1)}, bf16[768,1024]{1,0:T(8,128)(2,1)}) custom-call(bf16[384,2048]{1,0:T(8,128)(2,1)} %copy-done.72, bf16[384,2048]{1,0:T(8,128)(2,1)} %collective-permute-done.46.refs_1_, bf16[1024,2048]{1,0:T(8,128)(2,1)} %all-gather.9.cloned.1.call-done.refs_2_.refs_1_, ...), custom_call_target="tpu_custom_call" | custom-call | flops 6442450944 | bytes 14680064 | tf_op jit(solution)/shard_map/pallas_call | solution.py:709
  409.9 14.0 %shard_map.232 = (bf16[1024,2048]{1,0:T(8,128)(2,1)}, bf16[1024,1024]{1,0:T(8,128)(2,1)}, bf16[1024,1024]{1,0:T(8,128)(2,1)}, bf16[1024,1024]{1,0:T(8,128)(2,1)}) custom-call(bf16[512,2048]{1,0:T(8,128)(2,1)} %constant_dynamic-update-slice_fusion.14.refs_0_, bf16[512,2048]{1,0:T(8,128)(2,1)} %collective-permute-done.56.refs_1_, ...), custom_call_target="tpu_custom_call" | custom-call | flops 8589934592 | bytes 16777216 | tf_op jit(solution)/shard_map/pallas_call | solution.py:709
  439.4 14.0 %shard_map.233 = (bf16[1024,2048]{1,0:T(8,128)(2,1)}, bf16[1024,1024]{1,0:T(8,128)(2,1)}, bf16[1024,1024]{1,0:T(8,128)(2,1)}, bf16[1024,1024]{1,0:T(8,128)(2,1)}) custom-call(bf16[512,2048]{1,0:T(8,128)(2,1)} %copy-done.70, bf16[512,2048]{1,0:T(8,128)(2,1)} %copy-done.97, bf16[1024,2048]{1,0:T(8,128)(2,1)} %all-gather.9.cloned.1.call-done.refs_2_.refs_1_, ...), custom_call_target="tpu_custom_call" | custom-call | flops 8589934592 | bytes 16777216 | tf_op jit(solution)/shard_map/pallas_call | solution.py:709
  453.4 21.8 %shard_map.234 = bf16[1024,2048]{1,0:T(8,128)(2,1)} custom-call(bf16[768,1024]{1,0:T(8,128)(2,1)} %get-tuple-element.585.refs_0_.refs_2_, bf16[768,1024]{1,0:T(8,128)(2,1)} %get-tuple-element.586.refs_1_.refs_3_, bf16[1024,1024]{1,0:T(8,128)(2,1)} %get-tuple-element.583.refs_2_.refs_0_, bf16[1024,1024]{1,0:T(8,128)(2,1)} %get-tuple-element.584.refs_3_.refs_1_, ...), custom_call_target="tpu_custom_call" | custom-call | flops 15032385536 | bytes 22020096 | tf_op jit(solution)/shard_map/pallas_call | solution.py:790
  546.5 13.3 %shard_map.240 = (bf16[4,128,2048]{2,1,0:T(8,128)(2,1)}, bf16[4,128,2048]{2,1,0:T(8,128)(2,1)}) custom-call(bf16[1024,1024]{1,0:T(8,128)(2,1)} %get-tuple-element.572.refs_0_.refs_2_, bf16[1024,2048]{1,0:T(8,128)(2,1)} %all-gather.9.cloned.1.call-done.refs_2_.refs_1_, bf16[1024,1024]{1,0:T(8,128)(2,1)} %get-tuple-element.616.refs_2_, ...), custom_call_target="tpu_custom_call" | custom-call | flops 8589934592 | bytes 16777216 | tf_op jit(solution)/shard_map/pallas_call | solution.py:632
  589.5 13.4 %shard_map.242 = (bf16[4,128,2048]{2,1,0:T(8,128)(2,1)}, bf16[4,128,2048]{2,1,0:T(8,128)(2,1)}) custom-call(bf16[1024,1024]{1,0:T(8,128)(2,1)} %get-tuple-element.573.refs_0_.refs_3_, bf16[1024,2048]{1,0:T(8,128)(2,1)} %all-gather.9.cloned.1.call-done.refs_2_.refs_1_, bf16[1024,1024]{1,0:T(8,128)(2,1)} %get-tuple-element.617.refs_2_.refs_3_, ...), custom_call_target="tpu_custom_call" | custom-call | flops 8589934592 | bytes 16777216 | tf_op jit(solution)/shard_map/pallas_call | solution.py:632
  614.8 21.5 %shard_map.244 = bf16[1024,2048]{1,0:T(8,128)(2,1)} custom-call(bf16[768,1024]{1,0:T(8,128)(2,1)} %get-tuple-element.570.refs_0_, bf16[768,1024]{1,0:T(8,128)(2,1)} %get-tuple-element.571.refs_0_.refs_1_, bf16[1024,1024]{1,0:T(8,128)(2,1)} %get-tuple-element.572.refs_0_.refs_2_, bf16[1024,1024]{1,0:T(8,128)(2,1)} %get-tuple-element.573.refs_0_.refs_3_, ...), custom_call_target="tpu_custom_call" | custom-call | flops 15032385536 | bytes 22020096 | tf_op jit(solution)/shard_map/pallas_call | solution.py:790
  652.6 21.5 %shard_map.245 = (bf16[4,448,2048]{2,1,0:T(8,128)(2,1)}, bf16[4,448,2048]{2,1,0:T(8,128)(2,1)}) custom-call(bf16[1024,1024]{1,0:T(8,128)(2,1)} %get-tuple-element.583.refs_2_.refs_0_, bf16[1024,1024]{1,0:T(8,128)(2,1)} %get-tuple-element.584.refs_3_.refs_1_, bf16[768,1024]{1,0:T(8,128)(2,1)} %get-tuple-element.585.refs_0_.refs_2_, ...), custom_call_target="tpu_custom_call" | custom-call | flops 15032385536 | bytes 22020096 | tf_op jit(solution)/shard_map/pallas_call | solution.py:663
  691.4 45.4 %shard_map.247 = (f32[256,3584]{1,0:T(8,128)}, f32[256,3584]{1,0:T(8,128)}, bf16[256,1536]{1,0:T(8,128)(2,1)}, f32[8,1536]{1,0:T(8,128)}) custom-call(s32[13]{0:T(128)} %pad_add_fusion.1.info, bf16[768,3584]{1,0:T(8,128)(2,1)} %get-tuple-element.633.qkv, bf16[4,3584,64]{2,1,0:T(8,128)(2,1)} %get-tuple-element.373.knat, ...), custom_call_target="tpu_custom_call" | custom-call | flops 45097156608 | bytes 33554432 | tf_op jit(solution)/shard_map/pallas_call | solution.py:288
  745.4 21.6 %shard_map.248 = bf16[1024,2048]{1,0:T(8,128)(2,1)} custom-call(bf16[768,1024]{1,0:T(8,128)(2,1)} %get-tuple-element.614.refs_2_.refs_0_, bf16[768,1024]{1,0:T(8,128)(2,1)} %get-tuple-element.615.refs_2_.refs_1_, bf16[1024,1024]{1,0:T(8,128)(2,1)} %get-tuple-element.616.refs_2_, bf16[1024,1024]{1,0:T(8,128)(2,1)} %get-tuple-element.617.refs_2_.refs_3_, ...), custom_call_target="tpu_custom_call" | custom-call | flops 15032385536 | bytes 22020096 | tf_op jit(solution)/shard_map/pallas_call | solution.py:790
  820.0 42.4 %shard_map.251 = (bf16[768,3584]{1,0:T(8,128)(2,1)}, f32[8,3584]{1,0:T(8,128)}) custom-call(s32[13]{0:T(128)} %pad_add_fusion.1.info, bf16[768,3584]{1,0:T(8,128)(2,1)} %get-tuple-element.633.qkv, bf16[4,3584,64]{2,1,0:T(8,128)(2,1)} %get-tuple-element.373.knat, bf16[4,3584,64]{2,1,0:T(8,128)(2,1)} %get-tuple-element.601.vnat, ...), custom_call_target="tpu_custom_call" | custom-call | flops 45097156608 | bytes 33554432 | tf_op jit(solution)/shard_map/pallas_call | solution.py:288
  876.3 20.9 %shard_map.252 = (bf16[4,1792,512]{2,1,0:T(8,128)(2,1)}, bf16[4,1792,512]{2,1,0:T(8,128)(2,1)}) custom-call(s32[3]{0:T(128)} %pad_add_fusion.places, bf16[768,3584]{1,0:T(8,128)(2,1)} %get-tuple-element.663.d_qkv, bf16[768,2048]{1,0:T(8,128)(2,1)} %bitcast.425), custom_call_target="tpu_custom_call" | custom-call | flops 11274289152 | bytes 14680064 | tf_op jit(solution)/shard_map/pallas_call | solution.py:850
  915.0 17.1 %shard_map.253 = (bf16[768,2048]{1,0:T(8,128)(2,1)}, f32[8,2048]{1,0:T(8,128)}) custom-call(bf16[768,3584]{1,0:T(8,128)(2,1)} %get-tuple-element.663.d_qkv, bf16[3584,2048]{1,0:T(8,128)(2,1)} %get-tuple-element.369.low, bf16[768,2048]{1,0:T(8,128)(2,1)} %bitcast.426), custom_call_target="tpu_custom_call" | custom-call | flops 11274289152 | bytes 20185088 | tf_op jit(solution)/shard_map/pallas_call | solution.py:812
  1039.8 17.5 %collective-permute-done.130 = f32[4099]{0:T(1024)S(1)} collective-permute-done((f32[4099]{0:T(1024)S(1)}, f32[4099]{0:T(1024)S(1)}, u32[]{:S(2)}, u32[]{:S(2)}) %collective-permute-start.130) | collective-permute-done | bytes 16428 | tf_op jit(solution)/shard_map/ppermute | solution.py:360
  (863 shorter events, 608.0 us)
Async XLA Ops:
  7.2 123.5 %all-gather.5.cloned.1.call-start = ((), (), s32[]{:S(2)}) async-start(), calls=%async_computation.6 | async-start | bytes 5242880 | tf_op jit(solution)/shard_map/all_gather | solution.py:944
  30.1 297.4 %all-gather.9.cloned.1.call-start = ((), (), s32[]{:S(2)}) async-start(), calls=%async_computation.8 | async-start | bytes 5242880 | tf_op jit(solution)/shard_map/all_gather | solution.py:924
  51.2 76.2 %collective-permute-start.9 = (bf16[1792,512]{1,0:T(8,128)(2,1)S(1)}, bf16[1792,512]{1,0:T(8,128)(2,1)}, u32[]{:S(2)}, u32[]{:S(2)}) collective-permute-start(bf16[1792,512]{1,0:T(8,128)(2,1)S(1)} %copy-done.17), channel_id=1, source_target_pairs={{0,8},{8,0},{1,9},{9,1},{2,10},{10,2},{3,11},{11,3},{4,12},{12,4},... | collective-permute-start | bytes 5505032 | tf_op jit(solution)/shard_map/ppermute | solution.py:360
  56.7 270.8 %all-gather.11.cloned.1.call-start = ((), (), s32[]{:S(2)}) async-start(), calls=%async_computation.9 | async-start | bytes 5242880 | tf_op jit(solution)/shard_map/all_gather | solution.py:924
  127.4 57.6 %collective-permute-start.8 = (bf16[1792,512]{1,0:T(8,128)(2,1)}, bf16[1792,512]{1,0:T(8,128)(2,1)}, u32[]{:S(2)}, u32[]{:S(2)}) collective-permute-start(bf16[1792,512]{1,0:T(8,128)(2,1)} %refs_0_.1), channel_id=1, source_target_pairs={{0,8},{8,0},{1,9},{9,1},{2,10},{10,2},{3,11},{11,3},{4,12},{12,4},... | collective-permute-start | bytes 5505032 | tf_op jit(solution)/shard_map/ppermute | solution.py:360
  127.4 57.6 %collective-permute-start.7 = (bf16[1792,512]{1,0:T(8,128)(2,1)}, bf16[1792,512]{1,0:T(8,128)(2,1)S(1)}, u32[]{:S(2)}, u32[]{:S(2)}) collective-permute-start(bf16[1792,512]{1,0:T(8,128)(2,1)} %refs_0_.1), channel_id=1, source_target_pairs={{0,1},{1,0},{2,3},{3,2},{4,5},{5,4},{6,7},{7,6},{8,9},{9,8},{10,11... | collective-permute-start | bytes 5505032 | tf_op jit(solution)/shard_map/ppermute | solution.py:360
  129.2 55.9 %collective-permute-start.6 = (bf16[1792,512]{1,0:T(8,128)(2,1)}, bf16[1792,512]{1,0:T(8,128)(2,1)}, u32[]{:S(2)}, u32[]{:S(2)}) collective-permute-start(bf16[1792,512]{1,0:T(8,128)(2,1)} %refs_0_.1), channel_id=1, source_target_pairs={{0,16},{16,0},{1,17},{17,1},{2,18},{18,2},{3,19},{19,3},{4,20},{20... | collective-permute-start | bytes 5505032 | tf_op jit(solution)/shard_map/ppermute | solution.py:360
  191.9 218.1 %all-gather.7.cloned.1.call-start = ((), (), s32[]{:S(2)}) async-start(), calls=%async_computation.7 | async-start | bytes 5242880 | tf_op jit(solution)/shard_map/all_gather | solution.py:924
  238.3 63.2 %collective-permute-start.41 = (bf16[4,128,2048]{2,1,0:T(8,128)(2,1)}, bf16[4,128,2048]{2,1,0:T(8,128)(2,1)}, u32[]{:S(2)}, u32[]{:S(2)}) collective-permute-start(bf16[4,128,2048]{2,1,0:T(8,128)(2,1)} %get-tuple-element.412), channel_id=1, source_target_pairs={{0,8},{8,0},{1,9},{9,1},{2,10},{10,2},{3,11},{11,3},{4,12},{12,4},... | collective-permute-start | bytes 6291464 | tf_op jit(solution)/shard_map/ppermute | solution.py:360
  317.2 467.4 %reduce-scatter.8.cloned.1.call-start = ((), (), s32[]{:S(2)}) async-start(), calls=%async_computation.11 | async-start | bytes 5242880 | tf_op jit(solution)/shard_map/reduce_scatter | solution.py:998
  499.6 302.5 %reduce-scatter.6.cloned.1.call-start = ((), (), s32[]{:S(2)}) async-start(), calls=%async_computation.10 | async-start | bytes 5242880 | tf_op jit(solution)/shard_map/reduce_scatter | solution.py:998
  639.7 257.5 %reduce-scatter.10.cloned.1.call-start = ((), (), s32[]{:S(2)}) async-start(), calls=%async_computation.12 | async-start | bytes 5242880 | tf_op jit(solution)/shard_map/reduce_scatter | solution.py:998
  678.5 58.3 %collective-permute-start.97 = (bf16[64,2048]{1,0:T(8,128)(2,1)}, bf16[64,2048]{1,0:T(8,128)(2,1)}, u32[]{:S(2)}, u32[]{:S(2)}) collective-permute-start(bf16[64,2048]{1,0:T(8,128)(2,1)} %slice.1192), channel_id=1, source_target_pairs={{0,1},{1,0},{2,3},{3,2},{4,5},{5,4},{6,7},{7,6},{8,9},{9,8},{10,11... | collective-permute-start | bytes 786440 | tf_op jit(solution)/shard_map/ppermute | solution.py:360
  680.0 56.9 %collective-permute-start.96 = (bf16[64,2048]{1,0:T(8,128)(2,1)}, bf16[64,2048]{1,0:T(8,128)(2,1)}, u32[]{:S(2)}, u32[]{:S(2)}) collective-permute-start(bf16[64,2048]{1,0:T(8,128)(2,1)} %slice.1191), channel_id=1, source_target_pairs={{0,16},{16,0},{1,17},{17,1},{2,18},{18,2},{3,19},{19,3},{4,20},{20... | collective-permute-start | bytes 786440 | tf_op jit(solution)/shard_map/ppermute | solution.py:360
  685.9 118.6 %collective-permute-start.109 = (bf16[4,448,2048]{2,1,0:T(8,128)(2,1)}, bf16[4,448,2048]{2,1,0:T(8,128)(2,1)}, u32[]{:S(2)}, u32[]{:S(2)}) collective-permute-start(bf16[4,448,2048]{2,1,0:T(8,128)(2,1)} %get-tuple-element.599), channel_id=1, source_target_pairs={{0,8},{8,0},{1,9},{9,1},{2,10},{10,2},{3,11},{11,3},{4,12},{12,4},... | collective-permute-start | bytes 22020104 | tf_op jit(solution)/shard_map/ppermute | solution.py:360
  689.8 49.2 %collective-permute-start.99 = (bf16[64,2048]{1,0:T(8,128)(2,1)}, bf16[64,2048]{1,0:T(8,128)(2,1)S(1)}, u32[]{:S(2)}, u32[]{:S(2)}) collective-permute-start(bf16[64,2048]{1,0:T(8,128)(2,1)} %fusion.77), channel_id=1, source_target_pairs={{0,16},{16,0},{1,17},{17,1},{2,18},{18,2},{3,19},{19,3},{4,20},{20... | collective-permute-start | bytes 786440 | tf_op jit(solution)/shard_map/ppermute | solution.py:360
  738.9 49.4 %collective-permute-start.101 = (bf16[512,2048]{1,0:T(8,128)(2,1)S(1)}, bf16[512,2048]{1,0:T(8,128)(2,1)}, u32[]{:S(2)}, u32[]{:S(2)}) collective-permute-start(bf16[512,2048]{1,0:T(8,128)(2,1)S(1)} %constant_dynamic-update-slice_fusion.42.refs_0_), channel_id=1, source_target_pairs={{0,8},{8,0},{1,9},{9,1},{2,10},{10,2},{3,11},{11,3},{4,12},{12,4},... | collective-permute-start | bytes 6291464 | tf_op jit(solution)/shard_map/ppermute | solution.py:360
  783.4 232.0 %reduce-scatter.12.cloned.1.call-start = ((), (), s32[]{:S(2)}) async-start(), calls=%async_computation.13 | async-start | bytes 3932160 | tf_op jit(solution)/shard_map/reduce_scatter | solution.py:998
  787.1 75.4 %collective-permute-start.113 = (bf16[2,256,512]{2,1,0:T(8,128)(2,1)}, bf16[2,256,512]{2,1,0:T(8,128)(2,1)}, u32[]{:S(2)}, u32[]{:S(2)}) collective-permute-start(bf16[2,256,512]{2,1,0:T(8,128)(2,1)} %get-tuple-element.632), channel_id=1, source_target_pairs={{0,16},{16,0},{1,17},{17,1},{2,18},{18,2},{3,19},{19,3},{4,20},{20... | collective-permute-start | bytes 1572872 | tf_op jit(solution)/shard_map/ppermute | solution.py:360
  803.6 61.2 %collective-permute-start.100 = (bf16[2,256,512]{2,1,0:T(8,128)(2,1)S(1)}, bf16[2,256,512]{2,1,0:T(8,128)(2,1)S(1)}, u32[]{:S(2)}, u32[]{:S(2)}) collective-permute-start(bf16[2,256,512]{2,1,0:T(8,128)(2,1)S(1)} %get-tuple-element.618), channel_id=1, source_target_pairs={{0,16},{16,0},{1,17},{17,1},{2,18},{18,2},{3,19},{19,3},{4,20},{20... | collective-permute-start | bytes 1572872 | tf_op jit(solution)/shard_map/ppermute | solution.py:360
  818.1 50.5 %collective-permute-start.111 = (bf16[2,224,2048]{2,1,0:T(8,128)(2,1)}, bf16[2,224,2048]{2,1,0:T(8,128)(2,1)}, u32[]{:S(2)}, u32[]{:S(2)}) collective-permute-start(bf16[2,224,2048]{2,1,0:T(8,128)(2,1)} %pad_maximum_fusion.2), channel_id=1, source_target_pairs={{0,16},{16,0},{1,17},{17,1},{2,18},{18,2},{3,19},{19,3},{4,20},{20... | collective-permute-start | bytes 5505032 | tf_op jit(solution)/shard_map/ppermute | solution.py:360
  819.2 49.4 %collective-permute-start.112 = (bf16[2,224,2048]{2,1,0:T(8,128)(2,1)}, bf16[2,224,2048]{2,1,0:T(8,128)(2,1)}, u32[]{:S(2)}, u32[]{:S(2)}) collective-permute-start(bf16[2,224,2048]{2,1,0:T(8,128)(2,1)} %pad_maximum_fusion.3), channel_id=1, source_target_pairs={{0,1},{1,0},{2,3},{3,2},{4,5},{5,4},{6,7},{7,6},{8,9},{9,8},{10,11... | collective-permute-start | bytes 5505032 | tf_op jit(solution)/shard_map/ppermute | solution.py:360
  902.2 49.1 %collective-permute-start.120 = (bf16[4,1792,512]{2,1,0:T(8,128)(2,1)}, bf16[4,1792,512]{2,1,0:T(8,128)(2,1)}, u32[]{:S(2)}, u32[]{:S(2)}) collective-permute-start(bf16[4,1792,512]{2,1,0:T(8,128)(2,1)} %get-tuple-element.661), channel_id=1, source_target_pairs={{0,8},{8,0},{1,9},{9,1},{2,10},{10,2},{3,11},{11,3},{4,12},{12,4},... | collective-permute-start | bytes 22020104 | tf_op jit(solution)/shard_map/ppermute | solution.py:360
  947.4 109.9 %reduce-scatter.14.cloned.1.call-start = ((), (), s32[]{:S(2)}) async-start(), calls=%async_computation.14 | async-start | bytes 1310720 | tf_op jit(solution)/shard_map/reduce_scatter | solution.py:998
  (220 other events, 3890.7 us)
Sparse Core Ops, SparseCore 0:
  30.3 82.2 all-gather.4
  114.1 79.2 all-gather.8
  195.0 79.8 all-gather.10
  317.3 84.1 all-gather.6
  499.7 81.3 reduce-scatter.7
  639.8 81.5 reduce-scatter.5
  783.5 85.6 reduce-scatter.9
  932.4 69.2 reduce-scatter.11
  1004.1 27.5 reduce-scatter.13

commit v4 on v3

--- a/solution.py
+++ b/solution.py
@@ -104,7 +104,12 @@
         return carry
 
     lax.fori_loop(0, full // 4, wide_step, 0)
-    lax.fori_loop(full // 4 * 4, full, full_step, 0)
+
+    @pl.when(full % 4 >= 2)
+    def _():
+        step(full // 4 * 4, None, 2)
+
+    lax.fori_loop(full // 2 * 2, full, full_step, 0)
     lax.fori_loop(0, masked, mask_step, 0)
     for h in range(heads):
         total = tot[h : h + 1, :]
@@ -493,14 +498,14 @@
 
 def sum_steps(keep, send):
     (got,) = yield [(send, "c")]
-    sums = [halves(keep[k].astype(F32) + got[k].astype(F32)) for k in range(4)]
-    to_x = jnp.stack([sums[1][0], sums[3][0]]).astype(BF)
-    to_y = jnp.stack([sums[2][1], sums[3][1]]).astype(BF)
+    sums = [halves((keep[k].astype(F32) + got[k].astype(F32)).astype(BF)) for k in range(4)]
+    to_x = jnp.stack([sums[1][0], sums[3][0]])
+    to_y = jnp.stack([sums[2][1], sums[3][1]])
     by_x, by_y = yield [(to_x, "x"), (to_y, "y")]
-    over_y = (sums[2][0] + by_x[1].astype(F32)).astype(BF)
-    over_x = (sums[1][1] + by_y[1].astype(F32)).astype(BF)
-    former = sums[0][0] + by_x[0].astype(F32)
-    latter = sums[0][1] + by_y[0].astype(F32)
+    over_y = (sums[2][0].astype(F32) + by_x[1].astype(F32)).astype(BF)
+    over_x = (sums[1][1].astype(F32) + by_y[1].astype(F32)).astype(BF)
+    former = sums[0][0].astype(F32) + by_x[0].astype(F32)
+    latter = sums[0][1].astype(F32) + by_y[0].astype(F32)
     by_y, by_x = yield [(over_y, "y"), (over_x, "x")]
     return jnp.concatenate([former + by_y.astype(F32), latter + by_x.astype(F32)], 0)
 

time: 1090 us -> 1080 us (level)
  other arithmetic: 147 us -> 132 us
    add x10 -> x0, other arithmetic: 34 us -> none  [sum_steps(): sums = [halves(keep[k].astype(F32) + got[k].astype(F32)) for k in range(4)]]
    convert_element_type x20 -> x30, other arithmetic: 18.3 us -> 49.8 us  [the longest x10 33.9 us: sum_steps(): (keep[k].astype(F32) + got[k].astype(F32)).astype(BF)]
    unnamed x258 -> x278, local copies, waits for them, and re-layouts: 54.9 us -> 57.1 us
  transfers between devices with their start and end apart: 146 -> 146, of which waited for: 34 -> 33; matrix products, arithmetic and copies ran while one was open for 24% -> 23% of each run, Pallas kernels for 41% -> 42%
where the time goes in v4:
time: 1080 us; the launch traced here: 1070 us
  Pallas kernels  503 us (47%)
  waiting for transfers between devices  164 us (15%)
  local copies, waits for them, and re-layouts  134 us (12%)
  other arithmetic  132 us (12%)
  starting transfers between devices  118 us (11%)
  between operations  22.5 us (2%)
    ppermute x134, waiting for transfers between devices, flip(): return lax.ppermute(values, axis, [(0, 1), (1, 0)])  160 us
    ppermute x134, starting transfers between devices, flip(): return lax.ppermute(values, axis, [(0, 1), (1, 0)])  106 us
    pallas_call x2, Pallas kernels, attend_backward(): pl.pallas_call(functools.partial(backward_kernel, heads, 0 if final else...  87.8 us
    pallas_call x4, Pallas kernels, grad_product(): pl.pallas_call(functools.partial(grad_kernel, len(lefts), form, starts),...  74 us
    pallas_call x8, Pallas kernels, split_product(): pl.pallas_call(functools.partial(split_kernel, len(pairs), form, sub), gr...  68.1 us
    pallas_call x4, Pallas kernels, attend_forward(): pl.pallas_call(functools.partial(forward_kernel, heads, first), grid=(cou...  57.9 us
    unnamed x278, local copies, waits for them, and re-layouts  57.1 us
    pallas_call x4, Pallas kernels, unit_products(): pl.pallas_call(functools.partial(unit_kernel, len(pieces)), grid=(units /...  51.2 us
  transfers between devices with their start and end apart: 146, of which 33 were waited for; matrix products, arithmetic and copies ran while one was open for 23% of the time, Pallas kernels for 42%

profile of v4, /device:TPU:0, one launch (start us, length us, event | category | flops | bytes accessed | tf_op | source)
XLA Modules:
  0.0 1072.8 jit_solution(15937795274462495952)
XLA Ops:
  14.7 11.9 %collective-permute-done.2 = bf16[2,4,64,512]{3,2,0,1:T(8,128)(2,1)S(1)} collective-permute-done((bf16[2,4,64,512]{3,2,0,1:T(8,128)(2,1)S(1)}, bf16[2,4,64,512]{3,2,0,1:T(8,128)(2,1)S(1)}, u32[]{:S(2)}, u32[]{:S(2)}) %collective-permute-start.2) | collective-permute-done | bytes 524320 | tf_op jit(solution)/shard_map/ppermute | solution.py:365
  57.0 21.5 %collective-permute-done.refs_4_ = bf16[1792,512]{1,0:T(8,128)(2,1)} collective-permute-done((bf16[1792,512]{1,0:T(8,128)(2,1)S(1)}, bf16[1792,512]{1,0:T(8,128)(2,1)}, u32[]{:S(2)}, u32[]{:S(2)}) %collective-permute-start) | collective-permute-done | bytes 1835040 | tf_op jit(solution)/shard_map/ppermute | solution.py:365
  81.0 11.5 %collective-permute-done.4.refs_2_ = bf16[1792,512]{1,0:T(8,128)(2,1)} collective-permute-done((bf16[1792,512]{1,0:T(8,128)(2,1)S(1)}, bf16[1792,512]{1,0:T(8,128)(2,1)}, u32[]{:S(2)}, u32[]{:S(2)}) %collective-permute-start.4) | collective-permute-done | bytes 1835040 | tf_op jit(solution)/shard_map/ppermute | solution.py:365
  134.8 27.0 %shard_map.220 = (bf16[3584,2048]{1,0:T(8,128)(2,1)}, bf16[448,2048]{1,0:T(8,128)(2,1)}, bf16[768,3584]{1,0:T(8,128)(2,1)}, bf16[4,3584,64]{2,1,0:T(8,128)(2,1)}, bf16[4,3584,64]{2,1,0:T(8,128)(2,1)}) custom-call(s32[3]{0:T(128)} %pad_add_fusion.places, bf16[1792,512]{1,0:T(8,128)(2,1)} %refs_0_, bf16[1792,512]{1,0:T(8,128)(2,1)} %collective-permute-done.9.refs_1_, ...), custom_call_target="tpu_custom_call" | custom-call | flops 11318329344 | bytes 36700160 | tf_op jit(solution)/shard_map/pallas_call | solution.py:579
  162.2 14.6 %shard_map.221 = (bf16[256,768]{1,0:T(8,128)(2,1)}, f32[8,768]{1,0:T(8,128)}) custom-call(s32[13]{0:T(128)} %pad_add_fusion.1.info, bf16[768,3584]{1,0:T(8,128)(2,1)} %get-tuple-element.633.qkv, bf16[4,3584,64]{2,1,0:T(8,128)(2,1)} %get-tuple-element.373.knat), custom_call_target="tpu_custom_call" | custom-call | flops 12079595520 | bytes 16777216 | tf_op jit(solution)/shard_map/pallas_call | solution.py:122
  191.2 15.7 %shard_map.223 = (bf16[256,768]{1,0:T(8,128)(2,1)}, f32[8,768]{1,0:T(8,128)}) custom-call(s32[13]{0:T(128)} %pad_add_fusion.1.info, bf16[768,3584]{1,0:T(8,128)(2,1)} %get-tuple-element.633.qkv, bf16[4,3584,64]{2,1,0:T(8,128)(2,1)} %get-tuple-element.373.knat), custom_call_target="tpu_custom_call" | custom-call | flops 12079595520 | bytes 16777216 | tf_op jit(solution)/shard_map/pallas_call | solution.py:122
  250.2 16.8 %shard_map.227 = (bf16[256,1024]{1,0:T(8,128)(2,1)}, f32[8,1024]{1,0:T(8,128)}) custom-call(s32[13]{0:T(128)} %pad_add_fusion.1.info, bf16[768,3584]{1,0:T(8,128)(2,1)} %get-tuple-element.633.qkv, bf16[4,3584,64]{2,1,0:T(8,128)(2,1)} %get-tuple-element.373.knat), custom_call_target="tpu_custom_call" | custom-call | flops 16106127360 | bytes 16777216 | tf_op jit(solution)/shard_map/pallas_call | solution.py:122
  281.4 17.2 %shard_map.229 = (bf16[3584,2048]{1,0:T(8,128)(2,1)}, bf16[448,2048]{1,0:T(8,128)(2,1)}) custom-call(s32[3]{0:T(128)} %pad_add_fusion.places, bf16[1792,512]{1,0:T(8,128)(2,1)} %refs_0_.1, bf16[1792,512]{1,0:T(8,128)(2,1)} %collective-permute-done.8.refs_1_, bf16[1792,512]{1,0:T(8,128)(2,1)} %collective-permute-done.6.refs_2_, ...), custom_call_target="tpu_custom_call" | custom-call | flops 44040192 | bytes 36700160 | tf_op jit(solution)/shard_map/pallas_call | solution.py:579
  326.8 11.8 %shard_map.230 = (bf16[768,2048]{1,0:T(8,128)(2,1)}, bf16[768,1024]{1,0:T(8,128)(2,1)}, bf16[768,1024]{1,0:T(8,128)(2,1)}, bf16[768,1024]{1,0:T(8,128)(2,1)}) custom-call(bf16[384,2048]{1,0:T(8,128)(2,1)} %constant_dynamic-update-slice_fusion.4.refs_0_, bf16[384,2048]{1,0:T(8,128)(2,1)} %collective-permute-done.38.refs_1_, ...), custom_call_target="tpu_custom_call" | custom-call | flops 6442450944 | bytes 14680064 | tf_op jit(solution)/shard_map/pallas_call | solution.py:714
  363.4 11.4 %shard_map.231 = (bf16[768,2048]{1,0:T(8,128)(2,1)}, bf16[768,1024]{1,0:T(8,128)(2,1)}, bf16[768,1024]{1,0:T(8,128)(2,1)}, bf16[768,1024]{1,0:T(8,128)(2,1)}) custom-call(bf16[384,2048]{1,0:T(8,128)(2,1)} %copy-done.82, bf16[384,2048]{1,0:T(8,128)(2,1)} %collective-permute-done.46.refs_1_, bf16[1024,2048]{1,0:T(8,128)(2,1)} %all-gather.9.cloned.1.call-done.refs_2_.refs_1_, ...), custom_call_target="tpu_custom_call" | custom-call | flops 6442450944 | bytes 14680064 | tf_op jit(solution)/shard_map/pallas_call | solution.py:714
  407.2 14.0 %shard_map.232 = (bf16[1024,2048]{1,0:T(8,128)(2,1)}, bf16[1024,1024]{1,0:T(8,128)(2,1)}, bf16[1024,1024]{1,0:T(8,128)(2,1)}, bf16[1024,1024]{1,0:T(8,128)(2,1)}) custom-call(bf16[512,2048]{1,0:T(8,128)(2,1)} %constant_dynamic-update-slice_fusion.14.refs_0_, bf16[512,2048]{1,0:T(8,128)(2,1)} %collective-permute-done.56.refs_1_, ...), custom_call_target="tpu_custom_call" | custom-call | flops 8589934592 | bytes 16777216 | tf_op jit(solution)/shard_map/pallas_call | solution.py:714
  436.5 14.0 %shard_map.233 = (bf16[1024,2048]{1,0:T(8,128)(2,1)}, bf16[1024,1024]{1,0:T(8,128)(2,1)}, bf16[1024,1024]{1,0:T(8,128)(2,1)}, bf16[1024,1024]{1,0:T(8,128)(2,1)}) custom-call(bf16[512,2048]{1,0:T(8,128)(2,1)} %copy-done.80, bf16[512,2048]{1,0:T(8,128)(2,1)} %copy-done.107, bf16[1024,2048]{1,0:T(8,128)(2,1)} %all-gather.9.cloned.1.call-done.refs_2_.refs_1_, ...), custom_call_target="tpu_custom_call" | custom-call | flops 8589934592 | bytes 16777216 | tf_op jit(solution)/shard_map/pallas_call | solution.py:714
  450.4 21.5 %shard_map.234 = bf16[1024,2048]{1,0:T(8,128)(2,1)} custom-call(bf16[768,1024]{1,0:T(8,128)(2,1)} %get-tuple-element.585.refs_0_.refs_2_, bf16[768,1024]{1,0:T(8,128)(2,1)} %get-tuple-element.586.refs_1_.refs_3_, bf16[1024,1024]{1,0:T(8,128)(2,1)} %get-tuple-element.583.refs_2_.refs_0_, bf16[1024,1024]{1,0:T(8,128)(2,1)} %get-tuple-element.584.refs_3_.refs_1_, ...), custom_call_target="tpu_custom_call" | custom-call | flops 15032385536 | bytes 22020096 | tf_op jit(solution)/shard_map/pallas_call | solution.py:795
  543.4 13.4 %shard_map.240 = (bf16[4,128,2048]{2,1,0:T(8,128)(2,1)}, bf16[4,128,2048]{2,1,0:T(8,128)(2,1)}) custom-call(bf16[1024,1024]{1,0:T(8,128)(2,1)} %get-tuple-element.572.refs_0_.refs_2_, bf16[1024,2048]{1,0:T(8,128)(2,1)} %all-gather.9.cloned.1.call-done.refs_2_.refs_1_, bf16[1024,1024]{1,0:T(8,128)(2,1)} %get-tuple-element.616.refs_2_, ...), custom_call_target="tpu_custom_call" | custom-call | flops 8589934592 | bytes 16777216 | tf_op jit(solution)/shard_map/pallas_call | solution.py:637
  582.6 13.7 %shard_map.242 = (bf16[4,128,2048]{2,1,0:T(8,128)(2,1)}, bf16[4,128,2048]{2,1,0:T(8,128)(2,1)}) custom-call(bf16[1024,1024]{1,0:T(8,128)(2,1)} %get-tuple-element.573.refs_0_.refs_3_, bf16[1024,2048]{1,0:T(8,128)(2,1)} %all-gather.9.cloned.1.call-done.refs_2_.refs_1_, bf16[1024,1024]{1,0:T(8,128)(2,1)} %get-tuple-element.617.refs_2_.refs_3_, ...), custom_call_target="tpu_custom_call" | custom-call | flops 8589934592 | bytes 16777216 | tf_op jit(solution)/shard_map/pallas_call | solution.py:637
  613.0 21.6 %shard_map.244 = bf16[1024,2048]{1,0:T(8,128)(2,1)} custom-call(bf16[768,1024]{1,0:T(8,128)(2,1)} %get-tuple-element.570.refs_0_, bf16[768,1024]{1,0:T(8,128)(2,1)} %get-tuple-element.571.refs_0_.refs_1_, bf16[1024,1024]{1,0:T(8,128)(2,1)} %get-tuple-element.572.refs_0_.refs_2_, bf16[1024,1024]{1,0:T(8,128)(2,1)} %get-tuple-element.573.refs_0_.refs_3_, ...), custom_call_target="tpu_custom_call" | custom-call | flops 15032385536 | bytes 22020096 | tf_op jit(solution)/shard_map/pallas_call | solution.py:795
  650.5 21.5 %shard_map.245 = (bf16[4,448,2048]{2,1,0:T(8,128)(2,1)}, bf16[4,448,2048]{2,1,0:T(8,128)(2,1)}) custom-call(bf16[1024,1024]{1,0:T(8,128)(2,1)} %get-tuple-element.583.refs_2_.refs_0_, bf16[1024,1024]{1,0:T(8,128)(2,1)} %get-tuple-element.584.refs_3_.refs_1_, bf16[768,1024]{1,0:T(8,128)(2,1)} %get-tuple-element.585.refs_0_.refs_2_, ...), custom_call_target="tpu_custom_call" | custom-call | flops 15032385536 | bytes 22020096 | tf_op jit(solution)/shard_map/pallas_call | solution.py:668
  683.9 45.3 %shard_map.247 = (f32[256,3584]{1,0:T(8,128)}, f32[256,3584]{1,0:T(8,128)}, bf16[256,1536]{1,0:T(8,128)(2,1)}, f32[8,1536]{1,0:T(8,128)}) custom-call(s32[13]{0:T(128)} %pad_add_fusion.1.info, bf16[768,3584]{1,0:T(8,128)(2,1)} %get-tuple-element.633.qkv, bf16[4,3584,64]{2,1,0:T(8,128)(2,1)} %get-tuple-element.373.knat, ...), custom_call_target="tpu_custom_call" | custom-call | flops 45097156608 | bytes 33554432 | tf_op jit(solution)/shard_map/pallas_call | solution.py:293
  738.3 21.6 %shard_map.248 = bf16[1024,2048]{1,0:T(8,128)(2,1)} custom-call(bf16[768,1024]{1,0:T(8,128)(2,1)} %get-tuple-element.614.refs_2_.refs_0_, bf16[768,1024]{1,0:T(8,128)(2,1)} %get-tuple-element.615.refs_2_.refs_1_, bf16[1024,1024]{1,0:T(8,128)(2,1)} %get-tuple-element.616.refs_2_, bf16[1024,1024]{1,0:T(8,128)(2,1)} %get-tuple-element.617.refs_2_.refs_3_, ...), custom_call_target="tpu_custom_call" | custom-call | flops 15032385536 | bytes 22020096 | tf_op jit(solution)/shard_map/pallas_call | solution.py:795
  811.9 42.5 %shard_map.251 = (bf16[768,3584]{1,0:T(8,128)(2,1)}, f32[8,3584]{1,0:T(8,128)}) custom-call(s32[13]{0:T(128)} %pad_add_fusion.1.info, bf16[768,3584]{1,0:T(8,128)(2,1)} %get-tuple-element.633.qkv, bf16[4,3584,64]{2,1,0:T(8,128)(2,1)} %get-tuple-element.373.knat, bf16[4,3584,64]{2,1,0:T(8,128)(2,1)} %get-tuple-element.601.vnat, ...), custom_call_target="tpu_custom_call" | custom-call | flops 45097156608 | bytes 33554432 | tf_op jit(solution)/shard_map/pallas_call | solution.py:293
  868.6 20.9 %shard_map.252 = (bf16[4,1792,512]{2,1,0:T(8,128)(2,1)}, bf16[4,1792,512]{2,1,0:T(8,128)(2,1)}) custom-call(s32[3]{0:T(128)} %pad_add_fusion.places, bf16[768,3584]{1,0:T(8,128)(2,1)} %get-tuple-element.663.d_qkv, bf16[768,2048]{1,0:T(8,128)(2,1)} %bitcast.385), custom_call_target="tpu_custom_call" | custom-call | flops 11274289152 | bytes 14680064 | tf_op jit(solution)/shard_map/pallas_call | solution.py:855
  908.8 17.1 %shard_map.253 = (bf16[768,2048]{1,0:T(8,128)(2,1)}, f32[8,2048]{1,0:T(8,128)}) custom-call(bf16[768,3584]{1,0:T(8,128)(2,1)} %get-tuple-element.663.d_qkv, bf16[3584,2048]{1,0:T(8,128)(2,1)} %get-tuple-element.369.low, bf16[768,2048]{1,0:T(8,128)(2,1)} %bitcast.386), custom_call_target="tpu_custom_call" | custom-call | flops 11274289152 | bytes 20185088 | tf_op jit(solution)/shard_map/pallas_call | solution.py:817
  988.5 14.5 %collective-permute-done.122 = bf16[2,896,512]{2,1,0:T(8,128)(2,1)} collective-permute-done((bf16[2,896,512]{2,1,0:T(8,128)(2,1)}, bf16[2,896,512]{2,1,0:T(8,128)(2,1)}, u32[]{:S(2)}, u32[]{:S(2)}) %collective-permute-start.122) | collective-permute-done | bytes 1835040 | tf_op jit(solution)/shard_map/ppermute | solution.py:365
  1027.5 17.2 %collective-permute-done.130 = f32[4099]{0:T(1024)S(1)} collective-permute-done((f32[4099]{0:T(1024)S(1)}, f32[4099]{0:T(1024)S(1)}, u32[]{:S(2)}, u32[]{:S(2)}) %collective-permute-start.130) | collective-permute-done | bytes 16428 | tf_op jit(solution)/shard_map/ppermute | solution.py:365
  (883 shorter events, 592.2 us)
Async XLA Ops:
  7.2 123.6 %all-gather.5.cloned.1.call-start = ((), (), s32[]{:S(2)}) async-start(), calls=%async_computation.6 | async-start | bytes 5242880 | tf_op jit(solution)/shard_map/all_gather | solution.py:949
  30.1 296.6 %all-gather.9.cloned.1.call-start = ((), (), s32[]{:S(2)}) async-start(), calls=%async_computation.8 | async-start | bytes 5242880 | tf_op jit(solution)/shard_map/all_gather | solution.py:929
  51.2 76.3 %collective-permute-start.9 = (bf16[1792,512]{1,0:T(8,128)(2,1)S(1)}, bf16[1792,512]{1,0:T(8,128)(2,1)}, u32[]{:S(2)}, u32[]{:S(2)}) collective-permute-start(bf16[1792,512]{1,0:T(8,128)(2,1)S(1)} %copy-done.11), channel_id=1, source_target_pairs={{0,8},{8,0},{1,9},{9,1},{2,10},{10,2},{3,11},{11,3},{4,12},{12,4},... | collective-permute-start | bytes 5505032 | tf_op jit(solution)/shard_map/ppermute | solution.py:365
  56.7 270.1 %all-gather.11.cloned.1.call-start = ((), (), s32[]{:S(2)}) async-start(), calls=%async_computation.9 | async-start | bytes 5242880 | tf_op jit(solution)/shard_map/all_gather | solution.py:929
  127.5 56.3 %collective-permute-start.8 = (bf16[1792,512]{1,0:T(8,128)(2,1)}, bf16[1792,512]{1,0:T(8,128)(2,1)}, u32[]{:S(2)}, u32[]{:S(2)}) collective-permute-start(bf16[1792,512]{1,0:T(8,128)(2,1)} %refs_0_.1), channel_id=1, source_target_pairs={{0,8},{8,0},{1,9},{9,1},{2,10},{10,2},{3,11},{11,3},{4,12},{12,4},... | collective-permute-start | bytes 5505032 | tf_op jit(solution)/shard_map/ppermute | solution.py:365
  127.5 56.2 %collective-permute-start.7 = (bf16[1792,512]{1,0:T(8,128)(2,1)}, bf16[1792,512]{1,0:T(8,128)(2,1)S(1)}, u32[]{:S(2)}, u32[]{:S(2)}) collective-permute-start(bf16[1792,512]{1,0:T(8,128)(2,1)} %refs_0_.1), channel_id=1, source_target_pairs={{0,1},{1,0},{2,3},{3,2},{4,5},{5,4},{6,7},{7,6},{8,9},{9,8},{10,11... | collective-permute-start | bytes 5505032 | tf_op jit(solution)/shard_map/ppermute | solution.py:365
  129.3 54.5 %collective-permute-start.6 = (bf16[1792,512]{1,0:T(8,128)(2,1)}, bf16[1792,512]{1,0:T(8,128)(2,1)}, u32[]{:S(2)}, u32[]{:S(2)}) collective-permute-start(bf16[1792,512]{1,0:T(8,128)(2,1)} %refs_0_.1), channel_id=1, source_target_pairs={{0,16},{16,0},{1,17},{17,1},{2,18},{18,2},{3,19},{19,3},{4,20},{20... | collective-permute-start | bytes 5505032 | tf_op jit(solution)/shard_map/ppermute | solution.py:365
  190.6 216.6 %all-gather.7.cloned.1.call-start = ((), (), s32[]{:S(2)}) async-start(), calls=%async_computation.7 | async-start | bytes 5242880 | tf_op jit(solution)/shard_map/all_gather | solution.py:929
  238.4 64.1 %collective-permute-start.41 = (bf16[4,128,2048]{2,1,0:T(8,128)(2,1)}, bf16[4,128,2048]{2,1,0:T(8,128)(2,1)S(1)}, u32[]{:S(2)}, u32[]{:S(2)}) collective-permute-start(bf16[4,128,2048]{2,1,0:T(8,128)(2,1)} %get-tuple-element.412), channel_id=1, source_target_pairs={{0,8},{8,0},{1,9},{9,1},{2,10},{10,2},{3,11},{11,3},{4,12},{12,4},... | collective-permute-start | bytes 6291464 | tf_op jit(solution)/shard_map/ppermute | solution.py:365
  317.1 460.3 %reduce-scatter.8.cloned.1.call-start = ((), (), s32[]{:S(2)}) async-start(), calls=%async_computation.11 | async-start | bytes 5242880 | tf_op jit(solution)/shard_map/reduce_scatter | solution.py:1003
  496.4 299.0 %reduce-scatter.6.cloned.1.call-start = ((), (), s32[]{:S(2)}) async-start(), calls=%async_computation.10 | async-start | bytes 5242880 | tf_op jit(solution)/shard_map/reduce_scatter | solution.py:1003
  637.9 251.7 %reduce-scatter.10.cloned.1.call-start = ((), (), s32[]{:S(2)}) async-start(), calls=%async_computation.12 | async-start | bytes 5242880 | tf_op jit(solution)/shard_map/reduce_scatter | solution.py:1003
  672.8 56.5 %collective-permute-start.97 = (bf16[64,2048]{1,0:T(8,128)(2,1)}, bf16[64,2048]{1,0:T(8,128)(2,1)}, u32[]{:S(2)}, u32[]{:S(2)}) collective-permute-start(bf16[64,2048]{1,0:T(8,128)(2,1)} %slice.1152), channel_id=1, source_target_pairs={{0,1},{1,0},{2,3},{3,2},{4,5},{5,4},{6,7},{7,6},{8,9},{9,8},{10,11... | collective-permute-start | bytes 786440 | tf_op jit(solution)/shard_map/ppermute | solution.py:365
  674.4 54.9 %collective-permute-start.96 = (bf16[64,2048]{1,0:T(8,128)(2,1)S(1)}, bf16[64,2048]{1,0:T(8,128)(2,1)}, u32[]{:S(2)}, u32[]{:S(2)}) collective-permute-start(bf16[64,2048]{1,0:T(8,128)(2,1)S(1)} %slice.1151), channel_id=1, source_target_pairs={{0,16},{16,0},{1,17},{17,1},{2,18},{18,2},{3,19},{19,3},{4,20},{20... | collective-permute-start | bytes 786440 | tf_op jit(solution)/shard_map/ppermute | solution.py:365
  681.1 116.2 %collective-permute-start.109 = (bf16[4,448,2048]{2,1,0:T(8,128)(2,1)}, bf16[4,448,2048]{2,1,0:T(8,128)(2,1)}, u32[]{:S(2)}, u32[]{:S(2)}) collective-permute-start(bf16[4,448,2048]{2,1,0:T(8,128)(2,1)} %get-tuple-element.599), channel_id=1, source_target_pairs={{0,8},{8,0},{1,9},{9,1},{2,10},{10,2},{3,11},{11,3},{4,12},{12,4},... | collective-permute-start | bytes 22020104 | tf_op jit(solution)/shard_map/ppermute | solution.py:365
  683.3 48.2 %collective-permute-start.99 = (bf16[64,2048]{1,0:T(8,128)(2,1)S(1)}, bf16[64,2048]{1,0:T(8,128)(2,1)S(1)}, u32[]{:S(2)}, u32[]{:S(2)}) collective-permute-start(bf16[64,2048]{1,0:T(8,128)(2,1)S(1)} %fusion.17), channel_id=1, source_target_pairs={{0,16},{16,0},{1,17},{17,1},{2,18},{18,2},{3,19},{19,3},{4,20},{20... | collective-permute-start | bytes 786440 | tf_op jit(solution)/shard_map/ppermute | solution.py:365
  683.5 48.0 %collective-permute-start.98 = (bf16[64,2048]{1,0:T(8,128)(2,1)S(1)}, bf16[64,2048]{1,0:T(8,128)(2,1)S(1)}, u32[]{:S(2)}, u32[]{:S(2)}) collective-permute-start(bf16[64,2048]{1,0:T(8,128)(2,1)S(1)} %fusion.16), channel_id=1, source_target_pairs={{0,1},{1,0},{2,3},{3,2},{4,5},{5,4},{6,7},{7,6},{8,9},{9,8},{10,11... | collective-permute-start | bytes 786440 | tf_op jit(solution)/shard_map/ppermute | solution.py:365
  731.3 50.3 %collective-permute-start.101 = (bf16[512,2048]{1,0:T(8,128)(2,1)S(1)}, bf16[512,2048]{1,0:T(8,128)(2,1)}, u32[]{:S(2)}, u32[]{:S(2)}) collective-permute-start(bf16[512,2048]{1,0:T(8,128)(2,1)S(1)} %constant_dynamic-update-slice_fusion.42.refs_0_), channel_id=1, source_target_pairs={{0,8},{8,0},{1,9},{9,1},{2,10},{10,2},{3,11},{11,3},{4,12},{12,4},... | collective-permute-start | bytes 6291464 | tf_op jit(solution)/shard_map/ppermute | solution.py:365
  776.3 232.2 %reduce-scatter.12.cloned.1.call-start = ((), (), s32[]{:S(2)}) async-start(), calls=%async_computation.13 | async-start | bytes 3932160 | tf_op jit(solution)/shard_map/reduce_scatter | solution.py:1003
  779.9 74.5 %collective-permute-start.113 = (bf16[2,256,512]{2,1,0:T(8,128)(2,1)}, bf16[2,256,512]{2,1,0:T(8,128)(2,1)}, u32[]{:S(2)}, u32[]{:S(2)}) collective-permute-start(bf16[2,256,512]{2,1,0:T(8,128)(2,1)} %get-tuple-element.632), channel_id=1, source_target_pairs={{0,16},{16,0},{1,17},{17,1},{2,18},{18,2},{3,19},{19,3},{4,20},{20... | collective-permute-start | bytes 1572872 | tf_op jit(solution)/shard_map/ppermute | solution.py:365
  796.8 60.1 %collective-permute-start.100 = (bf16[2,256,512]{2,1,0:T(8,128)(2,1)S(1)}, bf16[2,256,512]{2,1,0:T(8,128)(2,1)S(1)}, u32[]{:S(2)}, u32[]{:S(2)}) collective-permute-start(bf16[2,256,512]{2,1,0:T(8,128)(2,1)S(1)} %get-tuple-element.618), channel_id=1, source_target_pairs={{0,16},{16,0},{1,17},{17,1},{2,18},{18,2},{3,19},{19,3},{4,20},{20... | collective-permute-start | bytes 1572872 | tf_op jit(solution)/shard_map/ppermute | solution.py:365
  809.8 51.0 %collective-permute-start.111 = (bf16[2,224,2048]{2,1,0:T(8,128)(2,1)}, bf16[2,224,2048]{2,1,0:T(8,128)(2,1)}, u32[]{:S(2)}, u32[]{:S(2)}) collective-permute-start(bf16[2,224,2048]{2,1,0:T(8,128)(2,1)} %pad_maximum_fusion.2), channel_id=1, source_target_pairs={{0,16},{16,0},{1,17},{17,1},{2,18},{18,2},{3,19},{19,3},{4,20},{20... | collective-permute-start | bytes 5505032 | tf_op jit(solution)/shard_map/ppermute | solution.py:365
  811.4 49.4 %collective-permute-start.112 = (bf16[2,224,2048]{2,1,0:T(8,128)(2,1)}, bf16[2,224,2048]{2,1,0:T(8,128)(2,1)}, u32[]{:S(2)}, u32[]{:S(2)}) collective-permute-start(bf16[2,224,2048]{2,1,0:T(8,128)(2,1)} %pad_maximum_fusion.3), channel_id=1, source_target_pairs={{0,1},{1,0},{2,3},{3,2},{4,5},{5,4},{6,7},{7,6},{8,9},{9,8},{10,11... | collective-permute-start | bytes 5505032 | tf_op jit(solution)/shard_map/ppermute | solution.py:365
  940.7 104.0 %reduce-scatter.14.cloned.1.call-start = ((), (), s32[]{:S(2)}) async-start(), calls=%async_computation.14 | async-start | bytes 1310720 | tf_op jit(solution)/shard_map/reduce_scatter | solution.py:1003
  (230 other events, 3990.7 us)
Sparse Core Ops, SparseCore 0:
  30.3 82.2 all-gather.4
  114.1 79.2 all-gather.8
  195.0 79.2 all-gather.10
  317.2 81.2 all-gather.6
  496.5 78.9 reduce-scatter.7
  638.0 79.0 reduce-scatter.5
  776.4 79.9 reduce-scatter.9
  926.2 62.8 reduce-scatter.11
  991.4 27.5 reduce-scatter.13

commit v5 on v4

--- a/solution.py
+++ b/solution.py
@@ -497,17 +497,27 @@
 
 
 def sum_steps(keep, send):
+    shape = (4, 2, keep.shape[1] // 2, keep.shape[2])
+
+    def pair(*values):
+        first, second = (v.reshape(shape) for v in values)
+        return lambda *at: first[at].astype(F32) + second[at].astype(F32)
+
     (got,) = yield [(send, "c")]
-    sums = [halves((keep[k].astype(F32) + got[k].astype(F32)).astype(BF)) for k in range(4)]
-    to_x = jnp.stack([sums[1][0], sums[3][0]])
-    to_y = jnp.stack([sums[2][1], sums[3][1]])
+    part = pair(keep, got)
+    to_x = part(slice(1, 4, 2), 0).astype(BF)
+    to_y = part(slice(2, 4), 1).astype(BF)
     by_x, by_y = yield [(to_x, "x"), (to_y, "y")]
-    over_y = (sums[2][0].astype(F32) + by_x[1].astype(F32)).astype(BF)
-    over_x = (sums[1][1].astype(F32) + by_y[1].astype(F32)).astype(BF)
-    former = sums[0][0].astype(F32) + by_x[0].astype(F32)
-    latter = sums[0][1].astype(F32) + by_y[0].astype(F32)
-    by_y, by_x = yield [(over_y, "y"), (over_x, "x")]
-    return jnp.concatenate([former + by_y.astype(F32), latter + by_x.astype(F32)], 0)
+    keep, got = after((keep, got), by_x, by_y)
+    part = pair(keep, got)
+    over_y = (part(2, 0) + by_x[1].astype(F32)).astype(BF)
+    over_x = (part(1, 1) + by_y[1].astype(F32)).astype(BF)
+    last_y, last_x = yield [(over_y, "y"), (over_x, "x")]
+    keep, got = after((keep, got), last_y, last_x)
+    part = pair(keep, got)
+    former = part(0, 0) + by_x[0].astype(F32) + last_y.astype(F32)
+    latter = part(0, 1) + by_y[0].astype(F32) + last_x.astype(F32)
+    return jnp.concatenate([former, latter], 0)
 
 
 def norm_kernel(mode, heads, places, *refs):
@@ -1197,13 +1207,16 @@
         )
         turned = lines.wanted["last"][1][0][0]
         sums = outcome(after(layer_out, out_grad), share[0])
-        lines.start("sums", summed(after(sums, turned), ("c", "z1", "z2", "x", "y")))
+        lines.start("sums", summed(sums, ("c", "z1", "z2", "x", "y")))
+        for _ in range(3):
+            tick(None, "sums")
         tick(None, "last")
-        for _ in range(5):
+        lines.last = [lines.results["last"]]
+        for _ in range(2):
             tick(None, "sums")
         d_one, inner, sums = (lines.results[n] for n in ("last", "inner", "sums"))
-        join_sum, up_home = after((join_sum, lines.results["up"]), turned)
-        lines.results["up"] = up_home
+        join_sum, out_sum = after((join_sum, total(out_grad)), d_one)
+        lines.results["up"] = after(lines.results["up"], turned)
         lines.results["gate"], lines.results["down"], attended, layer_pieces, inner = after(
             (lines.results["gate"], lines.results["down"], attended, layer_pieces, inner), out_grad
         )
@@ -1264,7 +1277,7 @@
         part = part.reshape(heads // 4, 3, HD, depth).transpose(1, 0, 2, 3)
         part = spread(columns_of(part.reshape(3, heads // 4 * HD, depth), 4, width))
         part = part.transpose(1, 0, 2, 3).reshape(3, head_width, width)
-        out_part = spread(columns_of(total(out_grad), 4, width)).reshape(1, head_width, width)
+        out_part = spread(columns_of(out_sum if quick else total(out_grad), 4, width)).reshape(1, head_width, width)
         part = jnp.concatenate([part, out_part], 0)
     else:
         part = jnp.concatenate(

time: 1080 us -> 1070 us (level)
  local copies, waits for them, and re-layouts: 134 us -> 120 us
    another operation x20 -> x0, other arithmetic: 13.5 us -> none  [the longest x10 7 us: sum_steps(): to_x = jnp.stack([sums[1][0], sums[3][0]])]
    add x10, other arithmetic: 10.8 us -> 22.8 us  [sum_steps(): former = part(0, 0) + by_x[0].astype(F32) + last_y.astype(F32)]
    unnamed x278 -> x226, local copies, waits for them, and re-layouts: 57.1 us -> 50.5 us
    convert_element_type x30 -> x20, other arithmetic: 49.8 us -> 52.1 us  [the longest x10 30 us: sum_steps(): to_y = part(slice(2, 4), 1).astype(BF)]
  transfers between devices with their start and end apart: 146 -> 146, of which waited for: 33 -> 31; matrix products, arithmetic and copies ran while one was open for 23% -> 22% of each run, Pallas kernels for 42% -> 42%
where the time goes in v5:
time: 1070 us; the launch traced here: 1060 us
  Pallas kernels  500 us (47%)
  waiting for transfers between devices  161 us (15%)
  other arithmetic  132 us (12%)
  starting transfers between devices  124 us (12%)
  local copies, waits for them, and re-layouts  120 us (11%)
  between operations  21.9 us (2%)
    ppermute x134, waiting for transfers between devices, flip(): return lax.ppermute(values, axis, [(0, 1), (1, 0)])  158 us
    ppermute x134, starting transfers between devices, flip(): return lax.ppermute(values, axis, [(0, 1), (1, 0)])  107 us
    pallas_call x2, Pallas kernels, attend_backward(): pl.pallas_call(functools.partial(backward_kernel, heads, 0 if final else...  87.1 us
    pallas_call x4, Pallas kernels, grad_product(): pl.pallas_call(functools.partial(grad_kernel, len(lefts), form, starts),...  74.2 us
    pallas_call x8, Pallas kernels, split_product(): pl.pallas_call(functools.partial(split_kernel, len(pairs), form, sub), gr...  67.7 us
    pallas_call x4, Pallas kernels, attend_forward(): pl.pallas_call(functools.partial(forward_kernel, heads, first), grid=(cou...  57 us
    pallas_call x4, Pallas kernels, unit_products(): pl.pallas_call(functools.partial(unit_kernel, len(pieces)), grid=(units /...  50.8 us
    unnamed x226, local copies, waits for them, and re-layouts  50.5 us
  transfers between devices with their start and end apart: 146, of which 31 were waited for; matrix products, arithmetic and copies ran while one was open for 22% of the time, Pallas kernels for 42%

profile of v5, /device:TPU:0, one launch (start us, length us, event | category | flops | bytes accessed | tf_op | source)
XLA Modules:
  0.0 1059.4 jit_solution(11287297347469966510)
XLA Ops:
  14.7 11.9 %collective-permute-done.2 = bf16[2,4,64,512]{3,2,0,1:T(8,128)(2,1)S(1)} collective-permute-done((bf16[2,4,64,512]{3,2,0,1:T(8,128)(2,1)S(1)}, bf16[2,4,64,512]{3,2,0,1:T(8,128)(2,1)S(1)}, u32[]{:S(2)}, u32[]{:S(2)}) %collective-permute-start.2) | collective-permute-done | bytes 524320 | tf_op jit(solution)/shard_map/ppermute | solution.py:365
  57.0 21.6 %collective-permute-done.refs_4_ = bf16[1792,512]{1,0:T(8,128)(2,1)} collective-permute-done((bf16[1792,512]{1,0:T(8,128)(2,1)S(1)}, bf16[1792,512]{1,0:T(8,128)(2,1)}, u32[]{:S(2)}, u32[]{:S(2)}) %collective-permute-start) | collective-permute-done | bytes 1835040 | tf_op jit(solution)/shard_map/ppermute | solution.py:365
  81.0 11.5 %collective-permute-done.4.refs_2_ = bf16[1792,512]{1,0:T(8,128)(2,1)} collective-permute-done((bf16[1792,512]{1,0:T(8,128)(2,1)S(1)}, bf16[1792,512]{1,0:T(8,128)(2,1)}, u32[]{:S(2)}, u32[]{:S(2)}) %collective-permute-start.4) | collective-permute-done | bytes 1835040 | tf_op jit(solution)/shard_map/ppermute | solution.py:365
  134.8 27.0 %shard_map.220 = (bf16[3584,2048]{1,0:T(8,128)(2,1)}, bf16[448,2048]{1,0:T(8,128)(2,1)}, bf16[768,3584]{1,0:T(8,128)(2,1)}, bf16[4,3584,64]{2,1,0:T(8,128)(2,1)}, bf16[4,3584,64]{2,1,0:T(8,128)(2,1)}) custom-call(s32[3]{0:T(128)} %pad_add_fusion.places, bf16[1792,512]{1,0:T(8,128)(2,1)} %refs_0_, bf16[1792,512]{1,0:T(8,128)(2,1)} %collective-permute-done.9.refs_1_, ...), custom_call_target="tpu_custom_call" | custom-call | flops 11318329344 | bytes 36700160 | tf_op jit(solution)/shard_map/pallas_call | solution.py:589
  162.1 14.6 %shard_map.221 = (bf16[256,768]{1,0:T(8,128)(2,1)}, f32[8,768]{1,0:T(8,128)}) custom-call(s32[13]{0:T(128)} %pad_add_fusion.1.info, bf16[768,3584]{1,0:T(8,128)(2,1)} %get-tuple-element.705.qkv, bf16[4,3584,64]{2,1,0:T(8,128)(2,1)} %get-tuple-element.413.knat), custom_call_target="tpu_custom_call" | custom-call | flops 12079595520 | bytes 16777216 | tf_op jit(solution)/shard_map/pallas_call | solution.py:122
  190.9 15.1 %shard_map.223 = (bf16[256,768]{1,0:T(8,128)(2,1)}, f32[8,768]{1,0:T(8,128)}) custom-call(s32[13]{0:T(128)} %pad_add_fusion.1.info, bf16[768,3584]{1,0:T(8,128)(2,1)} %get-tuple-element.705.qkv, bf16[4,3584,64]{2,1,0:T(8,128)(2,1)} %get-tuple-element.413.knat), custom_call_target="tpu_custom_call" | custom-call | flops 12079595520 | bytes 16777216 | tf_op jit(solution)/shard_map/pallas_call | solution.py:122
  244.9 16.6 %shard_map.227 = (bf16[256,1024]{1,0:T(8,128)(2,1)}, f32[8,1024]{1,0:T(8,128)}) custom-call(s32[13]{0:T(128)} %pad_add_fusion.1.info, bf16[768,3584]{1,0:T(8,128)(2,1)} %get-tuple-element.705.qkv, bf16[4,3584,64]{2,1,0:T(8,128)(2,1)} %get-tuple-element.413.knat), custom_call_target="tpu_custom_call" | custom-call | flops 16106127360 | bytes 16777216 | tf_op jit(solution)/shard_map/pallas_call | solution.py:122
  276.7 17.2 %shard_map.229 = (bf16[3584,2048]{1,0:T(8,128)(2,1)}, bf16[448,2048]{1,0:T(8,128)(2,1)}) custom-call(s32[3]{0:T(128)} %pad_add_fusion.places, bf16[1792,512]{1,0:T(8,128)(2,1)} %refs_0_.1, bf16[1792,512]{1,0:T(8,128)(2,1)} %collective-permute-done.8.refs_1_, bf16[1792,512]{1,0:T(8,128)(2,1)} %collective-permute-done.6.refs_2_, ...), custom_call_target="tpu_custom_call" | custom-call | flops 44040192 | bytes 36700160 | tf_op jit(solution)/shard_map/pallas_call | solution.py:589
  316.6 11.5 %shard_map.230 = (bf16[768,2048]{1,0:T(8,128)(2,1)}, bf16[768,1024]{1,0:T(8,128)(2,1)}, bf16[768,1024]{1,0:T(8,128)(2,1)}, bf16[768,1024]{1,0:T(8,128)(2,1)}) custom-call(bf16[384,2048]{1,0:T(8,128)(2,1)} %constant_dynamic-update-slice_fusion.4.refs_0_, bf16[384,2048]{1,0:T(8,128)(2,1)} %collective-permute-done.38.refs_1_, ...), custom_call_target="tpu_custom_call" | custom-call | flops 6442450944 | bytes 14680064 | tf_op jit(solution)/shard_map/pallas_call | solution.py:724
  359.1 11.3 %shard_map.231 = (bf16[768,2048]{1,0:T(8,128)(2,1)}, bf16[768,1024]{1,0:T(8,128)(2,1)}, bf16[768,1024]{1,0:T(8,128)(2,1)}, bf16[768,1024]{1,0:T(8,128)(2,1)}) custom-call(bf16[384,2048]{1,0:T(8,128)(2,1)} %constant_dynamic-update-slice_fusion.9.refs_0_, bf16[384,2048]{1,0:T(8,128)(2,1)} %collective-permute-done.46.refs_1_, ...), custom_call_target="tpu_custom_call" | custom-call | flops 6442450944 | bytes 14680064 | tf_op jit(solution)/shard_map/pallas_call | solution.py:724
  405.6 14.0 %shard_map.232 = (bf16[1024,2048]{1,0:T(8,128)(2,1)}, bf16[1024,1024]{1,0:T(8,128)(2,1)}, bf16[1024,1024]{1,0:T(8,128)(2,1)}, bf16[1024,1024]{1,0:T(8,128)(2,1)}) custom-call(bf16[512,2048]{1,0:T(8,128)(2,1)} %constant_dynamic-update-slice_fusion.14.refs_0_, bf16[512,2048]{1,0:T(8,128)(2,1)} %collective-permute-done.56.refs_1_, ...), custom_call_target="tpu_custom_call" | custom-call | flops 8589934592 | bytes 16777216 | tf_op jit(solution)/shard_map/pallas_call | solution.py:724
  434.8 14.0 %shard_map.233 = (bf16[1024,2048]{1,0:T(8,128)(2,1)}, bf16[1024,1024]{1,0:T(8,128)(2,1)}, bf16[1024,1024]{1,0:T(8,128)(2,1)}, bf16[1024,1024]{1,0:T(8,128)(2,1)}) custom-call(bf16[512,2048]{1,0:T(8,128)(2,1)} %copy-done.56, bf16[512,2048]{1,0:T(8,128)(2,1)} %copy-done.81, bf16[1024,2048]{1,0:T(8,128)(2,1)} %all-gather.9.cloned.1.call-done.refs_2_.refs_1_, ...), custom_call_target="tpu_custom_call" | custom-call | flops 8589934592 | bytes 16777216 | tf_op jit(solution)/shard_map/pallas_call | solution.py:724
  448.8 21.7 %shard_map.234 = bf16[1024,2048]{1,0:T(8,128)(2,1)} custom-call(bf16[768,1024]{1,0:T(8,128)(2,1)} %get-tuple-element.653.refs_0_.refs_2_, bf16[768,1024]{1,0:T(8,128)(2,1)} %get-tuple-element.654.refs_1_.refs_3_, bf16[1024,1024]{1,0:T(8,128)(2,1)} %get-tuple-element.651.refs_2_.refs_0_, bf16[1024,1024]{1,0:T(8,128)(2,1)} %get-tuple-element.652.refs_3_.refs_1_, ...), custom_call_target="tpu_custom_call" | custom-call | flops 15032385536 | bytes 22020096 | tf_op jit(solution)/shard_map/pallas_call | solution.py:805
  479.4 10.8 %shard_map.236 = (bf16[4,96,2048]{2,1,0:T(8,128)(2,1)}, bf16[4,96,2048]{2,1,0:T(8,128)(2,1)}) custom-call(bf16[768,1024]{1,0:T(8,128)(2,1)} %get-tuple-element.636.refs_0_, bf16[1024,2048]{1,0:T(8,128)(2,1)} %all-gather.9.cloned.1.call-done.refs_2_.refs_1_, bf16[768,1024]{1,0:T(8,128)(2,1)} %get-tuple-element.686.refs_2_.refs_0_, ...), custom_call_target="tpu_custom_call" | custom-call | flops 6442450944 | bytes 14680064 | tf_op jit(solution)/shard_map/pallas_call | solution.py:647
  542.0 13.2 %shard_map.240 = (bf16[4,128,2048]{2,1,0:T(8,128)(2,1)}, bf16[4,128,2048]{2,1,0:T(8,128)(2,1)}) custom-call(bf16[1024,1024]{1,0:T(8,128)(2,1)} %get-tuple-element.638.refs_0_.refs_2_, bf16[1024,2048]{1,0:T(8,128)(2,1)} %all-gather.9.cloned.1.call-done.refs_2_.refs_1_, bf16[1024,1024]{1,0:T(8,128)(2,1)} %get-tuple-element.688.refs_2_, ...), custom_call_target="tpu_custom_call" | custom-call | flops 8589934592 | bytes 16777216 | tf_op jit(solution)/shard_map/pallas_call | solution.py:647
  583.8 13.4 %shard_map.242 = (bf16[4,128,2048]{2,1,0:T(8,128)(2,1)}, bf16[4,128,2048]{2,1,0:T(8,128)(2,1)}) custom-call(bf16[1024,1024]{1,0:T(8,128)(2,1)} %get-tuple-element.639.refs_0_.refs_3_, bf16[1024,2048]{1,0:T(8,128)(2,1)} %all-gather.9.cloned.1.call-done.refs_2_.refs_1_, bf16[1024,1024]{1,0:T(8,128)(2,1)} %get-tuple-element.689.refs_2_.refs_3_, ...), custom_call_target="tpu_custom_call" | custom-call | flops 8589934592 | bytes 16777216 | tf_op jit(solution)/shard_map/pallas_call | solution.py:647
  611.6 21.6 %shard_map.244 = bf16[1024,2048]{1,0:T(8,128)(2,1)} custom-call(bf16[768,1024]{1,0:T(8,128)(2,1)} %get-tuple-element.636.refs_0_, bf16[768,1024]{1,0:T(8,128)(2,1)} %get-tuple-element.637.refs_0_.refs_1_, bf16[1024,1024]{1,0:T(8,128)(2,1)} %get-tuple-element.638.refs_0_.refs_2_, bf16[1024,1024]{1,0:T(8,128)(2,1)} %get-tuple-element.639.refs_0_.refs_3_, ...), custom_call_target="tpu_custom_call" | custom-call | flops 15032385536 | bytes 22020096 | tf_op jit(solution)/shard_map/pallas_call | solution.py:805
  649.3 21.7 %shard_map.245 = (bf16[4,448,2048]{2,1,0:T(8,128)(2,1)}, bf16[4,448,2048]{2,1,0:T(8,128)(2,1)}) custom-call(bf16[1024,1024]{1,0:T(8,128)(2,1)} %get-tuple-element.651.refs_2_.refs_0_, bf16[1024,1024]{1,0:T(8,128)(2,1)} %get-tuple-element.652.refs_3_.refs_1_, bf16[768,1024]{1,0:T(8,128)(2,1)} %get-tuple-element.653.refs_0_.refs_2_, ...), custom_call_target="tpu_custom_call" | custom-call | flops 15032385536 | bytes 22020096 | tf_op jit(solution)/shard_map/pallas_call | solution.py:678
  688.3 44.6 %shard_map.247 = (f32[256,3584]{1,0:T(8,128)}, f32[256,3584]{1,0:T(8,128)}, bf16[256,1536]{1,0:T(8,128)(2,1)}, f32[8,1536]{1,0:T(8,128)}) custom-call(s32[13]{0:T(128)} %pad_add_fusion.1.info, bf16[768,3584]{1,0:T(8,128)(2,1)} %get-tuple-element.705.qkv, bf16[4,3584,64]{2,1,0:T(8,128)(2,1)} %get-tuple-element.413.knat, ...), custom_call_target="tpu_custom_call" | custom-call | flops 45097156608 | bytes 33554432 | tf_op jit(solution)/shard_map/pallas_call | solution.py:293
  742.0 21.5 %shard_map.248 = bf16[1024,2048]{1,0:T(8,128)(2,1)} custom-call(bf16[768,1024]{1,0:T(8,128)(2,1)} %get-tuple-element.686.refs_2_.refs_0_, bf16[768,1024]{1,0:T(8,128)(2,1)} %get-tuple-element.687.refs_2_.refs_1_, bf16[1024,1024]{1,0:T(8,128)(2,1)} %get-tuple-element.688.refs_2_, bf16[1024,1024]{1,0:T(8,128)(2,1)} %get-tuple-element.689.refs_2_.refs_3_, ...), custom_call_target="tpu_custom_call" | custom-call | flops 15032385536 | bytes 22020096 | tf_op jit(solution)/shard_map/pallas_call | solution.py:805
  809.9 42.5 %shard_map.251 = (bf16[768,3584]{1,0:T(8,128)(2,1)}, f32[8,3584]{1,0:T(8,128)}) custom-call(s32[13]{0:T(128)} %pad_add_fusion.1.info, bf16[768,3584]{1,0:T(8,128)(2,1)} %get-tuple-element.705.qkv, bf16[4,3584,64]{2,1,0:T(8,128)(2,1)} %get-tuple-element.413.knat, bf16[4,3584,64]{2,1,0:T(8,128)(2,1)} %get-tuple-element.671.vnat, ...), custom_call_target="tpu_custom_call" | custom-call | flops 45097156608 | bytes 33554432 | tf_op jit(solution)/shard_map/pallas_call | solution.py:293
  866.4 20.9 %shard_map.252 = (bf16[4,1792,512]{2,1,0:T(8,128)(2,1)}, bf16[4,1792,512]{2,1,0:T(8,128)(2,1)}) custom-call(s32[3]{0:T(128)} %pad_add_fusion.places, bf16[768,3584]{1,0:T(8,128)(2,1)} %get-tuple-element.739.d_qkv, bf16[768,2048]{1,0:T(8,128)(2,1)} %bitcast.731), custom_call_target="tpu_custom_call" | custom-call | flops 11274289152 | bytes 14680064 | tf_op jit(solution)/shard_map/pallas_call | solution.py:865
  905.7 16.9 %shard_map.253 = (bf16[768,2048]{1,0:T(8,128)(2,1)}, f32[8,2048]{1,0:T(8,128)}) custom-call(bf16[768,3584]{1,0:T(8,128)(2,1)} %get-tuple-element.739.d_qkv, bf16[3584,2048]{1,0:T(8,128)(2,1)} %get-tuple-element.409.low, bf16[768,2048]{1,0:T(8,128)(2,1)} %bitcast.732), custom_call_target="tpu_custom_call" | custom-call | flops 11274289152 | bytes 20185088 | tf_op jit(solution)/shard_map/pallas_call | solution.py:827
  966.7 30.5 %collective-permute-done.122 = bf16[2,896,512]{2,1,0:T(8,128)(2,1)} collective-permute-done((bf16[2,896,512]{2,1,0:T(8,128)(2,1)}, bf16[2,896,512]{2,1,0:T(8,128)(2,1)}, u32[]{:S(2)}, u32[]{:S(2)}) %collective-permute-start.122) | collective-permute-done | bytes 1835040 | tf_op jit(solution)/shard_map/ppermute | solution.py:365
  (771 shorter events, 571.8 us)
Async XLA Ops:
  7.2 123.6 %all-gather.5.cloned.1.call-start = ((), (), s32[]{:S(2)}) async-start(), calls=%async_computation.6 | async-start | bytes 5242880 | tf_op jit(solution)/shard_map/all_gather | solution.py:959
  30.1 286.5 %all-gather.9.cloned.1.call-start = ((), (), s32[]{:S(2)}) async-start(), calls=%async_computation.8 | async-start | bytes 5242880 | tf_op jit(solution)/shard_map/all_gather | solution.py:939
  51.2 76.3 %collective-permute-start.9 = (bf16[1792,512]{1,0:T(8,128)(2,1)S(1)}, bf16[1792,512]{1,0:T(8,128)(2,1)}, u32[]{:S(2)}, u32[]{:S(2)}) collective-permute-start(bf16[1792,512]{1,0:T(8,128)(2,1)S(1)} %copy-done.10), channel_id=1, source_target_pairs={{0,8},{8,0},{1,9},{9,1},{2,10},{10,2},{3,11},{11,3},{4,12},{12,4},... | collective-permute-start | bytes 5505032 | tf_op jit(solution)/shard_map/ppermute | solution.py:365
  56.7 259.9 %all-gather.11.cloned.1.call-start = ((), (), s32[]{:S(2)}) async-start(), calls=%async_computation.9 | async-start | bytes 5242880 | tf_op jit(solution)/shard_map/all_gather | solution.py:939
  127.5 56.1 %collective-permute-start.8 = (bf16[1792,512]{1,0:T(8,128)(2,1)}, bf16[1792,512]{1,0:T(8,128)(2,1)}, u32[]{:S(2)}, u32[]{:S(2)}) collective-permute-start(bf16[1792,512]{1,0:T(8,128)(2,1)} %refs_0_.1), channel_id=1, source_target_pairs={{0,8},{8,0},{1,9},{9,1},{2,10},{10,2},{3,11},{11,3},{4,12},{12,4},... | collective-permute-start | bytes 5505032 | tf_op jit(solution)/shard_map/ppermute | solution.py:365
  127.5 56.1 %collective-permute-start.7 = (bf16[1792,512]{1,0:T(8,128)(2,1)}, bf16[1792,512]{1,0:T(8,128)(2,1)S(1)}, u32[]{:S(2)}, u32[]{:S(2)}) collective-permute-start(bf16[1792,512]{1,0:T(8,128)(2,1)} %refs_0_.1), channel_id=1, source_target_pairs={{0,1},{1,0},{2,3},{3,2},{4,5},{5,4},{6,7},{7,6},{8,9},{9,8},{10,11... | collective-permute-start | bytes 5505032 | tf_op jit(solution)/shard_map/ppermute | solution.py:365
  129.3 54.3 %collective-permute-start.6 = (bf16[1792,512]{1,0:T(8,128)(2,1)}, bf16[1792,512]{1,0:T(8,128)(2,1)}, u32[]{:S(2)}, u32[]{:S(2)}) collective-permute-start(bf16[1792,512]{1,0:T(8,128)(2,1)} %refs_0_.1), channel_id=1, source_target_pairs={{0,16},{16,0},{1,17},{17,1},{2,18},{18,2},{3,19},{19,3},{4,20},{20... | collective-permute-start | bytes 5505032 | tf_op jit(solution)/shard_map/ppermute | solution.py:365
  190.4 215.1 %all-gather.7.cloned.1.call-start = ((), (), s32[]{:S(2)}) async-start(), calls=%async_computation.7 | async-start | bytes 5242880 | tf_op jit(solution)/shard_map/all_gather | solution.py:939
  235.3 74.2 %collective-permute-start.41 = (bf16[4,128,2048]{2,1,0:T(8,128)(2,1)}, bf16[4,128,2048]{2,1,0:T(8,128)(2,1)S(1)}, u32[]{:S(2)}, u32[]{:S(2)}) collective-permute-start(bf16[4,128,2048]{2,1,0:T(8,128)(2,1)} %get-tuple-element.454), channel_id=1, source_target_pairs={{0,8},{8,0},{1,9},{9,1},{2,10},{10,2},{3,11},{11,3},{4,12},{12,4},... | collective-permute-start | bytes 6291464 | tf_op jit(solution)/shard_map/ppermute | solution.py:365
  312.4 468.5 %reduce-scatter.8.cloned.1.call-start = ((), (), s32[]{:S(2)}) async-start(), calls=%async_computation.11 | async-start | bytes 5242880 | tf_op jit(solution)/shard_map/reduce_scatter | solution.py:1013
  495.0 303.8 %reduce-scatter.6.cloned.1.call-start = ((), (), s32[]{:S(2)}) async-start(), calls=%async_computation.10 | async-start | bytes 5242880 | tf_op jit(solution)/shard_map/reduce_scatter | solution.py:1013
  636.5 250.8 %reduce-scatter.10.cloned.1.call-start = ((), (), s32[]{:S(2)}) async-start(), calls=%async_computation.12 | async-start | bytes 5242880 | tf_op jit(solution)/shard_map/reduce_scatter | solution.py:1013
  674.7 58.2 %collective-permute-start.97 = (bf16[64,2048]{1,0:T(8,128)(2,1)}, bf16[64,2048]{1,0:T(8,128)(2,1)}, u32[]{:S(2)}, u32[]{:S(2)}) collective-permute-start(bf16[64,2048]{1,0:T(8,128)(2,1)} %slice.918), channel_id=1, source_target_pairs={{0,1},{1,0},{2,3},{3,2},{4,5},{5,4},{6,7},{7,6},{8,9},{9,8},{10,11... | collective-permute-start | bytes 786440 | tf_op jit(solution)/shard_map/ppermute | solution.py:365
  676.1 56.8 %collective-permute-start.96 = (bf16[64,2048]{1,0:T(8,128)(2,1)S(1)}, bf16[64,2048]{1,0:T(8,128)(2,1)}, u32[]{:S(2)}, u32[]{:S(2)}) collective-permute-start(bf16[64,2048]{1,0:T(8,128)(2,1)S(1)} %slice.917), channel_id=1, source_target_pairs={{0,16},{16,0},{1,17},{17,1},{2,18},{18,2},{3,19},{19,3},{4,20},{20... | collective-permute-start | bytes 786440 | tf_op jit(solution)/shard_map/ppermute | solution.py:365
  682.4 118.5 %collective-permute-start.109 = (bf16[4,448,2048]{2,1,0:T(8,128)(2,1)}, bf16[4,448,2048]{2,1,0:T(8,128)(2,1)}, u32[]{:S(2)}, u32[]{:S(2)}) collective-permute-start(bf16[4,448,2048]{2,1,0:T(8,128)(2,1)} %get-tuple-element.669), channel_id=1, source_target_pairs={{0,8},{8,0},{1,9},{9,1},{2,10},{10,2},{3,11},{11,3},{4,12},{12,4},... | collective-permute-start | bytes 22020104 | tf_op jit(solution)/shard_map/ppermute | solution.py:365
  735.0 50.0 %collective-permute-start.101 = (bf16[512,2048]{1,0:T(8,128)(2,1)S(1)}, bf16[512,2048]{1,0:T(8,128)(2,1)}, u32[]{:S(2)}, u32[]{:S(2)}) collective-permute-start(bf16[512,2048]{1,0:T(8,128)(2,1)S(1)} %constant_dynamic-update-slice_fusion.42.refs_0_), channel_id=1, source_target_pairs={{0,8},{8,0},{1,9},{9,1},{2,10},{10,2},{3,11},{11,3},{4,12},{12,4},... | collective-permute-start | bytes 6291464 | tf_op jit(solution)/shard_map/ppermute | solution.py:365
  779.8 251.8 %reduce-scatter.12.cloned.1.call-start = ((), (), s32[]{:S(2)}) async-start(), calls=%async_computation.13 | async-start | bytes 3932160 | tf_op jit(solution)/shard_map/reduce_scatter | solution.py:1013
  783.5 68.9 %collective-permute-start.113 = (bf16[2,256,512]{2,1,0:T(8,128)(2,1)}, bf16[2,256,512]{2,1,0:T(8,128)(2,1)}, u32[]{:S(2)}, u32[]{:S(2)}) collective-permute-start(bf16[2,256,512]{2,1,0:T(8,128)(2,1)} %get-tuple-element.704), channel_id=1, source_target_pairs={{0,16},{16,0},{1,17},{17,1},{2,18},{18,2},{3,19},{19,3},{4,20},{20... | collective-permute-start | bytes 1572872 | tf_op jit(solution)/shard_map/ppermute | solution.py:365
  800.3 54.4 %collective-permute-start.100 = (bf16[2,256,512]{2,1,0:T(8,128)(2,1)S(1)}, bf16[2,256,512]{2,1,0:T(8,128)(2,1)S(1)}, u32[]{:S(2)}, u32[]{:S(2)}) collective-permute-start(bf16[2,256,512]{2,1,0:T(8,128)(2,1)S(1)} %get-tuple-element.690), channel_id=1, source_target_pairs={{0,16},{16,0},{1,17},{17,1},{2,18},{18,2},{3,19},{19,3},{4,20},{20... | collective-permute-start | bytes 1572872 | tf_op jit(solution)/shard_map/ppermute | solution.py:365
  807.9 50.8 %collective-permute-start.111 = (bf16[2,224,2048]{2,1,0:T(8,128)(2,1)}, bf16[2,224,2048]{2,1,0:T(8,128)(2,1)}, u32[]{:S(2)}, u32[]{:S(2)}) collective-permute-start(bf16[2,224,2048]{2,1,0:T(8,128)(2,1)} %get-tuple-element.702), channel_id=1, source_target_pairs={{0,16},{16,0},{1,17},{17,1},{2,18},{18,2},{3,19},{19,3},{4,20},{20... | collective-permute-start | bytes 5505032 | tf_op jit(solution)/shard_map/ppermute | solution.py:365
  809.4 49.2 %collective-permute-start.112 = (bf16[2,224,2048]{2,1,0:T(8,128)(2,1)}, bf16[2,224,2048]{2,1,0:T(8,128)(2,1)}, u32[]{:S(2)}, u32[]{:S(2)}) collective-permute-start(bf16[2,224,2048]{2,1,0:T(8,128)(2,1)} %get-tuple-element.703), channel_id=1, source_target_pairs={{0,1},{1,0},{2,3},{3,2},{4,5},{5,4},{6,7},{7,6},{8,9},{9,8},{10,11... | collective-permute-start | bytes 5505032 | tf_op jit(solution)/shard_map/ppermute | solution.py:365
  928.6 103.0 %reduce-scatter.14.cloned.1.call-start = ((), (), s32[]{:S(2)}) async-start(), calls=%async_computation.14 | async-start | bytes 1310720 | tf_op jit(solution)/shard_map/reduce_scatter | solution.py:1013
  946.9 50.3 %collective-permute-start.122 = (bf16[2,896,512]{2,1,0:T(8,128)(2,1)}, bf16[2,896,512]{2,1,0:T(8,128)(2,1)}, u32[]{:S(2)}, u32[]{:S(2)}) collective-permute-start(bf16[2,896,512]{2,1,0:T(8,128)(2,1)} %get-tuple-element.744), channel_id=1, source_target_pairs={{0,16},{16,0},{1,17},{17,1},{2,18},{18,2},{3,19},{19,3},{4,20},{20... | collective-permute-start | bytes 5505032 | tf_op jit(solution)/shard_map/ppermute | solution.py:365
  948.4 48.9 %collective-permute-start.123 = (bf16[2,896,512]{2,1,0:T(8,128)(2,1)}, bf16[2,896,512]{2,1,0:T(8,128)(2,1)}, u32[]{:S(2)}, u32[]{:S(2)}) collective-permute-start(bf16[2,896,512]{2,1,0:T(8,128)(2,1)} %get-tuple-element.745), channel_id=1, source_target_pairs={{0,1},{1,0},{2,3},{3,2},{4,5},{5,4},{6,7},{7,6},{8,9},{9,8},{10,11... | collective-permute-start | bytes 5505032 | tf_op jit(solution)/shard_map/ppermute | solution.py:365
  (204 other events, 3789.0 us)
Sparse Core Ops, SparseCore 0:
  30.3 82.2 all-gather.4
  114.1 79.2 all-gather.8
  195.0 79.9 all-gather.10
  312.6 83.2 all-gather.6
  495.1 80.7 reduce-scatter.7
  636.6 80.7 reduce-scatter.5
  779.9 84.2 reduce-scatter.9
  922.7 67.4 reduce-scatter.11
  992.6 27.6 reduce-scatter.13

commit v6 on v5

--- a/solution.py
+++ b/solution.py
@@ -1167,15 +1167,12 @@
         lines.start("down", home_steps(down_sum))
         lines.start("gate", home_steps(gate_sum))
         d_qkv, inner = tick(lambda ties: backward(prompts, ties, before), "mixed", "down", "gate")
-        inner = straighten(inner[0].reshape(BLOCKS, team, sub), rank).reshape(GTOK)
-        lines.start("inner", summed(inner, ("x", "c", "y")))
         lines.start("up", home_steps(up_sum))
         own, other = tick(
             lambda ties: last_product(places, after(d_qkv, *ties), join_weight),
             "mixed",
             "down",
             "gate",
-            "inner",
         )
         lines.start("last", sum_steps(own, other))
         mixed = lines.results["mixed"]
@@ -1194,9 +1191,11 @@
             lambda ties: join_product(after(d_qkv, *ties), low_one, join_weight),
             "last",
             "up",
-            "inner",
         )
         join_sum = total(join_grad)
+        inner = after(inner, join_grad)
+        inner = straighten(inner[0].reshape(BLOCKS, team, sub), rank).reshape(GTOK)
+        lines.start("inner", summed(inner, ("x", "c", "y")))
         out_grad = tick(
             lambda ties: grad_product(
                 after([heads_parts[k] for k in ordered], *ties), [attended[k] for k in ordered], NN
@@ -1208,8 +1207,9 @@
         turned = lines.wanted["last"][1][0][0]
         sums = outcome(after(layer_out, out_grad), share[0])
         lines.start("sums", summed(sums, ("c", "z1", "z2", "x", "y")))
-        for _ in range(3):
-            tick(None, "sums")
+        tick(None, "sums", "inner")
+        tick(None, "sums", "inner")
+        tick(None, "sums")
         tick(None, "last")
         lines.last = [lines.results["last"]]
         for _ in range(2):

time: 1070 us -> 1070 us (level)
    ppermute x134, waiting for transfers between devices: 158 us -> 171 us  [flip(): return lax.ppermute(values, axis, [(0, 1), (1, 0)])]
    unnamed x226 -> x228, local copies, waits for them, and re-layouts: 50.5 us -> 45.9 us
  transfers between devices with their start and end apart: 146 -> 146, of which waited for: 31 -> 31; matrix products, arithmetic and copies ran while one was open for 22% -> 21% of each run, Pallas kernels for 42% -> 42%
where the time goes in v6:
time: 1070 us; the launch traced here: 1060 us
  Pallas kernels  506 us (47%)
  waiting for transfers between devices  171 us (16%)
  other arithmetic  130 us (12%)
  starting transfers between devices  120 us (11%)
  local copies, waits for them, and re-layouts  113 us (11%)
  between operations  21.9 us (2%)
    ppermute x134, waiting for transfers between devices, flip(): return lax.ppermute(values, axis, [(0, 1), (1, 0)])  171 us
    ppermute x134, starting transfers between devices, flip(): return lax.ppermute(values, axis, [(0, 1), (1, 0)])  109 us
    pallas_call x2, Pallas kernels, attend_backward(): pl.pallas_call(functools.partial(backward_kernel, heads, 0 if final else...  90 us
    pallas_call x4, Pallas kernels, grad_product(): pl.pallas_call(functools.partial(grad_kernel, len(lefts), form, starts),...  74.3 us
    pallas_call x8, Pallas kernels, split_product(): pl.pallas_call(functools.partial(split_kernel, len(pairs), form, sub), gr...  67.7 us
    pallas_call x4, Pallas kernels, attend_forward(): pl.pallas_call(functools.partial(forward_kernel, heads, first), grid=(cou...  59.2 us
    pallas_call x4, Pallas kernels, unit_products(): pl.pallas_call(functools.partial(unit_kernel, len(pieces)), grid=(units /...  50.8 us
    unnamed x228, local copies, waits for them, and re-layouts  45.9 us
  transfers between devices with their start and end apart: 146, of which 31 were waited for; matrix products, arithmetic and copies ran while one was open for 21% of the time, Pallas kernels for 42%

profile of v6, /device:TPU:0, one launch (start us, length us, event | category | flops | bytes accessed | tf_op | source)
XLA Modules:
  0.0 1062.4 jit_solution(9673132060998927474)
XLA Ops:
  14.7 11.9 %collective-permute-done.2 = bf16[2,4,64,512]{3,2,0,1:T(8,128)(2,1)S(1)} collective-permute-done((bf16[2,4,64,512]{3,2,0,1:T(8,128)(2,1)S(1)}, bf16[2,4,64,512]{3,2,0,1:T(8,128)(2,1)S(1)}, u32[]{:S(2)}, u32[]{:S(2)}) %collective-permute-start.2) | collective-permute-done | bytes 524320 | tf_op jit(solution)/shard_map/ppermute | solution.py:365
  57.0 21.6 %collective-permute-done.refs_4_ = bf16[1792,512]{1,0:T(8,128)(2,1)} collective-permute-done((bf16[1792,512]{1,0:T(8,128)(2,1)S(1)}, bf16[1792,512]{1,0:T(8,128)(2,1)}, u32[]{:S(2)}, u32[]{:S(2)}) %collective-permute-start) | collective-permute-done | bytes 1835040 | tf_op jit(solution)/shard_map/ppermute | solution.py:365
  81.0 11.5 %collective-permute-done.4.refs_2_ = bf16[1792,512]{1,0:T(8,128)(2,1)} collective-permute-done((bf16[1792,512]{1,0:T(8,128)(2,1)S(1)}, bf16[1792,512]{1,0:T(8,128)(2,1)}, u32[]{:S(2)}, u32[]{:S(2)}) %collective-permute-start.4) | collective-permute-done | bytes 1835040 | tf_op jit(solution)/shard_map/ppermute | solution.py:365
  134.8 27.0 %shard_map.220 = (bf16[3584,2048]{1,0:T(8,128)(2,1)}, bf16[448,2048]{1,0:T(8,128)(2,1)}, bf16[768,3584]{1,0:T(8,128)(2,1)}, bf16[4,3584,64]{2,1,0:T(8,128)(2,1)}, bf16[4,3584,64]{2,1,0:T(8,128)(2,1)}) custom-call(s32[3]{0:T(128)} %pad_add_fusion.places, bf16[1792,512]{1,0:T(8,128)(2,1)} %refs_0_, bf16[1792,512]{1,0:T(8,128)(2,1)} %collective-permute-done.9.refs_1_, ...), custom_call_target="tpu_custom_call" | custom-call | flops 11318329344 | bytes 36700160 | tf_op jit(solution)/shard_map/pallas_call | solution.py:589
  162.1 16.0 %shard_map.221 = (bf16[256,768]{1,0:T(8,128)(2,1)}, f32[8,768]{1,0:T(8,128)}) custom-call(s32[13]{0:T(128)} %pad_add_fusion.1.info, bf16[768,3584]{1,0:T(8,128)(2,1)} %get-tuple-element.704.qkv, bf16[4,3584,64]{2,1,0:T(8,128)(2,1)} %get-tuple-element.412.knat), custom_call_target="tpu_custom_call" | custom-call | flops 12079595520 | bytes 16777216 | tf_op jit(solution)/shard_map/pallas_call | solution.py:122
  192.2 15.8 %shard_map.223 = (bf16[256,768]{1,0:T(8,128)(2,1)}, f32[8,768]{1,0:T(8,128)}) custom-call(s32[13]{0:T(128)} %pad_add_fusion.1.info, bf16[768,3584]{1,0:T(8,128)(2,1)} %get-tuple-element.704.qkv, bf16[4,3584,64]{2,1,0:T(8,128)(2,1)} %get-tuple-element.412.knat), custom_call_target="tpu_custom_call" | custom-call | flops 12079595520 | bytes 16777216 | tf_op jit(solution)/shard_map/pallas_call | solution.py:122
  247.0 16.7 %shard_map.227 = (bf16[256,1024]{1,0:T(8,128)(2,1)}, f32[8,1024]{1,0:T(8,128)}) custom-call(s32[13]{0:T(128)} %pad_add_fusion.1.info, bf16[768,3584]{1,0:T(8,128)(2,1)} %get-tuple-element.704.qkv, bf16[4,3584,64]{2,1,0:T(8,128)(2,1)} %get-tuple-element.412.knat), custom_call_target="tpu_custom_call" | custom-call | flops 16106127360 | bytes 16777216 | tf_op jit(solution)/shard_map/pallas_call | solution.py:122
  278.7 17.2 %shard_map.229 = (bf16[3584,2048]{1,0:T(8,128)(2,1)}, bf16[448,2048]{1,0:T(8,128)(2,1)}) custom-call(s32[3]{0:T(128)} %pad_add_fusion.places, bf16[1792,512]{1,0:T(8,128)(2,1)} %refs_0_.1, bf16[1792,512]{1,0:T(8,128)(2,1)} %collective-permute-done.8.refs_1_, bf16[1792,512]{1,0:T(8,128)(2,1)} %collective-permute-done.6.refs_2_, ...), custom_call_target="tpu_custom_call" | custom-call | flops 44040192 | bytes 36700160 | tf_op jit(solution)/shard_map/pallas_call | solution.py:589
  318.7 11.4 %shard_map.230 = (bf16[768,2048]{1,0:T(8,128)(2,1)}, bf16[768,1024]{1,0:T(8,128)(2,1)}, bf16[768,1024]{1,0:T(8,128)(2,1)}, bf16[768,1024]{1,0:T(8,128)(2,1)}) custom-call(bf16[384,2048]{1,0:T(8,128)(2,1)} %constant_dynamic-update-slice_fusion.4.refs_0_, bf16[384,2048]{1,0:T(8,128)(2,1)} %collective-permute-done.38.refs_1_, ...), custom_call_target="tpu_custom_call" | custom-call | flops 6442450944 | bytes 14680064 | tf_op jit(solution)/shard_map/pallas_call | solution.py:724
  361.2 11.4 %shard_map.231 = (bf16[768,2048]{1,0:T(8,128)(2,1)}, bf16[768,1024]{1,0:T(8,128)(2,1)}, bf16[768,1024]{1,0:T(8,128)(2,1)}, bf16[768,1024]{1,0:T(8,128)(2,1)}) custom-call(bf16[384,2048]{1,0:T(8,128)(2,1)} %constant_dynamic-update-slice_fusion.9.refs_0_, bf16[384,2048]{1,0:T(8,128)(2,1)} %collective-permute-done.46.refs_1_, ...), custom_call_target="tpu_custom_call" | custom-call | flops 6442450944 | bytes 14680064 | tf_op jit(solution)/shard_map/pallas_call | solution.py:724
  407.7 14.0 %shard_map.232 = (bf16[1024,2048]{1,0:T(8,128)(2,1)}, bf16[1024,1024]{1,0:T(8,128)(2,1)}, bf16[1024,1024]{1,0:T(8,128)(2,1)}, bf16[1024,1024]{1,0:T(8,128)(2,1)}) custom-call(bf16[512,2048]{1,0:T(8,128)(2,1)} %constant_dynamic-update-slice_fusion.14.refs_0_, bf16[512,2048]{1,0:T(8,128)(2,1)} %collective-permute-done.56.refs_1_, ...), custom_call_target="tpu_custom_call" | custom-call | flops 8589934592 | bytes 16777216 | tf_op jit(solution)/shard_map/pallas_call | solution.py:724
  436.9 14.0 %shard_map.233 = (bf16[1024,2048]{1,0:T(8,128)(2,1)}, bf16[1024,1024]{1,0:T(8,128)(2,1)}, bf16[1024,1024]{1,0:T(8,128)(2,1)}, bf16[1024,1024]{1,0:T(8,128)(2,1)}) custom-call(bf16[512,2048]{1,0:T(8,128)(2,1)} %copy-done.57, bf16[512,2048]{1,0:T(8,128)(2,1)} %copy-done.82, bf16[1024,2048]{1,0:T(8,128)(2,1)} %all-gather.9.cloned.1.call-done.refs_2_.refs_1_, ...), custom_call_target="tpu_custom_call" | custom-call | flops 8589934592 | bytes 16777216 | tf_op jit(solution)/shard_map/pallas_call | solution.py:724
  450.9 21.7 %shard_map.234 = bf16[1024,2048]{1,0:T(8,128)(2,1)} custom-call(bf16[768,1024]{1,0:T(8,128)(2,1)} %get-tuple-element.652.refs_0_.refs_2_, bf16[768,1024]{1,0:T(8,128)(2,1)} %get-tuple-element.653.refs_1_.refs_3_, bf16[1024,1024]{1,0:T(8,128)(2,1)} %get-tuple-element.650.refs_2_.refs_0_, bf16[1024,1024]{1,0:T(8,128)(2,1)} %get-tuple-element.651.refs_3_.refs_1_, ...), custom_call_target="tpu_custom_call" | custom-call | flops 15032385536 | bytes 22020096 | tf_op jit(solution)/shard_map/pallas_call | solution.py:805
  481.4 10.8 %shard_map.236 = (bf16[4,96,2048]{2,1,0:T(8,128)(2,1)}, bf16[4,96,2048]{2,1,0:T(8,128)(2,1)}) custom-call(bf16[768,1024]{1,0:T(8,128)(2,1)} %get-tuple-element.635.refs_0_, bf16[1024,2048]{1,0:T(8,128)(2,1)} %all-gather.9.cloned.1.call-done.refs_2_.refs_1_, bf16[768,1024]{1,0:T(8,128)(2,1)} %get-tuple-element.685.refs_2_.refs_0_, ...), custom_call_target="tpu_custom_call" | custom-call | flops 6442450944 | bytes 14680064 | tf_op jit(solution)/shard_map/pallas_call | solution.py:647
  544.0 13.3 %shard_map.240 = (bf16[4,128,2048]{2,1,0:T(8,128)(2,1)}, bf16[4,128,2048]{2,1,0:T(8,128)(2,1)}) custom-call(bf16[1024,1024]{1,0:T(8,128)(2,1)} %get-tuple-element.637.refs_0_.refs_2_, bf16[1024,2048]{1,0:T(8,128)(2,1)} %all-gather.9.cloned.1.call-done.refs_2_.refs_1_, bf16[1024,1024]{1,0:T(8,128)(2,1)} %get-tuple-element.687.refs_2_, ...), custom_call_target="tpu_custom_call" | custom-call | flops 8589934592 | bytes 16777216 | tf_op jit(solution)/shard_map/pallas_call | solution.py:647
  585.8 13.4 %shard_map.242 = (bf16[4,128,2048]{2,1,0:T(8,128)(2,1)}, bf16[4,128,2048]{2,1,0:T(8,128)(2,1)}) custom-call(bf16[1024,1024]{1,0:T(8,128)(2,1)} %get-tuple-element.638.refs_0_.refs_3_, bf16[1024,2048]{1,0:T(8,128)(2,1)} %all-gather.9.cloned.1.call-done.refs_2_.refs_1_, bf16[1024,1024]{1,0:T(8,128)(2,1)} %get-tuple-element.688.refs_2_.refs_3_, ...), custom_call_target="tpu_custom_call" | custom-call | flops 8589934592 | bytes 16777216 | tf_op jit(solution)/shard_map/pallas_call | solution.py:647
  612.1 21.6 %shard_map.244 = bf16[1024,2048]{1,0:T(8,128)(2,1)} custom-call(bf16[768,1024]{1,0:T(8,128)(2,1)} %get-tuple-element.635.refs_0_, bf16[768,1024]{1,0:T(8,128)(2,1)} %get-tuple-element.636.refs_0_.refs_1_, bf16[1024,1024]{1,0:T(8,128)(2,1)} %get-tuple-element.637.refs_0_.refs_2_, bf16[1024,1024]{1,0:T(8,128)(2,1)} %get-tuple-element.638.refs_0_.refs_3_, ...), custom_call_target="tpu_custom_call" | custom-call | flops 15032385536 | bytes 22020096 | tf_op jit(solution)/shard_map/pallas_call | solution.py:805
  649.1 21.5 %shard_map.245 = (bf16[4,448,2048]{2,1,0:T(8,128)(2,1)}, bf16[4,448,2048]{2,1,0:T(8,128)(2,1)}) custom-call(bf16[1024,1024]{1,0:T(8,128)(2,1)} %get-tuple-element.650.refs_2_.refs_0_, bf16[1024,1024]{1,0:T(8,128)(2,1)} %get-tuple-element.651.refs_3_.refs_1_, bf16[768,1024]{1,0:T(8,128)(2,1)} %get-tuple-element.652.refs_0_.refs_2_, ...), custom_call_target="tpu_custom_call" | custom-call | flops 15032385536 | bytes 22020096 | tf_op jit(solution)/shard_map/pallas_call | solution.py:678
  686.1 47.7 %shard_map.247 = (f32[256,3584]{1,0:T(8,128)}, f32[256,3584]{1,0:T(8,128)}, bf16[256,1536]{1,0:T(8,128)(2,1)}, f32[8,1536]{1,0:T(8,128)}) custom-call(s32[13]{0:T(128)} %pad_add_fusion.1.info, bf16[768,3584]{1,0:T(8,128)(2,1)} %get-tuple-element.704.qkv, bf16[4,3584,64]{2,1,0:T(8,128)(2,1)} %get-tuple-element.412.knat, ...), custom_call_target="tpu_custom_call" | custom-call | flops 45097156608 | bytes 33554432 | tf_op jit(solution)/shard_map/pallas_call | solution.py:293
  742.8 21.6 %shard_map.248 = bf16[1024,2048]{1,0:T(8,128)(2,1)} custom-call(bf16[768,1024]{1,0:T(8,128)(2,1)} %get-tuple-element.685.refs_2_.refs_0_, bf16[768,1024]{1,0:T(8,128)(2,1)} %get-tuple-element.686.refs_2_.refs_1_, bf16[1024,1024]{1,0:T(8,128)(2,1)} %get-tuple-element.687.refs_2_, bf16[1024,1024]{1,0:T(8,128)(2,1)} %get-tuple-element.688.refs_2_.refs_3_, ...), custom_call_target="tpu_custom_call" | custom-call | flops 15032385536 | bytes 22020096 | tf_op jit(solution)/shard_map/pallas_call | solution.py:805
  808.5 42.4 %shard_map.251 = (bf16[768,3584]{1,0:T(8,128)(2,1)}, f32[8,3584]{1,0:T(8,128)}) custom-call(s32[13]{0:T(128)} %pad_add_fusion.1.info, bf16[768,3584]{1,0:T(8,128)(2,1)} %get-tuple-element.704.qkv, bf16[4,3584,64]{2,1,0:T(8,128)(2,1)} %get-tuple-element.412.knat, bf16[4,3584,64]{2,1,0:T(8,128)(2,1)} %get-tuple-element.670.vnat, ...), custom_call_target="tpu_custom_call" | custom-call | flops 45097156608 | bytes 33554432 | tf_op jit(solution)/shard_map/pallas_call | solution.py:293
  861.5 20.9 %shard_map.252 = (bf16[4,1792,512]{2,1,0:T(8,128)(2,1)}, bf16[4,1792,512]{2,1,0:T(8,128)(2,1)}) custom-call(s32[3]{0:T(128)} %pad_add_fusion.places, bf16[768,3584]{1,0:T(8,128)(2,1)} %get-tuple-element.735.d_qkv, bf16[768,2048]{1,0:T(8,128)(2,1)} %bitcast.731), custom_call_target="tpu_custom_call" | custom-call | flops 11274289152 | bytes 14680064 | tf_op jit(solution)/shard_map/pallas_call | solution.py:865
  901.6 16.9 %shard_map.253 = (bf16[768,2048]{1,0:T(8,128)(2,1)}, f32[8,2048]{1,0:T(8,128)}) custom-call(bf16[768,3584]{1,0:T(8,128)(2,1)} %get-tuple-element.735.d_qkv, bf16[3584,2048]{1,0:T(8,128)(2,1)} %get-tuple-element.408.low, bf16[768,2048]{1,0:T(8,128)(2,1)} %bitcast.732), custom_call_target="tpu_custom_call" | custom-call | flops 11274289152 | bytes 20185088 | tf_op jit(solution)/shard_map/pallas_call | solution.py:827
  963.0 32.9 %collective-permute-done.121 = f32[3584]{0:T(1024)S(1)} collective-permute-done((f32[3584]{0:T(1024)S(1)}, f32[3584]{0:T(1024)S(1)}, u32[]{:S(2)}, u32[]{:S(2)}) %collective-permute-start.121) | collective-permute-done | bytes 14368 | tf_op jit(solution)/shard_map/ppermute | solution.py:365
  (773 shorter events, 567.3 us)
Async XLA Ops:
  7.2 123.7 %all-gather.5.cloned.1.call-start = ((), (), s32[]{:S(2)}) async-start(), calls=%async_computation.6 | async-start | bytes 5242880 | tf_op jit(solution)/shard_map/all_gather | solution.py:959
  30.1 288.5 %all-gather.9.cloned.1.call-start = ((), (), s32[]{:S(2)}) async-start(), calls=%async_computation.8 | async-start | bytes 5242880 | tf_op jit(solution)/shard_map/all_gather | solution.py:939
  51.2 76.4 %collective-permute-start.9 = (bf16[1792,512]{1,0:T(8,128)(2,1)S(1)}, bf16[1792,512]{1,0:T(8,128)(2,1)}, u32[]{:S(2)}, u32[]{:S(2)}) collective-permute-start(bf16[1792,512]{1,0:T(8,128)(2,1)S(1)} %copy-done.10), channel_id=1, source_target_pairs={{0,8},{8,0},{1,9},{9,1},{2,10},{10,2},{3,11},{11,3},{4,12},{12,4},... | collective-permute-start | bytes 5505032 | tf_op jit(solution)/shard_map/ppermute | solution.py:365
  56.7 261.9 %all-gather.11.cloned.1.call-start = ((), (), s32[]{:S(2)}) async-start(), calls=%async_computation.9 | async-start | bytes 5242880 | tf_op jit(solution)/shard_map/all_gather | solution.py:939
  127.5 57.5 %collective-permute-start.8 = (bf16[1792,512]{1,0:T(8,128)(2,1)}, bf16[1792,512]{1,0:T(8,128)(2,1)}, u32[]{:S(2)}, u32[]{:S(2)}) collective-permute-start(bf16[1792,512]{1,0:T(8,128)(2,1)} %refs_0_.1), channel_id=1, source_target_pairs={{0,8},{8,0},{1,9},{9,1},{2,10},{10,2},{3,11},{11,3},{4,12},{12,4},... | collective-permute-start | bytes 5505032 | tf_op jit(solution)/shard_map/ppermute | solution.py:365
  127.6 57.5 %collective-permute-start.7 = (bf16[1792,512]{1,0:T(8,128)(2,1)}, bf16[1792,512]{1,0:T(8,128)(2,1)S(1)}, u32[]{:S(2)}, u32[]{:S(2)}) collective-permute-start(bf16[1792,512]{1,0:T(8,128)(2,1)} %refs_0_.1), channel_id=1, source_target_pairs={{0,1},{1,0},{2,3},{3,2},{4,5},{5,4},{6,7},{7,6},{8,9},{9,8},{10,11... | collective-permute-start | bytes 5505032 | tf_op jit(solution)/shard_map/ppermute | solution.py:365
  129.3 55.7 %collective-permute-start.6 = (bf16[1792,512]{1,0:T(8,128)(2,1)}, bf16[1792,512]{1,0:T(8,128)(2,1)}, u32[]{:S(2)}, u32[]{:S(2)}) collective-permute-start(bf16[1792,512]{1,0:T(8,128)(2,1)} %refs_0_.1), channel_id=1, source_target_pairs={{0,16},{16,0},{1,17},{17,1},{2,18},{18,2},{3,19},{19,3},{4,20},{20... | collective-permute-start | bytes 5505032 | tf_op jit(solution)/shard_map/ppermute | solution.py:365
  191.8 215.9 %all-gather.7.cloned.1.call-start = ((), (), s32[]{:S(2)}) async-start(), calls=%async_computation.7 | async-start | bytes 5242880 | tf_op jit(solution)/shard_map/all_gather | solution.py:939
  237.4 74.1 %collective-permute-start.41 = (bf16[4,128,2048]{2,1,0:T(8,128)(2,1)}, bf16[4,128,2048]{2,1,0:T(8,128)(2,1)S(1)}, u32[]{:S(2)}, u32[]{:S(2)}) collective-permute-start(bf16[4,128,2048]{2,1,0:T(8,128)(2,1)} %get-tuple-element.453), channel_id=1, source_target_pairs={{0,8},{8,0},{1,9},{9,1},{2,10},{10,2},{3,11},{11,3},{4,12},{12,4},... | collective-permute-start | bytes 6291464 | tf_op jit(solution)/shard_map/ppermute | solution.py:365
  314.5 465.2 %reduce-scatter.8.cloned.1.call-start = ((), (), s32[]{:S(2)}) async-start(), calls=%async_computation.11 | async-start | bytes 5242880 | tf_op jit(solution)/shard_map/reduce_scatter | solution.py:1013
  497.0 300.0 %reduce-scatter.6.cloned.1.call-start = ((), (), s32[]{:S(2)}) async-start(), calls=%async_computation.10 | async-start | bytes 5242880 | tf_op jit(solution)/shard_map/reduce_scatter | solution.py:1013
  635.6 246.8 %reduce-scatter.10.cloned.1.call-start = ((), (), s32[]{:S(2)}) async-start(), calls=%async_computation.12 | async-start | bytes 5242880 | tf_op jit(solution)/shard_map/reduce_scatter | solution.py:1013
  672.9 60.8 %collective-permute-start.97 = (bf16[64,2048]{1,0:T(8,128)(2,1)}, bf16[64,2048]{1,0:T(8,128)(2,1)S(1)}, u32[]{:S(2)}, u32[]{:S(2)}) collective-permute-start(bf16[64,2048]{1,0:T(8,128)(2,1)} %slice.918), channel_id=1, source_target_pairs={{0,1},{1,0},{2,3},{3,2},{4,5},{5,4},{6,7},{7,6},{8,9},{9,8},{10,11... | collective-permute-start | bytes 786440 | tf_op jit(solution)/shard_map/ppermute | solution.py:365
  674.2 59.5 %collective-permute-start.96 = (bf16[64,2048]{1,0:T(8,128)(2,1)}, bf16[64,2048]{1,0:T(8,128)(2,1)S(1)}, u32[]{:S(2)}, u32[]{:S(2)}) collective-permute-start(bf16[64,2048]{1,0:T(8,128)(2,1)} %slice.917), channel_id=1, source_target_pairs={{0,16},{16,0},{1,17},{17,1},{2,18},{18,2},{3,19},{19,3},{4,20},{20... | collective-permute-start | bytes 786440 | tf_op jit(solution)/shard_map/ppermute | solution.py:365
  680.2 119.3 %collective-permute-start.109 = (bf16[4,448,2048]{2,1,0:T(8,128)(2,1)}, bf16[4,448,2048]{2,1,0:T(8,128)(2,1)}, u32[]{:S(2)}, u32[]{:S(2)}) collective-permute-start(bf16[4,448,2048]{2,1,0:T(8,128)(2,1)} %get-tuple-element.668), channel_id=1, source_target_pairs={{0,8},{8,0},{1,9},{9,1},{2,10},{10,2},{3,11},{11,3},{4,12},{12,4},... | collective-permute-start | bytes 22020104 | tf_op jit(solution)/shard_map/ppermute | solution.py:365
  684.5 52.5 %collective-permute-start.98 = (bf16[64,2048]{1,0:T(8,128)(2,1)S(1)}, bf16[64,2048]{1,0:T(8,128)(2,1)S(1)}, u32[]{:S(2)}, u32[]{:S(2)}) collective-permute-start(bf16[64,2048]{1,0:T(8,128)(2,1)S(1)} %get-tuple-element.665), channel_id=1, source_target_pairs={{0,1},{1,0},{2,3},{3,2},{4,5},{5,4},{6,7},{7,6},{8,9},{9,8},{10,11... | collective-permute-start | bytes 786440 | tf_op jit(solution)/shard_map/ppermute | solution.py:365
  685.3 51.6 %collective-permute-start.99 = (bf16[64,2048]{1,0:T(8,128)(2,1)S(1)}, bf16[64,2048]{1,0:T(8,128)(2,1)S(1)}, u32[]{:S(2)}, u32[]{:S(2)}) collective-permute-start(bf16[64,2048]{1,0:T(8,128)(2,1)S(1)} %get-tuple-element.666), channel_id=1, source_target_pairs={{0,16},{16,0},{1,17},{17,1},{2,18},{18,2},{3,19},{19,3},{4,20},{20... | collective-permute-start | bytes 786440 | tf_op jit(solution)/shard_map/ppermute | solution.py:365
  778.5 255.1 %reduce-scatter.12.cloned.1.call-start = ((), (), s32[]{:S(2)}) async-start(), calls=%async_computation.13 | async-start | bytes 3932160 | tf_op jit(solution)/shard_map/reduce_scatter | solution.py:1013
  782.0 68.8 %collective-permute-start.113 = (bf16[2,256,512]{2,1,0:T(8,128)(2,1)}, bf16[2,256,512]{2,1,0:T(8,128)(2,1)S(1)}, u32[]{:S(2)}, u32[]{:S(2)}) collective-permute-start(bf16[2,256,512]{2,1,0:T(8,128)(2,1)} %get-tuple-element.703), channel_id=1, source_target_pairs={{0,16},{16,0},{1,17},{17,1},{2,18},{18,2},{3,19},{19,3},{4,20},{20... | collective-permute-start | bytes 1572872 | tf_op jit(solution)/shard_map/ppermute | solution.py:365
  798.5 53.4 %collective-permute-start.100 = (bf16[2,256,512]{2,1,0:T(8,128)(2,1)S(1)}, bf16[2,256,512]{2,1,0:T(8,128)(2,1)S(1)}, u32[]{:S(2)}, u32[]{:S(2)}) collective-permute-start(bf16[2,256,512]{2,1,0:T(8,128)(2,1)S(1)} %get-tuple-element.689), channel_id=1, source_target_pairs={{0,16},{16,0},{1,17},{17,1},{2,18},{18,2},{3,19},{19,3},{4,20},{20... | collective-permute-start | bytes 1572872 | tf_op jit(solution)/shard_map/ppermute | solution.py:365
  929.2 66.8 %all-to-all-start = ((bf16[8,224,512]{2,1,0:T(8,128)(2,1)}), bf16[8,224,512]{2,1,0:T(8,128)(2,1)}, u32[]{:S(2)}, u32[]{:S(2)}) async-start(bf16[8,224,512]{2,1,0:T(8,128)(2,1)} %fusion.66), calls=%async_computation.2 | async-start | bytes 3670016 | tf_op jit(solution)/shard_map/all_to_all | solution.py:1189
  933.5 100.1 %reduce-scatter.14.cloned.1.call-start = ((), (), s32[]{:S(2)}) async-start(), calls=%async_computation.14 | async-start | bytes 1310720 | tf_op jit(solution)/shard_map/reduce_scatter | solution.py:1013
  945.0 56.5 %collective-permute-start.122 = (bf16[2,896,512]{2,1,0:T(8,128)(2,1)}, bf16[2,896,512]{2,1,0:T(8,128)(2,1)}, u32[]{:S(2)}, u32[]{:S(2)}) collective-permute-start(bf16[2,896,512]{2,1,0:T(8,128)(2,1)} %get-tuple-element.740), channel_id=1, source_target_pairs={{0,16},{16,0},{1,17},{17,1},{2,18},{18,2},{3,19},{19,3},{4,20},{20... | collective-permute-start | bytes 5505032 | tf_op jit(solution)/shard_map/ppermute | solution.py:365
  945.2 56.3 %collective-permute-start.123 = (bf16[2,896,512]{2,1,0:T(8,128)(2,1)}, bf16[2,896,512]{2,1,0:T(8,128)(2,1)}, u32[]{:S(2)}, u32[]{:S(2)}) collective-permute-start(bf16[2,896,512]{2,1,0:T(8,128)(2,1)} %get-tuple-element.741), channel_id=1, source_target_pairs={{0,1},{1,0},{2,3},{3,2},{4,5},{5,4},{6,7},{7,6},{8,9},{9,8},{10,11... | collective-permute-start | bytes 5505032 | tf_op jit(solution)/shard_map/ppermute | solution.py:365
  (205 other events, 3717.4 us)
Sparse Core Ops, SparseCore 0:
  30.3 82.2 all-gather.4
  114.1 79.2 all-gather.8
  195.1 79.3 all-gather.10
  314.6 81.3 all-gather.6
  497.1 78.8 reduce-scatter.7
  635.7 78.6 reduce-scatter.5
  778.6 79.3 reduce-scatter.9
  918.8 63.8 reduce-scatter.11
  985.0 27.2 reduce-scatter.13
